TPU v7x, 32 devices: a whole 2x2x4 slice. The times are simulated.
32 devices in a mesh: dp: 8 (over z, x), mp: 4 (over y, core).
Axes of the slice: x: 2, y: 2, z: 4, core: 2. Of those that a mesh axis runs over, the one named last changes fastest.
Arguments:
- tokens: bfloat16 [4096, 1024], P(('dp', 'mp')), may hold values from -6 to 6
- gain_attn: float32 [1024], replicated, may hold values from 0.5 to 1.5
- w_query: bfloat16 [1024, 1024], P(None, 'mp'), may hold values from -0.0234375 to 0.0234375
- w_key: bfloat16 [1024, 1024], P(None, 'mp'), may hold values from -0.1875 to 0.1875
- w_value: bfloat16 [1024, 1024], P(None, 'mp'), may hold values from -0.1875 to 0.1875
- w_output: bfloat16 [1024, 1024], P('mp'), may hold values from -1 to 1
- rel_bias: float32 [32, 16], P(None, 'mp'), may hold values from -4 to 4
- bucket_table: int32 [512, 512], replicated, may hold values from 0 to 31
- gain_moe: float32 [1024], replicated, may hold values from 0.5 to 1.5
- router: float32 [1024, 16], replicated, may hold values from -0.09375 to 0.09375
- w_in: bfloat16 [16, 1024, 2816], P('dp', None, 'mp'), may hold values from -0.1875 to 0.1875
- w_out: bfloat16 [16, 2816, 1024], P('dp', 'mp'), may hold values from -1.75 to 1.75
- routes: int32 [4096], P(('dp', 'mp')), may hold values from 0 to 15
- slots: int32 [4096], P(('dp', 'mp')), may hold values from 0 to 10, as said below
- cotangent: bfloat16 [4096, 1024], P(('dp', 'mp')), may hold values from -6 to 6
Outputs:
- block_out: bfloat16 [4096, 1024], P(('dp', 'mp'))
- input_grad: bfloat16 [4096, 1024], P(('dp', 'mp'))
- grad_gain_attn: float32 [1024], replicated
- grad_w_query: float32 [1024, 1024], P(None, 'mp')
- grad_w_key: float32 [1024, 1024], P(None, 'mp')
- grad_w_value: float32 [1024, 1024], P(None, 'mp')
- grad_w_output: float32 [1024, 1024], P('mp')
- grad_rel_bias: float32 [32, 16], P(None, 'mp')
- grad_gain_moe: float32 [1024], replicated
- grad_router: float32 [1024, 16], replicated
- grad_w_in: float32 [16, 1024, 2816], P('dp', None, 'mp')
- grad_w_out: float32 [16, 2816, 1024], P('dp', 'mp')
Inputs may be any that keep to these rules, and one draw needn't show every extreme that they name: slots[t] is the number of earlier tokens of the same device (aligned block of 128 tokens) with the same route, or 10 where that number is 10 or more (the token is dropped).
All inputs are finite; a program needn't handle non-finite values.
Results may differ from a plain program's by a relative error of at most 0.023.
Values may be sent and summed in bfloat16 or wider, within the bound.
No kernel may reach another device: no remote copies, remote signals or barrier semaphores. Data moves between devices by JAX's collectives and lax.ppermute only.
A program may use at most 128 MiB of HBM per device.

v0:
```python
import functools

import jax
import jax.numpy as jnp
import numpy as np
from jax import lax
from jax.experimental import pallas as pl
from jax.experimental.pallas import tpu as pltpu
from jax.sharding import PartitionSpec as P

norm_eps = 1e-06
highest = lax.Precision.HIGHEST
bf16 = jnp.bfloat16
f32 = jnp.float32
LANES = 128
MIB = 1 << 20


def swap(block, axis, offset):
    size = lax.axis_size(axis)
    return lax.ppermute(block, axis, [(i, i ^ offset) for i in range(size)])


def bit_count(axis):
    return lax.axis_size(axis).bit_length() - 1


def gather_members(block, beside=None):
    held = block[None]
    for bit in reversed(range(bit_count("mp"))):
        other = swap(held, "mp", 1 << bit)
        if beside is not None and held.shape[0] == 1:
            other, beside = lax.optimization_barrier((other, beside))
        held = jnp.stack([held, other], axis=1).reshape((-1,) + block.shape)
    return held if beside is None else (held, beside)


def scatter_pairs(keep, received, first_bit):
    held = keep.astype(f32) + received.astype(f32)
    for bit in range(first_bit, bit_count("mp")):
        halves = held.reshape((-1, 2) + held.shape[1:])
        got = swap(halves[:, 1].astype(bf16), "mp", 1 << bit)
        held = halves[:, 0] + got.astype(f32)
    return held[0]


def exchange_groups(buffer):
    return lax.all_to_all(buffer, "dp", split_axis=0, concat_axis=0, tiled=True)


def near_step(part):
    mine = lax.axis_index("dp") & 1
    halves = part.reshape(2, part.shape[0] // 2, part.shape[1])
    got = swap(lax.dynamic_index_in_dim(halves, 1 - mine, 0, keepdims=False), "dp", 1)
    return lax.dynamic_index_in_dim(halves, mine, 0, keepdims=False), got


def far_steps(keep, got):
    rest = lax.axis_size("dp") // 2
    mine = lax.axis_index("dp") >> 1
    held = (keep.astype(f32) + got.astype(f32)).astype(bf16)
    blocks = held.reshape(rest, held.shape[0] // rest, held.shape[1])

    def block_of(offset):
        return lax.dynamic_index_in_dim(blocks, mine ^ offset, 0, keepdims=False)

    parts = [swap(block_of(offset), "dp", 2 * offset) for offset in range(1, rest)]
    total = block_of(0).astype(f32)
    for item in parts:
        total = total + item.astype(f32)
    own = total.astype(bf16)
    return jnp.stack([own] + [swap(own, "dp", 2 * offset) for offset in range(1, rest)])


def last_step(own_half):
    other = swap(own_half, "dp", 1)
    rest = lax.axis_size("dp") // 2
    me = lax.axis_index("dp")
    both = jnp.concatenate([own_half, other], axis=0)
    rows = []
    for half in range(2):
        for block in range(rest):
            at = (half ^ (me & 1)) * rest + (block ^ (me >> 1))
            rows.append(lax.dynamic_index_in_dim(both, at, 0, keepdims=False))
    return jnp.concatenate(rows, axis=0).astype(f32)


def sum_all(part, axes):
    held = part
    for axis in axes:
        for bit in range(bit_count(axis)):
            held = held + swap(held, axis, 1 << bit)
    return held


def bias_kernel(block, shift_ref, table_ref, bucket_ref, bias_ref, moved_ref):
    shift = shift_ref[0]
    for at in range(table_ref.shape[1] // block):
        source = pl.multiple_of((at ^ shift) * block, block)
        labels = table_ref[:, pl.ds(source, block)]
        columns = slice(at * block, (at + 1) * block)
        moved_ref[:, columns] = labels
        for head in range(bucket_ref.shape[0]):
            row = jnp.broadcast_to(bucket_ref[head : head + 1, :], labels.shape)
            bias_ref[head, :, columns] = jnp.take_along_axis(row, labels, axis=1, mode="promise_in_bounds")


def make_bias(table, bucket_rows, shift, block):
    seq_len = table.shape[0]
    heads = bucket_rows.shape[0]
    return pl.pallas_call(
        functools.partial(bias_kernel, block),
        grid_spec=pltpu.PrefetchScalarGridSpec(
            num_scalar_prefetch=1,
            grid=(seq_len // block,),
            in_specs=[
                pl.BlockSpec((block, seq_len), lambda i, s: (i ^ s[0], 0)),
                pl.BlockSpec((heads, LANES), lambda i, s: (0, 0)),
            ],
            out_specs=[
                pl.BlockSpec((heads, block, seq_len), lambda i, s: (0, i, 0)),
                pl.BlockSpec((block, seq_len), lambda i, s: (i, 0)),
            ],
        ),
        out_shape=[
            jax.ShapeDtypeStruct((heads, seq_len, seq_len), f32),
            jax.ShapeDtypeStruct((seq_len, seq_len), jnp.int32),
        ],
        compiler_params=pltpu.CompilerParams(vmem_limit_bytes=32 * MIB),
        cost_estimate=pl.CostEstimate(
            flops=seq_len * seq_len * heads, bytes_accessed=4 * seq_len * seq_len * (heads + 2), transcendentals=0
        ),
        name="bias_lookup",
    )(shift, table, bucket_rows)


def bucket_kernel(buckets, table_ref, grad_ref, out_ref):
    seqs, heads, rows, seq_len = grad_ref.shape

    @pl.when(pl.program_id(0) == 0)
    def _():
        out_ref[...] = jnp.zeros_like(out_ref)

    labels = lax.broadcasted_iota(jnp.int32, (rows, buckets, seq_len), 1)
    onehot = (table_ref[...][:, None, :] == labels).astype(f32).astype(bf16).reshape(rows * buckets, seq_len)
    total = jnp.zeros((rows * buckets, heads * rows), f32)
    for seq in range(seqs):
        grads = grad_ref[seq].reshape(heads * rows, seq_len)
        total += lax.dot_general(onehot, grads, (((1,), (1,)), ((), ())), preferred_element_type=f32)
    own_row = lax.broadcasted_iota(jnp.int32, (rows, buckets, heads * rows), 0)
    its_row = lax.broadcasted_iota(jnp.int32, (rows, buckets, heads * rows), 2) % rows
    kept = jnp.where(own_row == its_row, total.reshape(rows, buckets, heads * rows), 0.0)
    out_ref[...] += jnp.sum(kept, axis=0)


def bucket_grad(table, score_grad, buckets):
    seqs, heads, seq_len, _ = score_grad.shape
    rows = 32
    out = pl.pallas_call(
        functools.partial(bucket_kernel, buckets),
        grid=(seq_len // rows,),
        in_specs=[
            pl.BlockSpec((rows, seq_len), lambda i: (i, 0)),
            pl.BlockSpec((seqs, heads, rows, seq_len), lambda i: (0, 0, i, 0)),
        ],
        out_specs=pl.BlockSpec((buckets, heads * rows), lambda i: (0, 0)),
        out_shape=jax.ShapeDtypeStruct((buckets, heads * rows), f32),
        compiler_params=pltpu.CompilerParams(vmem_limit_bytes=32 * MIB),
        cost_estimate=pl.CostEstimate(
            flops=2 * seqs * seq_len * buckets * seq_len * heads * rows,
            bytes_accessed=2 * seqs * heads * seq_len * seq_len + 4 * seq_len * seq_len,
            transcendentals=0,
        ),
        name="bucket_grad",
    )(table, score_grad)
    return jnp.sum(out.reshape(buckets, heads, rows), axis=2)


def attend_kernel(head_size, joined_ref, bias_ref, mixed_ref, probs_ref):
    seq_len, width = joined_ref.shape
    head_cols = width // 3
    pair_heads = bias_ref.shape[0]
    pair_cols = pair_heads * head_size
    start = pl.program_id(1) * pair_cols
    columns = [
        joined_ref[:, pl.ds(pl.multiple_of(start + part * head_cols, pair_cols), pair_cols)] for part in range(3)
    ]
    rows = min(128, seq_len)
    for chunk in range(seq_len // rows):
        picked = slice(chunk * rows, (chunk + 1) * rows)
        outs = []
        for head in range(pair_heads):
            cols = slice(head * head_size, (head + 1) * head_size)
            scores = lax.dot_general(
                columns[0][picked, cols], columns[1][:, cols], (((1,), (1,)), ((), ())), preferred_element_type=f32
            )
            scores = scores + bias_ref[head, picked, :]
            expo = jnp.exp(scores - jnp.max(scores, axis=-1, keepdims=True))
            probs = expo / jnp.sum(expo, axis=-1, keepdims=True)
            probs_ref[0, head, picked, :] = probs
            outs.append(jnp.dot(probs.astype(bf16), columns[2][:, cols], preferred_element_type=f32))
        mixed_ref[picked, :] = jnp.concatenate(outs, axis=1).astype(bf16)


def attend(joined, bias, head_size):
    heads, seq_len, _ = bias.shape
    tokens, width = joined.shape
    seqs = tokens // seq_len
    head_cols = width // 3
    pair = min(heads, LANES // head_size)
    return pl.pallas_call(
        functools.partial(attend_kernel, head_size),
        grid=(seqs, heads // pair),
        in_specs=[
            pl.BlockSpec((seq_len, width), lambda s, h: (s, 0)),
            pl.BlockSpec((pair, seq_len, seq_len), lambda s, h: (h, 0, 0)),
        ],
        out_specs=[
            pl.BlockSpec((seq_len, pair * head_size), lambda s, h: (s, h)),
            pl.BlockSpec((1, pair, seq_len, seq_len), lambda s, h: (s, h, 0, 0)),
        ],
        out_shape=[
            jax.ShapeDtypeStruct((tokens, head_cols), bf16),
            jax.ShapeDtypeStruct((seqs, heads, seq_len, seq_len), f32),
        ],
        compiler_params=pltpu.CompilerParams(vmem_limit_bytes=32 * MIB),
        cost_estimate=pl.CostEstimate(
            flops=4 * seqs * heads * seq_len * seq_len * head_size,
            bytes_accessed=8 * seqs * heads * seq_len * seq_len,
            transcendentals=seqs * heads * seq_len * seq_len,
        ),
        name="attend",
    )(joined, bias)


def attend_back_kernel(head_size, joined_ref, grad_ref, probs_ref, out_ref, score_ref):
    seq_len, width = joined_ref.shape
    head_cols = width // 3
    pair_heads = probs_ref.shape[1]
    pair_cols = pair_heads * head_size
    start = pl.program_id(1) * pair_cols

    def place(part):
        return pl.ds(pl.multiple_of(start + part * head_cols, pair_cols), pair_cols)

    queries, keys, values = [joined_ref[:, place(part)] for part in range(3)]
    grads = grad_ref[...]
    queries_t, grads_t = queries.T, grads.T
    rows = min(128, seq_len)
    query_parts = []
    key_t = [jnp.zeros((head_size, seq_len), f32) for _ in range(pair_heads)]
    value_t = [jnp.zeros((head_size, seq_len), f32) for _ in range(pair_heads)]
    for chunk in range(seq_len // rows):
        picked = slice(chunk * rows, (chunk + 1) * rows)
        outs = []
        for head in range(pair_heads):
            cols = slice(head * head_size, (head + 1) * head_size)
            probs = probs_ref[0, head, picked, :]
            prob_grad = lax.dot_general(
                grads[picked, cols], values[:, cols], (((1,), (1,)), ((), ())), preferred_element_type=f32
            )
            weighted = jnp.sum(probs * prob_grad, axis=-1, keepdims=True)
            score_grad = (probs * (prob_grad - weighted)).astype(bf16)
            score_ref[0, head, picked, :] = score_grad
            outs.append(jnp.dot(score_grad, keys[:, cols], preferred_element_type=f32))
            key_t[head] += jnp.dot(queries_t[cols, picked], score_grad, preferred_element_type=f32)
            value_t[head] += jnp.dot(grads_t[cols, picked], probs.astype(bf16), preferred_element_type=f32)
        out_ref[picked, place(0)] = jnp.concatenate(outs, axis=1).astype(bf16)
    out_ref[:, place(1)] = jnp.concatenate(key_t, axis=0).T.astype(bf16)
    out_ref[:, place(2)] = jnp.concatenate(value_t, axis=0).T.astype(bf16)


def attend_back(joined, mixed_grad, probs, head_size):
    seqs, heads, seq_len, _ = probs.shape
    tokens, width = joined.shape
    pair = min(heads, LANES // head_size)
    return pl.pallas_call(
        functools.partial(attend_back_kernel, head_size),
        grid=(seqs, heads // pair),
        in_specs=[
            pl.BlockSpec((seq_len, width), lambda s, h: (s, 0)),
            pl.BlockSpec((seq_len, pair * head_size), lambda s, h: (s, h)),
            pl.BlockSpec((1, pair, seq_len, seq_len), lambda s, h: (s, h, 0, 0)),
        ],
        out_specs=[
            pl.BlockSpec((seq_len, width), lambda s, h: (s, 0)),
            pl.BlockSpec((1, pair, seq_len, seq_len), lambda s, h: (s, h, 0, 0)),
        ],
        out_shape=[
            jax.ShapeDtypeStruct((tokens, width), bf16),
            jax.ShapeDtypeStruct((seqs, heads, seq_len, seq_len), bf16),
        ],
        compiler_params=pltpu.CompilerParams(vmem_limit_bytes=32 * MIB),
        cost_estimate=pl.CostEstimate(
            flops=8 * seqs * heads * seq_len * seq_len * head_size,
            bytes_accessed=6 * seqs * heads * seq_len * seq_len,
            transcendentals=0,
        ),
        name="attend_back",
    )(joined, mixed_grad, probs)


gelu_scale = float(np.sqrt(2.0 / np.pi))


def gelu_parts(pre):
    bent = jnp.tanh(gelu_scale * (pre + 0.044715 * pre * pre * pre))
    return 0.5 * pre * (1.0 + bent), bent


def gelu_slope(pre):
    _, bent = gelu_parts(pre)
    return 0.5 * (1.0 + bent) + 0.5 * pre * (1.0 - bent * bent) * gelu_scale * (1.0 + 0.134145 * pre * pre)


def expert_kernel(cuts, middle_step, blocks_ref, sort_ref, unsort_ref, first_ref, second_ref, *refs):
    members, _, piece = blocks_ref.shape
    back_ref, rows_ref = refs[-1], refs[-2]
    expert_rows = sort_ref.shape[1] // cuts
    for member in range(members):
        moved = jnp.dot(sort_ref[0], blocks_ref[member], preferred_element_type=f32).astype(bf16)
        for cut in range(cuts):
            rows_ref[0, member * expert_rows : (member + 1) * expert_rows, cut * piece : (cut + 1) * piece] = moved[
                cut * expert_rows : (cut + 1) * expert_rows
            ]
    inner = lax.dot_general(rows_ref[0], first_ref[0], (((1,), (1,)), ((), ())), preferred_element_type=f32)
    inner = middle_step(inner, *refs[:-2])
    result = jnp.dot(inner, second_ref[0], preferred_element_type=f32).astype(bf16)
    for member in range(members):
        part = jnp.concatenate(
            [
                result[member * expert_rows : (member + 1) * expert_rows, cut * piece : (cut + 1) * piece]
                for cut in range(cuts)
            ],
            axis=0,
        )
        placed = jnp.dot(unsort_ref[0], part, preferred_element_type=f32).astype(bf16)

        @pl.when(pl.program_id(0) == 0)
        def _():
            back_ref[member] = placed

        @pl.when(pl.program_id(0) != 0)
        def _():
            back_ref[member] += placed


def forward_step(inner, pre_ref, hidden_ref):
    pre_ref[0] = inner
    hidden = gelu_parts(inner)[0].astype(bf16)
    hidden_ref[0] = hidden
    return hidden


def backward_step(inner, pre_ref, grad_ref):
    grad = (inner.astype(bf16).astype(f32) * gelu_slope(pre_ref[0])).astype(bf16)
    grad_ref[0] = grad
    return grad


def run_experts(blocks, sorting, unsorting, first, second, cuts, pre=None):
    members, all_rows, piece = blocks.shape
    experts, units, width = first.shape
    rows = members * (sorting.shape[1] // cuts)

    def per_expert(*shape):
        return pl.BlockSpec((1,) + shape, lambda j: (j, 0, 0))

    whole = pl.BlockSpec((members, all_rows, piece), lambda j: (0, 0, 0))
    inner = jax.ShapeDtypeStruct((experts, rows, units), bf16)
    in_specs = [
        whole,
        per_expert(*sorting.shape[1:]),
        per_expert(*unsorting.shape[1:]),
        per_expert(units, width),
        per_expert(units, width),
    ]
    operands = [blocks, sorting, unsorting, first, second]
    out_specs = [per_expert(rows, units), per_expert(rows, width), whole]
    out_shape = [inner, jax.ShapeDtypeStruct((experts, rows, width), bf16), jax.ShapeDtypeStruct(blocks.shape, bf16)]
    if pre is None:
        step, name = forward_step, "experts"
        out_specs.insert(0, per_expert(rows, units))
        out_shape.insert(0, jax.ShapeDtypeStruct(inner.shape, f32))
    else:
        step, name = backward_step, "experts_back"
        in_specs.append(per_expert(rows, units))
        operands.append(pre)
    return pl.pallas_call(
        functools.partial(expert_kernel, cuts, step),
        grid=(experts,),
        in_specs=in_specs,
        out_specs=out_specs,
        out_shape=out_shape,
        compiler_params=pltpu.CompilerParams(vmem_limit_bytes=40 * MIB),
        cost_estimate=pl.CostEstimate(
            flops=4 * experts * rows * units * width,
            bytes_accessed=4 * experts * units * width + 12 * experts * rows * width,
            transcendentals=experts * rows * units,
        ),
        name=name,
    )(*operands)


def root_inverse(values):
    return lax.rsqrt(jnp.mean(values * values, axis=-1, keepdims=True) + norm_eps)


def shards(
    tokens,
    gain_attn,
    w_query,
    w_key,
    w_value,
    w_output,
    rel_bias,
    bucket_table,
    gain_moe,
    router,
    w_in,
    w_out,
    routes,
    slots,
    cotangent,
):
    group_count = lax.axis_size("dp")
    member_count = lax.axis_size("mp")
    member = lax.axis_index("mp")
    tok_dev, width = tokens.shape
    expert_local = w_in.shape[0]
    expert_count = expert_local * group_count
    capacity = max(2, (5 * tok_dev + 4 * expert_count - 1) // (4 * expert_count))
    seq_len = bucket_table.shape[0]
    head_cols = w_query.shape[1]
    head_local = rel_bias.shape[1]
    head_size = head_cols // head_local
    group_tokens = tok_dev * member_count
    seq_members = seq_len // tok_dev

    bucket_rows = jnp.pad(rel_bias.T, ((0, 0), (0, LANES - rel_bias.shape[0])))
    shift = (member % seq_members).astype(jnp.int32)[None]
    bias, moved_table = make_bias(bucket_table, bucket_rows, shift, tok_dev)
    w_joined = jnp.concatenate([w_query, w_key, w_value], axis=1)
    all_tokens = gather_members(tokens, (bias, moved_table, w_joined))
    all_tokens, (bias, moved_table, w_joined) = all_tokens
    all_tokens = all_tokens.reshape(group_tokens, width).astype(f32)
    unit_attn = all_tokens * root_inverse(all_tokens)
    normed_low = (unit_attn * gain_attn).astype(bf16)
    joined = jnp.dot(normed_low, w_joined, preferred_element_type=f32).astype(bf16)
    mixed, probs = attend(joined, bias, head_size)
    mixed_pairs = mixed.reshape(member_count // 2, 2, tok_dev, head_cols)

    def project(rows):
        return jnp.einsum("stc,cd->std", rows, w_output, preferred_element_type=f32)

    attn_got = swap(project(mixed_pairs[:, 1]).astype(bf16), "mp", 1)
    attn = scatter_pairs(project(mixed_pairs[:, 0]), attn_got, 1)
    middle = tokens.astype(f32) + attn

    middle_root = root_inverse(middle)
    unit_moe = middle * middle_root
    moe_low = (unit_moe * gain_moe).astype(bf16)
    moe_rows = moe_low.astype(f32)
    router_t = router.T
    logits = lax.dot_general(
        moe_rows, router_t, (((1,), (1,)), ((), ())), precision=highest, preferred_element_type=f32
    )
    router_probs = jax.nn.softmax(logits, axis=-1)
    route_hot = (routes[:, None] == jnp.arange(expert_count, dtype=jnp.int32)[None, :]).astype(f32)
    gate_prob = jnp.sum(router_probs * route_hot, axis=-1, keepdims=True)

    chunk_slots = expert_local * capacity
    cuts = 1
    while cuts * chunk_slots % 8 != 0:
        cuts *= 2
    piece = width // cuts
    chunk_rows = cuts * chunk_slots
    all_rows = group_count * chunk_rows
    row_index = jnp.arange(all_rows, dtype=jnp.int32)
    row_chunk, row_cut, row_slot = (
        row_index // chunk_rows,
        (row_index // chunk_slots) % cuts,
        row_index % chunk_slots,
    )
    target = jnp.where(slots < capacity, routes * capacity + slots, -1)
    wanted = row_chunk * chunk_slots + row_slot
    hit = (wanted[:, None, None] == target[None, None, :]) & (
        row_cut[:, None, None] == jnp.arange(cuts, dtype=jnp.int32)[None, :, None]
    )
    placement = hit.astype(bf16).reshape(all_rows, cuts * tok_dev)

    def cut_rows(rows):
        return jnp.concatenate([rows[:, c * piece : (c + 1) * piece] for c in range(cuts)], axis=0)

    def join_rows(rows):
        return jnp.concatenate([rows[c * tok_dev : (c + 1) * tok_dev] for c in range(cuts)], axis=1)

    def send_rows(rows):
        return exchange_groups(jnp.dot(placement, cut_rows(rows), preferred_element_type=f32).astype(bf16))

    def collect(blocks):
        pairs = blocks.reshape(member_count // 2, 2, all_rows, piece)
        got = swap(pairs[:, 1], "mp", 1)
        back = exchange_groups(scatter_pairs(pairs[:, 0], got, 1).astype(bf16))
        rows = lax.dot_general(placement, back, (((0,), (0,)), ((), ())), preferred_element_type=f32)
        return join_rows(rows)

    order = np.arange(all_rows).reshape(group_count, cuts, expert_local, capacity).transpose(2, 1, 0, 3)
    picks = np.eye(all_rows, dtype=np.float32)[order.reshape(expert_local, -1)]
    sorting = jnp.asarray(picks, bf16)
    unsorting = jnp.asarray(picks.transpose(0, 2, 1), bf16)
    w_in_t = jnp.swapaxes(w_in, 1, 2)

    upstream = cotangent.astype(f32)
    sent = send_rows(moe_low)
    grad_sent = send_rows((gate_prob * upstream).astype(bf16))
    arrived = gather_members(sent)

    arrived, grad_sent = lax.optimization_barrier((arrived, grad_sent))
    grad_arrived = gather_members(grad_sent)
    pre, hidden, expert_in, value_blocks = run_experts(arrived, sorting, unsorting, w_in_t, w_out, cuts)
    pre_grad, result_grad, rows_blocks = run_experts(grad_arrived, sorting, unsorting, w_out, w_in_t, cuts, pre)
    combined = collect(value_blocks)
    moe_grad = collect(rows_blocks)
    grad_w_out = jnp.einsum("jrf,jrd->jfd", hidden, result_grad, preferred_element_type=f32)
    grad_w_in = jnp.swapaxes(
        jnp.einsum("jrf,jrd->jfd", pre_grad, expert_in, preferred_element_type=f32), 1, 2
    )

    block_out = (middle + gate_prob * combined).astype(bf16)
    gate_grad = jnp.sum(upstream * combined, axis=-1, keepdims=True)
    logit_grad = router_probs * (route_hot * gate_grad - gate_prob * gate_grad)
    grad_router_t = lax.dot_general(
        logit_grad, moe_rows, (((0,), (0,)), ((), ())), precision=highest, preferred_element_type=f32
    )
    moe_grad = moe_grad + jnp.dot(logit_grad, router_t, precision=highest, preferred_element_type=f32)
    grad_gain_moe = jnp.sum(moe_grad * unit_moe, axis=0, keepdims=True)
    scaled = moe_grad * gain_moe
    middle_grad = upstream + middle_root * (
        scaled - unit_moe * jnp.mean(scaled * unit_moe, axis=-1, keepdims=True)
    )

    grad_rows = gather_members(middle_grad.astype(bf16)).reshape(group_tokens, width)
    mixed_grad = jnp.einsum("td,cd->tc", grad_rows, w_output, preferred_element_type=f32).astype(bf16)
    output_part = jnp.einsum("tc,td->cd", mixed, grad_rows, preferred_element_type=f32).astype(bf16)
    output_near = near_step(output_part)
    joined_grad, score_grad = attend_back(joined, mixed_grad, probs, head_size)
    output_near, joined_grad = lax.optimization_barrier((output_near, joined_grad))
    joined_near = []
    for half in range(2):
        columns = normed_low[:, half * (width // 2) : (half + 1) * (width // 2)]
        local = jnp.einsum("td,tc->dc", columns, joined_grad, preferred_element_type=f32).astype(bf16)
        joined_near.append(near_step(local))
    grad_w_output = last_step(far_steps(*output_near))
    grad_joined = jnp.concatenate([last_step(far_steps(*near)) for near in joined_near], axis=0)
    grad_w_query, grad_w_key, grad_w_value = [
        grad_joined[:, part * head_cols : (part + 1) * head_cols] for part in range(3)
    ]
    attn_partial = jnp.einsum("tc,dc->td", joined_grad, w_joined, preferred_element_type=f32)
    attn_pairs = attn_partial.reshape(member_count // 2, 2, tok_dev, width)
    back_got = swap(attn_pairs[:, 1].astype(bf16), "mp", 1)
    attn_grad = scatter_pairs(attn_pairs[:, 0], back_got, 1)
    own_tokens = tokens.astype(f32)
    own_root = root_inverse(own_tokens)
    own_unit = own_tokens * own_root
    scaled = attn_grad * gain_attn
    input_grad = (
        middle_grad + own_root * (scaled - own_unit * jnp.mean(scaled * own_unit, axis=-1, keepdims=True))
    ).astype(bf16)
    grad_gain_attn = sum_all(jnp.sum(attn_grad * own_unit, axis=0, keepdims=True), ("mp", "dp"))[0]
    small = sum_all(jnp.concatenate([grad_gain_moe, grad_router_t], axis=0), ("mp", "dp"))
    grad_rel_bias = sum_all(bucket_grad(moved_table, score_grad, rel_bias.shape[0]), ("dp",))
    return (
        block_out,
        input_grad,
        grad_gain_attn,
        grad_w_query,
        grad_w_key,
        grad_w_value,
        grad_w_output,
        grad_rel_bias,
        small[0],
        small[1:].T,
        grad_w_in,
        grad_w_out,
    )


def solution(mesh):
    in_specs = (
        P(("dp", "mp"), None),
        P(),
        P(None, "mp"),
        P(None, "mp"),
        P(None, "mp"),
        P("mp", None),
        P(None, "mp"),
        P(),
        P(),
        P(),
        P("dp", None, "mp"),
        P("dp", "mp", None),
        P(("dp", "mp")),
        P(("dp", "mp")),
        P(("dp", "mp"), None),
    )
    out_specs = (
        P(("dp", "mp"), None),
        P(("dp", "mp"), None),
        P(),
        P(None, "mp"),
        P(None, "mp"),
        P(None, "mp"),
        P("mp", None),
        P(None, "mp"),
        P(),
        P(),
        P("dp", None, "mp"),
        P("dp", "mp", None),
    )
    return jax.shard_map(shards, mesh=mesh, in_specs=in_specs, out_specs=out_specs, check_vma=False)
```

profile of v0, /device:TPU:0, one launch (start us, length us, event | category | flops | bytes accessed | tf_op | source)
XLA Modules:
  0.0 290.7 jit_solution(7263056656212234742)
XLA Ops:
  16.1 6.1 %attend.1 = (bf16[512,256]{1,0:T(8,128)(2,1)S(1)}, f32[1,4,512,512]{3,2,1,0:T(8,128)S(1)}) custom-call(bf16[512,768]{1,0:T(8,128)(2,1)S(1)} %convolution_convert_fusion.2.joined_ref, f32[4,512,512]{2,1,0:T(8,128)S(1)} %get-tuple-element.38.bias_ref), custom_call_target="tpu_custom_call" | custom-call | flops 268435456 | bytes 8388608 | tf_op jit(solution)/shard_map/attend/pallas_call | solution.py:211
  28.2 7.2 %collective-permute-done.3 = bf16[1,128,1024]{2,1,0:T(8,128)(2,1)S(1)} collective-permute-done((bf16[1,128,1024]{2,1,0:T(8,128)(2,1)S(1)}, bf16[1,128,1024]{2,1,0:T(8,128)(2,1)S(1)}, u32[]{:S(2)}, u32[]{:S(2)}) %collective-permute-start.3) | collective-permute-done | bytes 262176 | tf_op jit(solution)/shard_map/ppermute | solution.py:21
  37.6 5.8 %all-to-all-start = ((bf16[8,40,512]{2,1,0:T(8,128)(2,1)}), bf16[8,40,512]{2,1,0:T(8,128)(2,1)S(1)}, u32[]{:S(2)}, u32[]{:S(2)}) async-start(bf16[8,40,512]{2,1,0:T(8,128)(2,1)} %bitcast.20), calls=%async_computation | async-start | bytes 655360 | tf_op jit(solution)/shard_map/all_to_all | solution.py:48
  43.7 9.4 %all-to-all-done = bf16[8,40,512]{2,1,0:T(8,128)(2,1)S(1)} async-done(((bf16[8,40,512]{2,1,0:T(8,128)(2,1)}), bf16[8,40,512]{2,1,0:T(8,128)(2,1)S(1)}, u32[]{:S(2)}, u32[]{:S(2)}) %all-to-all-start) | async-done | bytes 327712 | tf_op jit(solution)/shard_map/all_to_all | solution.py:48
  54.4 5.9 %collective-permute-done.4 = bf16[1,320,512]{2,1,0:T(8,128)(2,1)S(1)} collective-permute-done((bf16[1,320,512]{2,1,0:T(8,128)(2,1)S(1)}, bf16[1,320,512]{2,1,0:T(8,128)(2,1)S(1)}, u32[]{:S(2)}, u32[]{:S(2)}) %collective-permute-start.4) | collective-permute-done | bytes 327712 | tf_op jit(solution)/shard_map/ppermute | solution.py:21
  62.4 5.8 %all-to-all-start.1 = ((bf16[8,40,512]{2,1,0:T(8,128)(2,1)}), bf16[8,40,512]{2,1,0:T(8,128)(2,1)}, u32[]{:S(2)}, u32[]{:S(2)}) async-start(bf16[8,40,512]{2,1,0:T(8,128)(2,1)} %bitcast.347), calls=%async_computation.1 | async-start | bytes 655360 | tf_op jit(solution)/shard_map/all_to_all | solution.py:48
  70.7 8.6 %all-to-all-done.1 = bf16[8,40,512]{2,1,0:T(8,128)(2,1)} async-done(((bf16[8,40,512]{2,1,0:T(8,128)(2,1)}), bf16[8,40,512]{2,1,0:T(8,128)(2,1)}, u32[]{:S(2)}, u32[]{:S(2)}) %all-to-all-start.1) | async-done | bytes 327712 | tf_op jit(solution)/shard_map/all_to_all | solution.py:48
  85.4 5.9 %experts.1 = (f32[2,320,704]{2,1,0:T(8,128)S(1)}, bf16[2,320,704]{2,1,0:T(8,128)(2,1)S(1)}, bf16[2,320,1024]{2,1,0:T(8,128)(2,1)S(1)}, bf16[4,320,512]{2,1,0:T(8,128)(2,1)S(1)}) custom-call(bf16[4,320,512]{2,1,0:T(8,128)(2,1)S(1)} %bitcast.325, bf16[2,160,320]{2,1,0:T(8,128)(2,1)S(1)} %copy-done.22, bf16[2,320,160]{2,1,0:T(8,128)(2,1)S(1)} %copy-done.14, ...), custom_call_target="tpu_custom_call" | custom-call | flops 1845493760 | bytes 13631488 | tf_op jit(solution)/shard_map/experts/pallas_call | solution.py:389
  95.1 6.4 %experts_back.1 = (bf16[2,320,704]{2,1,0:T(8,128)(2,1)S(1)}, bf16[2,320,1024]{2,1,0:T(8,128)(2,1)S(1)}, bf16[4,320,512]{2,1,0:T(8,128)(2,1)S(1)}) custom-call(bf16[4,320,512]{2,1,0:T(8,128)(2,1)S(1)} %bitcast.324, bf16[2,160,320]{2,1,0:T(8,128)(2,1)S(1)} %copy-done.22, bf16[2,320,160]{2,1,0:T(8,128)(2,1)S(1)} %copy-done.14, ...), custom_call_target="tpu_custom_call" | custom-call | flops 1845493760 | bytes 13631488 | tf_op jit(solution)/shard_map/experts_back/pallas_call | solution.py:389
  103.9 8.9 %collective-permute-done.7 = bf16[1,320,512]{2,1,0:T(8,128)(2,1)S(1)} collective-permute-done((bf16[1,320,512]{2,1,0:T(8,128)(2,1)S(1)}, bf16[1,320,512]{2,1,0:T(8,128)(2,1)S(1)}, u32[]{:S(2)}, u32[]{:S(2)}) %collective-permute-start.7) | collective-permute-done | bytes 327712 | tf_op jit(solution)/shard_map/ppermute | solution.py:21
  113.7 3.6 %all-to-all-start.2 = ((bf16[8,40,512]{2,1,0:T(8,128)(2,1)}), bf16[8,40,512]{2,1,0:T(8,128)(2,1)S(1)}, u32[]{:S(2)}, u32[]{:S(2)}) async-start(bf16[8,40,512]{2,1,0:T(8,128)(2,1)} %bitcast.38), calls=%async_computation.2 | async-start | bytes 655360 | tf_op jit(solution)/shard_map/all_to_all | solution.py:48
  120.3 7.0 %all-to-all-done.2 = bf16[8,40,512]{2,1,0:T(8,128)(2,1)S(1)} async-done(((bf16[8,40,512]{2,1,0:T(8,128)(2,1)}), bf16[8,40,512]{2,1,0:T(8,128)(2,1)S(1)}, u32[]{:S(2)}, u32[]{:S(2)}) %all-to-all-start.2) | async-done | bytes 327712 | tf_op jit(solution)/shard_map/all_to_all | solution.py:48
  129.3 5.8 %all-to-all-start.3 = ((bf16[8,40,512]{2,1,0:T(8,128)(2,1)}), bf16[8,40,512]{2,1,0:T(8,128)(2,1)S(1)}, u32[]{:S(2)}, u32[]{:S(2)}) async-start(bf16[8,40,512]{2,1,0:T(8,128)(2,1)} %bitcast.54), calls=%async_computation.3 | async-start | bytes 655360 | tf_op jit(solution)/shard_map/all_to_all | solution.py:48
  135.5 8.2 %all-to-all-done.3 = bf16[8,40,512]{2,1,0:T(8,128)(2,1)S(1)} async-done(((bf16[8,40,512]{2,1,0:T(8,128)(2,1)}), bf16[8,40,512]{2,1,0:T(8,128)(2,1)S(1)}, u32[]{:S(2)}, u32[]{:S(2)}) %all-to-all-start.3) | async-done | bytes 327712 | tf_op jit(solution)/shard_map/all_to_all | solution.py:48
  148.9 9.0 %collective-permute-done.49 = f32[17,1024]{1,0:T(8,128)} collective-permute-done((f32[17,1024]{1,0:T(8,128)S(1)}, f32[17,1024]{1,0:T(8,128)}, u32[]{:S(2)}, u32[]{:S(2)}) %collective-permute-start.49) | collective-permute-done | bytes 69664 | tf_op jit(solution)/shard_map/ppermute | solution.py:21
  163.7 4.2 %fusion.104 = f32[2,1024,704]{1,2,0:T(8,128)} fusion(bf16[2,320,1024]{2,1,0:T(8,128)(2,1)S(1)} %copy-done.13, bf16[2,320,704]{2,1,0:T(8,128)(2,1)S(1)} %copy-done.21), kind=kOutput, calls=%fused_computation.235 | convolution fusion | flops 922746880 | bytes 7979008 | tf_op jit(solution)/shard_map/jrf,jrd->jfd/dot_general | solution.py:527
  172.2 5.8 %attend_back.1 = (bf16[512,768]{1,0:T(8,128)(2,1)S(1)}, bf16[1,4,512,512]{3,2,1,0:T(8,128)(2,1)S(1)}) custom-call(bf16[512,768]{1,0:T(8,128)(2,1)S(1)} %copy-done.8, bf16[512,256]{1,0:T(8,128)(2,1)S(1)} %convolution_convert_fusion.7.grad_ref, f32[1,4,512,512]{3,2,1,0:T(8,128)S(1)} %copy-done.6), custom_call_target="tpu_custom_call" | custom-call | flops 536870912 | bytes 6291456 | tf_op jit(solution)/shard_map/attend_back/pallas_call | solution.py:277
  178.8 7.6 %bucket_grad.1 = f32[32,128]{1,0:T(8,128)S(1)} custom-call(s32[512,512]{1,0:T(8,128)S(1)} %copy-done.24, bf16[1,4,512,512]{3,2,1,0:T(8,128)(2,1)S(1)} %get-tuple-element.51.grad_ref), custom_call_target="tpu_custom_call" | custom-call | flops 2147483648 | bytes 3145728 | tf_op jit(solution)/shard_map/bucket_grad/pallas_call | solution.py:159
  191.9 4.2 %fusion.105 = f32[2,704,1024]{2,1,0:T(8,128)} fusion(bf16[2,320,704]{2,1,0:T(8,128)(2,1)S(1)} %copy-done.19, bf16[2,320,1024]{2,1,0:T(8,128)(2,1)S(1)} %copy-done.11), kind=kOutput, calls=%fused_computation.236 | convolution fusion | flops 922746880 | bytes 7979008 | tf_op jit(solution)/shard_map/jrf,jrd->jfd/dot_general | solution.py:525
  228.1 5.2 %collective-permute-done.30 = bf16[256,768]{1,0:T(8,128)(2,1)S(1)} collective-permute-done((bf16[256,768]{1,0:T(8,128)(2,1)S(1)}, bf16[256,768]{1,0:T(8,128)(2,1)S(1)}, u32[]{:S(2)}, u32[]{:S(2)}) %collective-permute-start.30) | collective-permute-done | bytes 393248 | tf_op jit(solution)/shard_map/ppermute | solution.py:21
  250.7 4.1 %collective-permute-done.32 = bf16[64,768]{1,0:T(8,128)(2,1)S(1)} collective-permute-done((bf16[64,768]{1,0:T(8,128)(2,1)S(1)}, bf16[64,768]{1,0:T(8,128)(2,1)S(1)}, u32[]{:S(2)}, u32[]{:S(2)}) %collective-permute-start.32) | collective-permute-done | bytes 98336 | tf_op jit(solution)/shard_map/ppermute | solution.py:21
  275.4 4.3 %collective-permute-done.19 = f32[1,1024]{1,0:T(1,128)S(1)} collective-permute-done((f32[1,1024]{1,0:T(1,128)S(1)}, f32[1,1024]{1,0:T(1,128)S(1)}, u32[]{:S(2)}, u32[]{:S(2)}) %collective-permute-start.19) | collective-permute-done | bytes 4128 | tf_op jit(solution)/shard_map/ppermute | solution.py:21
  279.8 3.6 %collective-permute-done.20 = f32[1,1024]{1,0:T(1,128)S(1)} collective-permute-done((f32[1,1024]{1,0:T(1,128)S(1)}, f32[1,1024]{1,0:T(1,128)S(1)}, u32[]{:S(2)}, u32[]{:S(2)}) %collective-permute-start.20) | collective-permute-done | bytes 4128 | tf_op jit(solution)/shard_map/ppermute | solution.py:21
  284.5 3.4 %collective-permute-done.21 = f32[1,1024]{1,0:T(1,128)S(1)} collective-permute-done((f32[1,1024]{1,0:T(1,128)S(1)}, f32[1,1024]{1,0:T(1,128)S(1)}, u32[]{:S(2)}, u32[]{:S(2)}) %collective-permute-start.21) | collective-permute-done | bytes 4128 | tf_op jit(solution)/shard_map/ppermute | solution.py:21
  (323 shorter events, 142.8 us)
Async XLA Ops:
  0.7 10.2 %collective-permute-start = (bf16[1,128,1024]{2,1,0:T(8,128)(2,1)}, bf16[1,128,1024]{2,1,0:T(8,128)(2,1)S(1)}, u32[]{:S(2)}, u32[]{:S(2)}) collective-permute-start(bf16[1,128,1024]{2,1,0:T(8,128)(2,1)} %bitcast.334), channel_id=1, source_target_pairs={{0,2},{1,3},{2,0},{3,1},{4,6},{5,7},{6,4},{7,5},{8,10},{9,11},{10,... | collective-permute-start | bytes 786440 | tf_op jit(solution)/shard_map/ppermute | solution.py:21
  37.6 15.6 %all-to-all-start = ((bf16[8,40,512]{2,1,0:T(8,128)(2,1)}), bf16[8,40,512]{2,1,0:T(8,128)(2,1)S(1)}, u32[]{:S(2)}, u32[]{:S(2)}) async-start(bf16[8,40,512]{2,1,0:T(8,128)(2,1)} %bitcast.20), calls=%async_computation | async-start | bytes 655360 | tf_op jit(solution)/shard_map/all_to_all | solution.py:48
  62.4 16.9 %all-to-all-start.1 = ((bf16[8,40,512]{2,1,0:T(8,128)(2,1)}), bf16[8,40,512]{2,1,0:T(8,128)(2,1)}, u32[]{:S(2)}, u32[]{:S(2)}) async-start(bf16[8,40,512]{2,1,0:T(8,128)(2,1)} %bitcast.347), calls=%async_computation.1 | async-start | bytes 655360 | tf_op jit(solution)/shard_map/all_to_all | solution.py:48
  79.3 12.2 %collective-permute-start.8 = (bf16[1,320,512]{2,1,0:T(8,128)(2,1)}, bf16[1,320,512]{2,1,0:T(8,128)(2,1)S(1)}, u32[]{:S(2)}, u32[]{:S(2)}) collective-permute-start(bf16[1,320,512]{2,1,0:T(8,128)(2,1)} %bitcast.41), channel_id=1, source_target_pairs={{0,2},{1,3},{2,0},{3,1},{4,6},{5,7},{6,4},{7,5},{8,10},{9,11},{10,... | collective-permute-start | bytes 983048 | tf_op jit(solution)/shard_map/ppermute | solution.py:21
  102.5 14.8 %collective-permute-start.10 = (bf16[2,320,512]{2,1,0:T(8,128)(2,1)S(1)}, bf16[2,320,512]{2,1,0:T(8,128)(2,1)S(1)}, u32[]{:S(2)}, u32[]{:S(2)}) collective-permute-start(bf16[2,320,512]{2,1,0:T(8,128)(2,1)S(1)} %slice_bitcast_fusion.1), channel_id=1, source_target_pairs={{0,1},{1,0},{2,3},{3,2},{4,5},{5,4},{6,7},{7,6},{8,9},{9,8},{10,11... | collective-permute-start | bytes 1966088 | tf_op jit(solution)/shard_map/ppermute | solution.py:21
  113.7 13.6 %all-to-all-start.2 = ((bf16[8,40,512]{2,1,0:T(8,128)(2,1)}), bf16[8,40,512]{2,1,0:T(8,128)(2,1)S(1)}, u32[]{:S(2)}, u32[]{:S(2)}) async-start(bf16[8,40,512]{2,1,0:T(8,128)(2,1)} %bitcast.38), calls=%async_computation.2 | async-start | bytes 655360 | tf_op jit(solution)/shard_map/all_to_all | solution.py:48
  129.3 14.4 %all-to-all-start.3 = ((bf16[8,40,512]{2,1,0:T(8,128)(2,1)}), bf16[8,40,512]{2,1,0:T(8,128)(2,1)S(1)}, u32[]{:S(2)}, u32[]{:S(2)}) async-start(bf16[8,40,512]{2,1,0:T(8,128)(2,1)} %bitcast.54), calls=%async_computation.3 | async-start | bytes 655360 | tf_op jit(solution)/shard_map/all_to_all | solution.py:48
  146.8 13.4 %collective-permute-start.12 = (bf16[1,128,1024]{2,1,0:T(8,128)(2,1)}, bf16[1,128,1024]{2,1,0:T(8,128)(2,1)}, u32[]{:S(2)}, u32[]{:S(2)}) collective-permute-start(bf16[1,128,1024]{2,1,0:T(8,128)(2,1)} %convert_bitcast_fusion), channel_id=1, source_target_pairs={{0,2},{1,3},{2,0},{3,1},{4,6},{5,7},{6,4},{7,5},{8,10},{9,11},{10,... | collective-permute-start | bytes 786440 | tf_op jit(solution)/shard_map/ppermute | solution.py:21
  147.8 10.1 %collective-permute-start.49 = (f32[17,1024]{1,0:T(8,128)S(1)}, f32[17,1024]{1,0:T(8,128)}, u32[]{:S(2)}, u32[]{:S(2)}) collective-permute-start(f32[17,1024]{1,0:T(8,128)S(1)} %fusion.89), channel_id=1, source_target_pairs={{0,2},{1,3},{2,0},{3,1},{4,6},{5,7},{6,4},{7,5},{8,10},{9,11},{10,... | collective-permute-start | bytes 208904 | tf_op jit(solution)/shard_map/ppermute | solution.py:21
  168.2 27.9 %collective-permute-start.52 = (f32[17,1024]{1,0:T(8,128)S(1)}, f32[17,1024]{1,0:T(8,128)S(1)}, u32[]{:S(2)}, u32[]{:S(2)}) collective-permute-start(f32[17,1024]{1,0:T(8,128)S(1)} %add.370), channel_id=1, source_target_pairs={{0,16},{4,20},{8,24},{12,28},{16,0},{20,4},{24,8},{28,12},{1,17},{... | collective-permute-start | bytes 208904 | tf_op jit(solution)/shard_map/ppermute | solution.py:21
  190.2 11.3 %collective-permute-start.14 = (bf16[128,1024]{1,0:T(8,128)(2,1)}, bf16[128,1024]{1,0:T(8,128)(2,1)}, u32[]{:S(2)}, u32[]{:S(2)}) collective-permute-start(bf16[128,1024]{1,0:T(8,128)(2,1)} %get-tuple-element.89), channel_id=1, source_target_pairs={{0,4},{4,0},{8,12},{12,8},{16,20},{20,16},{24,28},{28,24},{1,5},{5... | collective-permute-start | bytes 786440 | tf_op jit(solution)/shard_map/ppermute | solution.py:21
  210.4 46.7 %collective-permute-start.15 = (bf16[2,128,1024]{2,1,0:T(8,128)(2,1)S(1)}, bf16[2,128,1024]{2,1,0:T(8,128)(2,1)S(1)}, u32[]{:S(2)}, u32[]{:S(2)}) collective-permute-start(bf16[2,128,1024]{2,1,0:T(8,128)(2,1)S(1)} %fusion.24), channel_id=1, source_target_pairs={{0,1},{1,0},{2,3},{3,2},{4,5},{5,4},{6,7},{7,6},{8,9},{9,8},{10,11... | collective-permute-start | bytes 1572872 | tf_op jit(solution)/shard_map/ppermute | solution.py:21
  210.5 13.9 %collective-permute-start.22 = (bf16[256,768]{1,0:T(8,128)(2,1)S(1)}, bf16[256,768]{1,0:T(8,128)(2,1)S(1)}, u32[]{:S(2)}, u32[]{:S(2)}) collective-permute-start(bf16[256,768]{1,0:T(8,128)(2,1)S(1)} %dynamic-slice_bitcast_fusion.1), channel_id=1, source_target_pairs={{0,4},{4,0},{8,12},{12,8},{16,20},{20,16},{24,28},{28,24},{1,5},{5... | collective-permute-start | bytes 1179656 | tf_op jit(solution)/shard_map/ppermute | solution.py:21
  221.7 11.7 %collective-permute-start.30 = (bf16[256,768]{1,0:T(8,128)(2,1)S(1)}, bf16[256,768]{1,0:T(8,128)(2,1)S(1)}, u32[]{:S(2)}, u32[]{:S(2)}) collective-permute-start(bf16[256,768]{1,0:T(8,128)(2,1)S(1)} %dynamic-slice_bitcast_fusion), channel_id=1, source_target_pairs={{0,4},{4,0},{8,12},{12,8},{16,20},{20,16},{24,28},{28,24},{1,5},{5... | collective-permute-start | bytes 1179656 | tf_op jit(solution)/shard_map/ppermute | solution.py:21
  223.1 13.0 %collective-permute-start.44 = (bf16[4,32,1024]{2,1,0:T(8,128)(2,1)S(1)}, bf16[4,32,1024]{2,1,0:T(8,128)(2,1)S(1)}, u32[]{:S(2)}, u32[]{:S(2)}) collective-permute-start(bf16[4,32,1024]{2,1,0:T(8,128)(2,1)S(1)} %pad_maximum_fusion.11), channel_id=1, source_target_pairs={{0,4},{4,0},{8,12},{12,8},{16,20},{20,16},{24,28},{28,24},{1,5},{5... | collective-permute-start | bytes 786440 | tf_op jit(solution)/shard_map/ppermute | solution.py:21
  224.6 14.3 %collective-permute-start.23 = (bf16[64,768]{1,0:T(8,128)(2,1)S(1)}, bf16[64,768]{1,0:T(8,128)(2,1)S(1)}, u32[]{:S(2)}, u32[]{:S(2)}) collective-permute-start(bf16[64,768]{1,0:T(8,128)(2,1)S(1)} %get-tuple-element.103), channel_id=1, source_target_pairs={{0,8},{4,12},{8,0},{12,4},{16,24},{20,28},{24,16},{28,20},{1,9},{5... | collective-permute-start | bytes 294920 | tf_op jit(solution)/shard_map/ppermute | solution.py:21
  225.8 16.0 %collective-permute-start.25 = (bf16[64,768]{1,0:T(8,128)(2,1)S(1)}, bf16[64,768]{1,0:T(8,128)(2,1)S(1)}, u32[]{:S(2)}, u32[]{:S(2)}) collective-permute-start(bf16[64,768]{1,0:T(8,128)(2,1)S(1)} %get-tuple-element.104), channel_id=1, source_target_pairs={{0,24},{4,28},{8,16},{12,20},{16,8},{20,12},{24,0},{28,4},{1,25},{... | collective-permute-start | bytes 294920 | tf_op jit(solution)/shard_map/ppermute | solution.py:21
  241.8 13.0 %collective-permute-start.32 = (bf16[64,768]{1,0:T(8,128)(2,1)S(1)}, bf16[64,768]{1,0:T(8,128)(2,1)S(1)}, u32[]{:S(2)}, u32[]{:S(2)}) collective-permute-start(bf16[64,768]{1,0:T(8,128)(2,1)S(1)} %get-tuple-element.102), channel_id=1, source_target_pairs={{0,16},{4,20},{8,24},{12,28},{16,0},{20,4},{24,8},{28,12},{1,17},{... | collective-permute-start | bytes 294920 | tf_op jit(solution)/shard_map/ppermute | solution.py:21
  241.9 15.4 %collective-permute-start.28 = (bf16[64,768]{1,0:T(8,128)(2,1)S(1)}, bf16[64,768]{1,0:T(8,128)(2,1)S(1)}, u32[]{:S(2)}, u32[]{:S(2)}) collective-permute-start(bf16[64,768]{1,0:T(8,128)(2,1)S(1)} %get-tuple-element.77), channel_id=1, source_target_pairs={{0,24},{4,28},{8,16},{12,20},{16,8},{20,12},{24,0},{28,4},{1,25},{... | collective-permute-start | bytes 294920 | tf_op jit(solution)/shard_map/ppermute | solution.py:21
  243.4 19.0 %collective-permute-start.27 = (bf16[64,768]{1,0:T(8,128)(2,1)S(1)}, bf16[64,768]{1,0:T(8,128)(2,1)S(1)}, u32[]{:S(2)}, u32[]{:S(2)}) collective-permute-start(bf16[64,768]{1,0:T(8,128)(2,1)S(1)} %get-tuple-element.77), channel_id=1, source_target_pairs={{0,16},{4,20},{8,24},{12,28},{16,0},{20,4},{24,8},{28,12},{1,17},{... | collective-permute-start | bytes 294920 | tf_op jit(solution)/shard_map/ppermute | solution.py:21
  247.6 15.7 %collective-permute-start.26 = (bf16[64,768]{1,0:T(8,128)(2,1)S(1)}, bf16[64,768]{1,0:T(8,128)(2,1)S(1)}, u32[]{:S(2)}, u32[]{:S(2)}) collective-permute-start(bf16[64,768]{1,0:T(8,128)(2,1)S(1)} %get-tuple-element.77), channel_id=1, source_target_pairs={{0,8},{4,12},{8,0},{12,4},{16,24},{20,28},{24,16},{28,20},{1,9},{5... | collective-permute-start | bytes 294920 | tf_op jit(solution)/shard_map/ppermute | solution.py:21
  254.8 10.2 %collective-permute-start.36 = (bf16[64,768]{1,0:T(8,128)(2,1)S(1)}, bf16[64,768]{1,0:T(8,128)(2,1)S(1)}, u32[]{:S(2)}, u32[]{:S(2)}) collective-permute-start(bf16[64,768]{1,0:T(8,128)(2,1)S(1)} %get-tuple-element.75), channel_id=1, source_target_pairs={{0,24},{4,28},{8,16},{12,20},{16,8},{20,12},{24,0},{28,4},{1,25},{... | collective-permute-start | bytes 294920 | tf_op jit(solution)/shard_map/ppermute | solution.py:21
  263.4 25.1 %collective-permute-start.29 = (bf16[4,64,768]{2,1,0:T(8,128)(2,1)S(1)}, bf16[4,64,768]{2,1,0:T(8,128)(2,1)S(1)}, u32[]{:S(2)}, u32[]{:S(2)}) collective-permute-start(bf16[4,64,768]{2,1,0:T(8,128)(2,1)S(1)} %pad_maximum_fusion.9), channel_id=1, source_target_pairs={{0,4},{4,0},{8,12},{12,8},{16,20},{20,16},{24,28},{28,24},{1,5},{5... | collective-permute-start | bytes 1179656 | tf_op jit(solution)/shard_map/ppermute | solution.py:21
  266.9 21.8 %collective-permute-start.37 = (bf16[4,64,768]{2,1,0:T(8,128)(2,1)S(1)}, bf16[4,64,768]{2,1,0:T(8,128)(2,1)S(1)}, u32[]{:S(2)}, u32[]{:S(2)}) collective-permute-start(bf16[4,64,768]{2,1,0:T(8,128)(2,1)S(1)} %pad_maximum_fusion.10), channel_id=1, source_target_pairs={{0,4},{4,0},{8,12},{12,8},{16,20},{20,16},{24,28},{28,24},{1,5},{5... | collective-permute-start | bytes 1179656 | tf_op jit(solution)/shard_map/ppermute | solution.py:21
  (77 other events, 475.0 us)
where the time goes:
time: 292 us; the launch traced here: 291 us
  waiting for transfers between devices  112 us (38%)
  starting transfers between devices  79.9 us (27%)
  Pallas kernels  35.1 us (12%)
  local copies, waits for them, and re-layouts  21.3 us (7%)
  other arithmetic  20.2 us (7%)
  matrix products  19.8 us (7%)
    ppermute x53, waiting for transfers between devices, swap(): return lax.ppermute(block, axis, [(i, i ^ offset) for i in range(size)])  79.3 us
    ppermute x53, starting transfers between devices, swap(): return lax.ppermute(block, axis, [(i, i ^ offset) for i in range(size)])  58.9 us
    all_to_all x4, waiting for transfers between devices, exchange_groups(): return lax.all_to_all(buffer, 'dp', split_axis=0, concat_axis=0, tiled=True)  33.2 us
    all_to_all x4, starting transfers between devices, exchange_groups(): return lax.all_to_all(buffer, 'dp', split_axis=0, concat_axis=0, tiled=True)  21 us
    unnamed x120, local copies, waits for them, and re-layouts  14.3 us
    pallas_call x2, Pallas kernels, run_experts(): pl.pallas_call(functools.partial(expert_kernel, cuts, step), grid=(expert...  12.3 us
    pallas_call x1, Pallas kernels, bucket_grad(): pl.pallas_call(functools.partial(bucket_kernel, buckets), grid=(seq_len /...  7.61 us
    another operation x8, other arithmetic, gather_members(): held = jnp.stack([held, other], axis=1).reshape((-1,) + block.shape)  7.3 us
  transfers between devices with their start and end apart: 57, of which 32 were waited for; matrix products, arithmetic and copies ran while one was open for 12% of the time, Pallas kernels for 8%

commit v1 on v0

--- a/solution.py
+++ b/solution.py
@@ -35,13 +35,20 @@
     return held if beside is None else (held, beside)
 
 
-def scatter_pairs(keep, received, first_bit):
+def core_hop(blocks):
+    pairs = blocks.reshape((-1, 2) + blocks.shape[1:])
+    return pairs[:, 0], swap(pairs[:, 1].astype(bf16), "mp", 1)
+
+
+def scatter_rest(keep, received, beside=None):
     held = keep.astype(f32) + received.astype(f32)
-    for bit in range(first_bit, bit_count("mp")):
+    for bit in range(1, bit_count("mp")):
         halves = held.reshape((-1, 2) + held.shape[1:])
         got = swap(halves[:, 1].astype(bf16), "mp", 1 << bit)
+        if beside is not None and bit == 1:
+            got, beside = lax.optimization_barrier((got, beside))
         held = halves[:, 0] + got.astype(f32)
-    return held[0]
+    return held[0] if beside is None else (held[0], beside)
 
 
 def exchange_groups(buffer):
@@ -55,7 +62,7 @@
     return lax.dynamic_index_in_dim(halves, mine, 0, keepdims=False), got
 
 
-def far_steps(keep, got):
+def far_sums(keep, got):
     rest = lax.axis_size("dp") // 2
     mine = lax.axis_index("dp") >> 1
     held = (keep.astype(f32) + got.astype(f32)).astype(bf16)
@@ -64,15 +71,19 @@
     def block_of(offset):
         return lax.dynamic_index_in_dim(blocks, mine ^ offset, 0, keepdims=False)
 
-    parts = [swap(block_of(offset), "dp", 2 * offset) for offset in range(1, rest)]
-    total = block_of(0).astype(f32)
-    for item in parts:
+    return [block_of(0)] + [swap(block_of(offset), "dp", 2 * offset) for offset in range(1, rest)]
+
+
+def far_gather(parts):
+    total = parts[0].astype(f32)
+    for item in parts[1:]:
         total = total + item.astype(f32)
     own = total.astype(bf16)
-    return jnp.stack([own] + [swap(own, "dp", 2 * offset) for offset in range(1, rest)])
-
-
-def last_step(own_half):
+    return [own] + [swap(own, "dp", 2 * offset) for offset in range(1, len(parts))]
+
+
+def last_step(parts):
+    own_half = jnp.stack(parts)
     other = swap(own_half, "dp", 1)
     rest = lax.axis_size("dp") // 2
     me = lax.axis_index("dp")
@@ -126,7 +137,7 @@
             jax.ShapeDtypeStruct((heads, seq_len, seq_len), f32),
             jax.ShapeDtypeStruct((seq_len, seq_len), jnp.int32),
         ],
-        compiler_params=pltpu.CompilerParams(vmem_limit_bytes=32 * MIB),
+        compiler_params=pltpu.CompilerParams(vmem_limit_bytes=8 * MIB),
         cost_estimate=pl.CostEstimate(
             flops=seq_len * seq_len * heads, bytes_accessed=4 * seq_len * seq_len * (heads + 2), transcendentals=0
         ),
@@ -165,7 +176,7 @@
         ],
         out_specs=pl.BlockSpec((buckets, heads * rows), lambda i: (0, 0)),
         out_shape=jax.ShapeDtypeStruct((buckets, heads * rows), f32),
-        compiler_params=pltpu.CompilerParams(vmem_limit_bytes=32 * MIB),
+        compiler_params=pltpu.CompilerParams(vmem_limit_bytes=16 * MIB),
         cost_estimate=pl.CostEstimate(
             flops=2 * seqs * seq_len * buckets * seq_len * heads * rows,
             bytes_accessed=2 * seqs * heads * seq_len * seq_len + 4 * seq_len * seq_len,
@@ -223,7 +234,7 @@
             jax.ShapeDtypeStruct((tokens, head_cols), bf16),
             jax.ShapeDtypeStruct((seqs, heads, seq_len, seq_len), f32),
         ],
-        compiler_params=pltpu.CompilerParams(vmem_limit_bytes=32 * MIB),
+        compiler_params=pltpu.CompilerParams(vmem_limit_bytes=20 * MIB),
         cost_estimate=pl.CostEstimate(
             flops=4 * seqs * heads * seq_len * seq_len * head_size,
             bytes_accessed=8 * seqs * heads * seq_len * seq_len,
@@ -290,7 +301,7 @@
             jax.ShapeDtypeStruct((tokens, width), bf16),
             jax.ShapeDtypeStruct((seqs, heads, seq_len, seq_len), bf16),
         ],
-        compiler_params=pltpu.CompilerParams(vmem_limit_bytes=32 * MIB),
+        compiler_params=pltpu.CompilerParams(vmem_limit_bytes=20 * MIB),
         cost_estimate=pl.CostEstimate(
             flops=8 * seqs * heads * seq_len * seq_len * head_size,
             bytes_accessed=6 * seqs * heads * seq_len * seq_len,
@@ -392,7 +403,7 @@
         in_specs=in_specs,
         out_specs=out_specs,
         out_shape=out_shape,
-        compiler_params=pltpu.CompilerParams(vmem_limit_bytes=40 * MIB),
+        compiler_params=pltpu.CompilerParams(vmem_limit_bytes=24 * MIB),
         cost_estimate=pl.CostEstimate(
             flops=4 * experts * rows * units * width,
             bytes_accessed=4 * experts * units * width + 12 * experts * rows * width,
@@ -454,7 +465,7 @@
         return jnp.einsum("stc,cd->std", rows, w_output, preferred_element_type=f32)
 
     attn_got = swap(project(mixed_pairs[:, 1]).astype(bf16), "mp", 1)
-    attn = scatter_pairs(project(mixed_pairs[:, 0]), attn_got, 1)
+    attn = scatter_rest(project(mixed_pairs[:, 0]), attn_got)
     middle = tokens.astype(f32) + attn
 
     middle_root = root_inverse(middle)
@@ -498,10 +509,7 @@
     def send_rows(rows):
         return exchange_groups(jnp.dot(placement, cut_rows(rows), preferred_element_type=f32).astype(bf16))
 
-    def collect(blocks):
-        pairs = blocks.reshape(member_count // 2, 2, all_rows, piece)
-        got = swap(pairs[:, 1], "mp", 1)
-        back = exchange_groups(scatter_pairs(pairs[:, 0], got, 1).astype(bf16))
+    def place_back(back):
         rows = lax.dot_general(placement, back, (((0,), (0,)), ((), ())), preferred_element_type=f32)
         return join_rows(rows)
 
@@ -514,18 +522,22 @@
     upstream = cotangent.astype(f32)
     sent = send_rows(moe_low)
     grad_sent = send_rows((gate_prob * upstream).astype(bf16))
-    arrived = gather_members(sent)
-
-    arrived, grad_sent = lax.optimization_barrier((arrived, grad_sent))
-    grad_arrived = gather_members(grad_sent)
+    arrived, grad_sent = gather_members(sent, grad_sent)
+
     pre, hidden, expert_in, value_blocks = run_experts(arrived, sorting, unsorting, w_in_t, w_out, cuts)
+    grad_arrived, value_blocks = gather_members(grad_sent, value_blocks)
+    value_hop = core_hop(value_blocks)
     pre_grad, result_grad, rows_blocks = run_experts(grad_arrived, sorting, unsorting, w_out, w_in_t, cuts, pre)
-    combined = collect(value_blocks)
-    moe_grad = collect(rows_blocks)
+    value_sum, rows_blocks = scatter_rest(*value_hop, beside=rows_blocks)
+    rows_hop = core_hop(rows_blocks)
+    value_back = exchange_groups(value_sum.astype(bf16))
+    rows_sum, value_back = scatter_rest(*rows_hop, beside=value_back)
+    rows_back = exchange_groups(rows_sum.astype(bf16))
     grad_w_out = jnp.einsum("jrf,jrd->jfd", hidden, result_grad, preferred_element_type=f32)
-    grad_w_in = jnp.swapaxes(
-        jnp.einsum("jrf,jrd->jfd", pre_grad, expert_in, preferred_element_type=f32), 1, 2
-    )
+    rows_back, grad_w_out = lax.optimization_barrier((rows_back, grad_w_out))
+    grad_w_in_t = jnp.einsum("jrf,jrd->jfd", pre_grad, expert_in, preferred_element_type=f32)
+    combined = place_back(value_back)
+    moe_grad = place_back(rows_back)
 
     block_out = (middle + gate_prob * combined).astype(bf16)
     gate_grad = jnp.sum(upstream * combined, axis=-1, keepdims=True)
@@ -540,26 +552,43 @@
         scaled - unit_moe * jnp.mean(scaled * unit_moe, axis=-1, keepdims=True)
     )
 
-    grad_rows = gather_members(middle_grad.astype(bf16)).reshape(group_tokens, width)
+    grad_rows, grad_w_in_t = gather_members(middle_grad.astype(bf16), grad_w_in_t)
+    grad_rows = grad_rows.reshape(group_tokens, width)
+    grad_w_in = jnp.swapaxes(grad_w_in_t, 1, 2)
     mixed_grad = jnp.einsum("td,cd->tc", grad_rows, w_output, preferred_element_type=f32).astype(bf16)
     output_part = jnp.einsum("tc,td->cd", mixed, grad_rows, preferred_element_type=f32).astype(bf16)
     output_near = near_step(output_part)
     joined_grad, score_grad = attend_back(joined, mixed_grad, probs, head_size)
     output_near, joined_grad = lax.optimization_barrier((output_near, joined_grad))
-    joined_near = []
+    locals_ = []
     for half in range(2):
         columns = normed_low[:, half * (width // 2) : (half + 1) * (width // 2)]
-        local = jnp.einsum("td,tc->dc", columns, joined_grad, preferred_element_type=f32).astype(bf16)
-        joined_near.append(near_step(local))
-    grad_w_output = last_step(far_steps(*output_near))
-    grad_joined = jnp.concatenate([last_step(far_steps(*near)) for near in joined_near], axis=0)
+        locals_.append(jnp.einsum("td,tc->dc", columns, joined_grad, preferred_element_type=f32).astype(bf16))
+    locals_, joined_grad, score_grad = lax.optimization_barrier((locals_, joined_grad, score_grad))
+    first_near = near_step(locals_[0])
+    second_near = near_step(locals_[1])
+    output_sums = far_sums(*output_near)
+    attn_partial = jnp.einsum("tc,dc->td", joined_grad, w_joined, preferred_element_type=f32)
+    attn_hop = core_hop(attn_partial.reshape(member_count, tok_dev, width))
+    gain_partial = jnp.sum(attn_partial * unit_attn, axis=0, keepdims=True)
+    first_near, output_sums, attn_hop, score_grad = lax.optimization_barrier(
+        (first_near, output_sums, attn_hop, score_grad)
+    )
+    first_sums = far_sums(*first_near)
+    output_parts = far_gather(output_sums)
+    bucket_part = bucket_grad(moved_table, score_grad, rel_bias.shape[0])
+    first_sums, second_near, bucket_part, output_parts = lax.optimization_barrier(
+        (first_sums, second_near, bucket_part, output_parts)
+    )
+    second_sums = far_sums(*second_near)
+    first_parts = far_gather(first_sums)
+    attn_grad = scatter_rest(*attn_hop)
+    grad_w_output = last_step(output_parts)
+    second_parts = far_gather(second_sums)
+    grad_joined = jnp.concatenate([last_step(first_parts), last_step(second_parts)], axis=0)
     grad_w_query, grad_w_key, grad_w_value = [
         grad_joined[:, part * head_cols : (part + 1) * head_cols] for part in range(3)
     ]
-    attn_partial = jnp.einsum("tc,dc->td", joined_grad, w_joined, preferred_element_type=f32)
-    attn_pairs = attn_partial.reshape(member_count // 2, 2, tok_dev, width)
-    back_got = swap(attn_pairs[:, 1].astype(bf16), "mp", 1)
-    attn_grad = scatter_pairs(attn_pairs[:, 0], back_got, 1)
     own_tokens = tokens.astype(f32)
     own_root = root_inverse(own_tokens)
     own_unit = own_tokens * own_root
@@ -567,20 +596,23 @@
     input_grad = (
         middle_grad + own_root * (scaled - own_unit * jnp.mean(scaled * own_unit, axis=-1, keepdims=True))
     ).astype(bf16)
-    grad_gain_attn = sum_all(jnp.sum(attn_grad * own_unit, axis=0, keepdims=True), ("mp", "dp"))[0]
-    small = sum_all(jnp.concatenate([grad_gain_moe, grad_router_t], axis=0), ("mp", "dp"))
-    grad_rel_bias = sum_all(bucket_grad(moved_table, score_grad, rel_bias.shape[0]), ("dp",))
+    bucket_row = lax.dynamic_update_slice(
+        jnp.zeros((1, width), f32), bucket_part.reshape(1, -1), (0, member * bucket_part.size)
+    )
+    small = sum_all(jnp.concatenate([grad_gain_moe, gain_partial, bucket_row, grad_router_t], axis=0), ("mp", "dp"))
+    grad_rel_bias = lax.dynamic_slice(small[2:3], (0, member * bucket_part.size), (1, bucket_part.size))
+    grad_rel_bias = grad_rel_bias.reshape(bucket_part.shape)
     return (
         block_out,
         input_grad,
-        grad_gain_attn,
+        small[1],
         grad_w_query,
         grad_w_key,
         grad_w_value,
         grad_w_output,
         grad_rel_bias,
         small[0],
-        small[1:].T,
+        small[3:].T,
         grad_w_in,
         grad_w_out,
     )

time: 292 us -> 242 us (0.83)
  waiting for transfers between devices: 112 us -> 74 us
  starting transfers between devices: 79.9 us -> 67.4 us
  local copies, waits for them, and re-layouts: 21.3 us -> 25.3 us
    ppermute x53 -> x45, waiting for transfers between devices: 79.3 us -> 44.4 us  [swap(): return lax.ppermute(block, axis, [(i, i ^ offset) for i in range(size)])]
    ppermute x53 -> x45, starting transfers between devices: 58.9 us -> 46.7 us  [swap(): return lax.ppermute(block, axis, [(i, i ^ offset) for i in range(size)])]
    all_to_all x4, waiting for transfers between devices: 33.2 us -> 29.5 us  [exchange_groups(): return lax.all_to_all(buffer, 'dp', split_axis=0, concat_axis=0, tiled=True)]
    unnamed x120 -> x145, local copies, waits for them, and re-layouts: 14.3 us -> 17.7 us
    another operation x8, other arithmetic: 7.3 us -> 4.05 us  [gather_members(): held = jnp.stack([held, other], axis=1).reshape((-1,) + block.shape)]
  transfers between devices with their start and end apart: 57 -> 49, of which waited for: 32 -> 25; matrix products, arithmetic and copies ran while one was open for 12% -> 15% of each run, Pallas kernels for 8% -> 12%
where the time goes in v1:
time: 242 us; the launch traced here: 240 us
  waiting for transfers between devices  74 us (31%)
  starting transfers between devices  67.4 us (28%)
  Pallas kernels  35.1 us (15%)
  local copies, waits for them, and re-layouts  25.3 us (10%)
  matrix products  18.9 us (8%)
  other arithmetic  17.7 us (7%)
    ppermute x45, starting transfers between devices, swap(): return lax.ppermute(block, axis, [(i, i ^ offset) for i in range(size)])  46.7 us
    ppermute x45, waiting for transfers between devices, swap(): return lax.ppermute(block, axis, [(i, i ^ offset) for i in range(size)])  44.4 us
    all_to_all x4, waiting for transfers between devices, exchange_groups(): return lax.all_to_all(buffer, 'dp', split_axis=0, concat_axis=0, tiled=True)  29.5 us
    all_to_all x4, starting transfers between devices, exchange_groups(): return lax.all_to_all(buffer, 'dp', split_axis=0, concat_axis=0, tiled=True)  20.7 us
    unnamed x145, local copies, waits for them, and re-layouts  17.7 us
    pallas_call x2, Pallas kernels, run_experts(): pl.pallas_call(functools.partial(expert_kernel, cuts, step), grid=(expert...  12.3 us
    pallas_call x1, Pallas kernels, bucket_grad(): pl.pallas_call(functools.partial(bucket_kernel, buckets), grid=(seq_len /...  7.6 us
    pallas_call x1, Pallas kernels, attend(): pl.pallas_call(functools.partial(attend_kernel, head_size), grid=(seqs, h...  6.11 us
  transfers between devices with their start and end apart: 49, of which 25 were waited for; matrix products, arithmetic and copies ran while one was open for 15% of the time, Pallas kernels for 12%

profile of v1, /device:TPU:0, one launch (start us, length us, event | category | flops | bytes accessed | tf_op | source)
XLA Modules:
  0.0 240.5 jit_solution(14555137743248046853)
XLA Ops:
  0.7 3.0 %collective-permute-start = (bf16[1,128,1024]{2,1,0:T(8,128)(2,1)}, bf16[1,128,1024]{2,1,0:T(8,128)(2,1)S(1)}, u32[]{:S(2)}, u32[]{:S(2)}) collective-permute-start(bf16[1,128,1024]{2,1,0:T(8,128)(2,1)} %bitcast.326), channel_id=1, source_target_pairs={{0,2},{1,3},{2,0},{3,1},{4,6},{5,7},{6,4},{7,5},{8,10},{9,11},{10,... | collective-permute-start | bytes 786440 | tf_op jit(solution)/shard_map/ppermute | solution.py:21
  5.6 3.3 %bias_lookup.1 = (f32[4,512,512]{2,1,0:T(8,128)S(1)}, s32[512,512]{1,0:T(8,128)S(1)}) custom-call(s32[1]{0:T(128)} %bitcast.2.shift_ref, s32[512,512]{1,0:T(8,128)S(1)} %copy-done.17, f32[4,128]{1,0:T(4,128)S(1)} %pad.4.bucket_ref), custom_call_target="tpu_custom_call" | custom-call | flops 1048576 | bytes 6291456 | tf_op jit(solution)/shard_map/bias_lookup/pallas_call | solution.py:122
  17.7 6.1 %attend.1 = (bf16[512,256]{1,0:T(8,128)(2,1)S(1)}, f32[1,4,512,512]{3,2,1,0:T(8,128)S(1)}) custom-call(bf16[512,768]{1,0:T(8,128)(2,1)S(1)} %convolution_convert_fusion.2.joined_ref, f32[4,512,512]{2,1,0:T(8,128)S(1)} %get-tuple-element.72.bias_ref), custom_call_target="tpu_custom_call" | custom-call | flops 268435456 | bytes 8388608 | tf_op jit(solution)/shard_map/attend/pallas_call | solution.py:222
  29.2 7.8 %collective-permute-done.3 = bf16[1,128,1024]{2,1,0:T(8,128)(2,1)S(1)} collective-permute-done((bf16[1,128,1024]{2,1,0:T(8,128)(2,1)S(1)}, bf16[1,128,1024]{2,1,0:T(8,128)(2,1)S(1)}, u32[]{:S(2)}, u32[]{:S(2)}) %collective-permute-start.3) | collective-permute-done | bytes 262176 | tf_op jit(solution)/shard_map/ppermute | solution.py:21
  40.8 5.8 %all-to-all-start = ((bf16[8,40,512]{2,1,0:T(8,128)(2,1)}), bf16[8,40,512]{2,1,0:T(8,128)(2,1)}, u32[]{:S(2)}, u32[]{:S(2)}) async-start(bf16[8,40,512]{2,1,0:T(8,128)(2,1)} %bitcast.19), calls=%async_computation | async-start | bytes 655360 | tf_op jit(solution)/shard_map/all_to_all | solution.py:55
  47.8 8.7 %all-to-all-done = bf16[8,40,512]{2,1,0:T(8,128)(2,1)} async-done(((bf16[8,40,512]{2,1,0:T(8,128)(2,1)}), bf16[8,40,512]{2,1,0:T(8,128)(2,1)}, u32[]{:S(2)}, u32[]{:S(2)}) %all-to-all-start) | async-done | bytes 327712 | tf_op jit(solution)/shard_map/all_to_all | solution.py:55
  56.5 4.3 %all-to-all-start.1 = ((bf16[8,40,512]{2,1,0:T(8,128)(2,1)}), bf16[8,40,512]{2,1,0:T(8,128)(2,1)}, u32[]{:S(2)}, u32[]{:S(2)}) async-start(bf16[8,40,512]{2,1,0:T(8,128)(2,1)} %bitcast.338), calls=%async_computation.1 | async-start | bytes 655360 | tf_op jit(solution)/shard_map/all_to_all | solution.py:55
  61.3 8.8 %all-to-all-done.1 = bf16[8,40,512]{2,1,0:T(8,128)(2,1)} async-done(((bf16[8,40,512]{2,1,0:T(8,128)(2,1)}), bf16[8,40,512]{2,1,0:T(8,128)(2,1)}, u32[]{:S(2)}, u32[]{:S(2)}) %all-to-all-start.1) | async-done | bytes 327712 | tf_op jit(solution)/shard_map/all_to_all | solution.py:55
  75.6 5.9 %experts.1 = (f32[2,320,704]{2,1,0:T(8,128)S(1)}, bf16[2,320,704]{2,1,0:T(8,128)(2,1)S(1)}, bf16[2,320,1024]{2,1,0:T(8,128)(2,1)S(1)}, bf16[4,320,512]{2,1,0:T(8,128)(2,1)S(1)}) custom-call(bf16[4,320,512]{2,1,0:T(8,128)(2,1)S(1)} %bitcast.314, bf16[2,160,320]{2,1,0:T(8,128)(2,1)S(1)} %copy-done.22, bf16[2,320,160]{2,1,0:T(8,128)(2,1)S(1)} %copy-done.13, ...), custom_call_target="tpu_custom_call" | custom-call | flops 1845493760 | bytes 13631488 | tf_op jit(solution)/shard_map/experts/pallas_call | solution.py:400
  85.6 6.4 %experts_back.1 = (bf16[2,320,704]{2,1,0:T(8,128)(2,1)S(1)}, bf16[2,320,1024]{2,1,0:T(8,128)(2,1)S(1)}, bf16[4,320,512]{2,1,0:T(8,128)(2,1)S(1)}) custom-call(bf16[4,320,512]{2,1,0:T(8,128)(2,1)S(1)} %bitcast.313, bf16[2,160,320]{2,1,0:T(8,128)(2,1)S(1)} %copy-done.23, bf16[2,320,160]{2,1,0:T(8,128)(2,1)S(1)} %copy-done.14, ...), custom_call_target="tpu_custom_call" | custom-call | flops 1845493760 | bytes 13631488 | tf_op jit(solution)/shard_map/experts_back/pallas_call | solution.py:400
  95.6 4.8 %all-to-all-start.2 = ((bf16[8,40,512]{2,1,0:T(8,128)(2,1)}), bf16[8,40,512]{2,1,0:T(8,128)(2,1)}, u32[]{:S(2)}, u32[]{:S(2)}) async-start(bf16[8,40,512]{2,1,0:T(8,128)(2,1)} %bitcast.50), calls=%async_computation.2 | async-start | bytes 655360 | tf_op jit(solution)/shard_map/all_to_all | solution.py:55
  102.7 4.3 %fusion.89 = f32[2,704,1024]{2,1,0:T(8,128)} fusion(bf16[2,320,704]{2,1,0:T(8,128)(2,1)S(1)} %copy-done.21, bf16[2,320,1024]{2,1,0:T(8,128)(2,1)S(1)} %copy-done.12), kind=kOutput, calls=%fused_computation.231 | convolution fusion | flops 922746880 | bytes 7979008 | tf_op jit(solution)/shard_map/jrf,jrd->jfd/dot_general | solution.py:536
  106.9 4.3 %all-to-all-done.2 = bf16[8,40,512]{2,1,0:T(8,128)(2,1)} async-done(((bf16[8,40,512]{2,1,0:T(8,128)(2,1)}), bf16[8,40,512]{2,1,0:T(8,128)(2,1)}, u32[]{:S(2)}, u32[]{:S(2)}) %all-to-all-start.2) | async-done | bytes 327712 | tf_op jit(solution)/shard_map/all_to_all | solution.py:55
  112.4 5.8 %all-to-all-start.3 = ((bf16[8,40,512]{2,1,0:T(8,128)(2,1)}), bf16[8,40,512]{2,1,0:T(8,128)(2,1)S(1)}, u32[]{:S(2)}, u32[]{:S(2)}) async-start(bf16[8,40,512]{2,1,0:T(8,128)(2,1)} %bitcast.53), calls=%async_computation.3 | async-start | bytes 655360 | tf_op jit(solution)/shard_map/all_to_all | solution.py:55
  119.7 7.8 %all-to-all-done.3 = bf16[8,40,512]{2,1,0:T(8,128)(2,1)S(1)} async-done(((bf16[8,40,512]{2,1,0:T(8,128)(2,1)}), bf16[8,40,512]{2,1,0:T(8,128)(2,1)S(1)}, u32[]{:S(2)}, u32[]{:S(2)}) %all-to-all-start.3) | async-done | bytes 327712 | tf_op jit(solution)/shard_map/all_to_all | solution.py:55
  131.0 4.3 %fusion.91 = f32[2,704,1024]{2,1,0:T(8,128)} fusion(bf16[2,320,704]{2,1,0:T(8,128)(2,1)S(1)} %copy-done.19, bf16[2,320,1024]{2,1,0:T(8,128)(2,1)S(1)} %copy-done.10), kind=kOutput, calls=%fused_computation.233 | convolution fusion | flops 922746880 | bytes 7979008 | tf_op jit(solution)/shard_map/jrf,jrd->jfd/dot_general | solution.py:538
  141.8 5.8 %attend_back.1 = (bf16[512,768]{1,0:T(8,128)(2,1)S(1)}, bf16[1,4,512,512]{3,2,1,0:T(8,128)(2,1)S(1)}) custom-call(bf16[512,768]{1,0:T(8,128)(2,1)S(1)} %copy-done.6, bf16[512,256]{1,0:T(8,128)(2,1)S(1)} %convolution_convert_fusion.7.grad_ref, f32[1,4,512,512]{3,2,1,0:T(8,128)S(1)} %copy-done.4), custom_call_target="tpu_custom_call" | custom-call | flops 536870912 | bytes 6291456 | tf_op jit(solution)/shard_map/attend_back/pallas_call | solution.py:288
  157.0 2.4 collective-permute-start.24
  159.3 2.5 %collective-permute-done.17 = bf16[32,1024]{1,0:T(8,128)(2,1)S(1)} collective-permute-done((bf16[32,1024]{1,0:T(8,128)(2,1)S(1)}, bf16[32,1024]{1,0:T(8,128)(2,1)S(1)}, u32[]{:S(2)}, u32[]{:S(2)}) %collective-permute-start.17) | collective-permute-done | bytes 65568 | tf_op jit(solution)/shard_map/ppermute | solution.py:21
  173.7 7.6 %bucket_grad.1 = f32[32,128]{1,0:T(8,128)S(1)} custom-call(s32[512,512]{1,0:T(8,128)S(1)} %copy-done.25, bf16[1,4,512,512]{3,2,1,0:T(8,128)(2,1)S(1)} %get-tuple-element.106.grad_ref), custom_call_target="tpu_custom_call" | custom-call | flops 2147483648 | bytes 3145728 | tf_op jit(solution)/shard_map/bucket_grad/pallas_call | solution.py:170
  194.9 3.2 %collective-permute-start.34 = (bf16[64,768]{1,0:T(8,128)(2,1)S(1)}, bf16[64,768]{1,0:T(8,128)(2,1)S(1)}, u32[]{:S(2)}, u32[]{:S(2)}) collective-permute-start(bf16[64,768]{1,0:T(8,128)(2,1)S(1)} %get-tuple-element.177), channel_id=1, source_target_pairs={{0,16},{4,20},{8,24},{12,28},{16,0},{20,4},{24,8},{28,12},{1,17},{... | collective-permute-start | bytes 294920 | tf_op jit(solution)/shard_map/ppermute | solution.py:21
  216.6 7.9 %collective-permute-done.30 = f32[19,1024]{1,0:T(8,128)S(1)} collective-permute-done((f32[19,1024]{1,0:T(8,128)S(1)}, f32[19,1024]{1,0:T(8,128)S(1)}, u32[]{:S(2)}, u32[]{:S(2)}) %collective-permute-start.30) | collective-permute-done | bytes 77856 | tf_op jit(solution)/shard_map/ppermute | solution.py:21
  224.7 4.7 %collective-permute-done.31 = f32[19,1024]{1,0:T(8,128)S(1)} collective-permute-done((f32[19,1024]{1,0:T(8,128)S(1)}, f32[19,1024]{1,0:T(8,128)S(1)}, u32[]{:S(2)}, u32[]{:S(2)}) %collective-permute-start.31) | collective-permute-done | bytes 77856 | tf_op jit(solution)/shard_map/ppermute | solution.py:21
  230.7 4.6 %collective-permute-done.32 = f32[19,1024]{1,0:T(8,128)S(1)} collective-permute-done((f32[19,1024]{1,0:T(8,128)S(1)}, f32[19,1024]{1,0:T(8,128)S(1)}, u32[]{:S(2)}, u32[]{:S(2)}) %collective-permute-start.32) | collective-permute-done | bytes 77856 | tf_op jit(solution)/shard_map/ppermute | solution.py:21
  (332 shorter events, 108.4 us)
Async XLA Ops:
  0.7 10.8 %collective-permute-start = (bf16[1,128,1024]{2,1,0:T(8,128)(2,1)}, bf16[1,128,1024]{2,1,0:T(8,128)(2,1)S(1)}, u32[]{:S(2)}, u32[]{:S(2)}) collective-permute-start(bf16[1,128,1024]{2,1,0:T(8,128)(2,1)} %bitcast.326), channel_id=1, source_target_pairs={{0,2},{1,3},{2,0},{3,1},{4,6},{5,7},{6,4},{7,5},{8,10},{9,11},{10,... | collective-permute-start | bytes 786440 | tf_op jit(solution)/shard_map/ppermute | solution.py:21
  40.8 15.7 %all-to-all-start = ((bf16[8,40,512]{2,1,0:T(8,128)(2,1)}), bf16[8,40,512]{2,1,0:T(8,128)(2,1)}, u32[]{:S(2)}, u32[]{:S(2)}) async-start(bf16[8,40,512]{2,1,0:T(8,128)(2,1)} %bitcast.19), calls=%async_computation | async-start | bytes 655360 | tf_op jit(solution)/shard_map/all_to_all | solution.py:55
  56.5 13.6 %all-to-all-start.1 = ((bf16[8,40,512]{2,1,0:T(8,128)(2,1)}), bf16[8,40,512]{2,1,0:T(8,128)(2,1)}, u32[]{:S(2)}, u32[]{:S(2)}) async-start(bf16[8,40,512]{2,1,0:T(8,128)(2,1)} %bitcast.338), calls=%async_computation.1 | async-start | bytes 655360 | tf_op jit(solution)/shard_map/all_to_all | solution.py:55
  71.5 10.3 %collective-permute-start.5 = (bf16[1,320,512]{2,1,0:T(8,128)(2,1)}, bf16[1,320,512]{2,1,0:T(8,128)(2,1)S(1)}, u32[]{:S(2)}, u32[]{:S(2)}) collective-permute-start(bf16[1,320,512]{2,1,0:T(8,128)(2,1)} %bitcast.23), channel_id=1, source_target_pairs={{0,2},{1,3},{2,0},{3,1},{4,6},{5,7},{6,4},{7,5},{8,10},{9,11},{10,... | collective-permute-start | bytes 983048 | tf_op jit(solution)/shard_map/ppermute | solution.py:21
  84.3 9.8 %collective-permute-start.8 = (bf16[1,320,512]{2,1,0:T(8,128)(2,1)S(1)}, bf16[1,320,512]{2,1,0:T(8,128)(2,1)S(1)}, u32[]{:S(2)}, u32[]{:S(2)}) collective-permute-start(bf16[1,320,512]{2,1,0:T(8,128)(2,1)S(1)} %fusion.37), channel_id=1, source_target_pairs={{0,2},{1,3},{2,0},{3,1},{4,6},{5,7},{6,4},{7,5},{8,10},{9,11},{10,... | collective-permute-start | bytes 983048 | tf_op jit(solution)/shard_map/ppermute | solution.py:21
  95.6 15.6 %all-to-all-start.2 = ((bf16[8,40,512]{2,1,0:T(8,128)(2,1)}), bf16[8,40,512]{2,1,0:T(8,128)(2,1)}, u32[]{:S(2)}, u32[]{:S(2)}) async-start(bf16[8,40,512]{2,1,0:T(8,128)(2,1)} %bitcast.50), calls=%async_computation.2 | async-start | bytes 655360 | tf_op jit(solution)/shard_map/all_to_all | solution.py:55
  112.4 15.1 %all-to-all-start.3 = ((bf16[8,40,512]{2,1,0:T(8,128)(2,1)}), bf16[8,40,512]{2,1,0:T(8,128)(2,1)S(1)}, u32[]{:S(2)}, u32[]{:S(2)}) async-start(bf16[8,40,512]{2,1,0:T(8,128)(2,1)} %bitcast.53), calls=%async_computation.3 | async-start | bytes 655360 | tf_op jit(solution)/shard_map/all_to_all | solution.py:55
  149.5 12.4 %collective-permute-start.15 = (bf16[256,768]{1,0:T(8,128)(2,1)S(1)}, bf16[256,768]{1,0:T(8,128)(2,1)S(1)}, u32[]{:S(2)}, u32[]{:S(2)}) collective-permute-start(bf16[256,768]{1,0:T(8,128)(2,1)S(1)} %get-tuple-element.187), channel_id=1, source_target_pairs={{0,4},{4,0},{8,12},{12,8},{16,20},{20,16},{24,28},{28,24},{1,5},{5... | collective-permute-start | bytes 1179656 | tf_op jit(solution)/shard_map/ppermute | solution.py:21
  152.2 9.7 %collective-permute-start.19 = (bf16[2,128,1024]{2,1,0:T(8,128)(2,1)S(1)}, bf16[2,128,1024]{2,1,0:T(8,128)(2,1)S(1)}, u32[]{:S(2)}, u32[]{:S(2)}) collective-permute-start(bf16[2,128,1024]{2,1,0:T(8,128)(2,1)S(1)} %fusion.16), channel_id=1, source_target_pairs={{0,1},{1,0},{2,3},{3,2},{4,5},{5,4},{6,7},{7,6},{8,9},{9,8},{10,11... | collective-permute-start | bytes 1572872 | tf_op jit(solution)/shard_map/ppermute | solution.py:21
  157.0 12.1 %collective-permute-start.24 = (bf16[256,768]{1,0:T(8,128)(2,1)S(1)}, bf16[256,768]{1,0:T(8,128)(2,1)S(1)}, u32[]{:S(2)}, u32[]{:S(2)}) collective-permute-start(bf16[256,768]{1,0:T(8,128)(2,1)S(1)} %get-tuple-element.185), channel_id=1, source_target_pairs={{0,4},{4,0},{8,12},{12,8},{16,20},{20,16},{24,28},{28,24},{1,5},{5... | collective-permute-start | bytes 1179656 | tf_op jit(solution)/shard_map/ppermute | solution.py:21
  163.8 17.8 %collective-permute-start.26 = (bf16[32,1024]{1,0:T(8,128)(2,1)}, bf16[32,1024]{1,0:T(8,128)(2,1)}, u32[]{:S(2)}, u32[]{:S(2)}) collective-permute-start(bf16[32,1024]{1,0:T(8,128)(2,1)} %add_convert_fusion.5), channel_id=1, source_target_pairs={{0,16},{4,20},{8,24},{12,28},{16,0},{20,4},{24,8},{28,12},{1,17},{... | collective-permute-start | bytes 196616 | tf_op jit(solution)/shard_map/ppermute | solution.py:21
  164.8 18.1 %collective-permute-start.27 = (bf16[32,1024]{1,0:T(8,128)(2,1)}, bf16[32,1024]{1,0:T(8,128)(2,1)}, u32[]{:S(2)}, u32[]{:S(2)}) collective-permute-start(bf16[32,1024]{1,0:T(8,128)(2,1)} %add_convert_fusion.5), channel_id=1, source_target_pairs={{0,24},{4,28},{8,16},{12,20},{16,8},{20,12},{24,0},{28,4},{1,25},{... | collective-permute-start | bytes 196616 | tf_op jit(solution)/shard_map/ppermute | solution.py:21
  168.7 14.2 %collective-permute-start.21 = (bf16[64,768]{1,0:T(8,128)(2,1)}, bf16[64,768]{1,0:T(8,128)(2,1)S(1)}, u32[]{:S(2)}, u32[]{:S(2)}) collective-permute-start(bf16[64,768]{1,0:T(8,128)(2,1)} %get-tuple-element.209), channel_id=1, source_target_pairs={{0,8},{4,12},{8,0},{12,4},{16,24},{20,28},{24,16},{28,20},{1,9},{5... | collective-permute-start | bytes 294920 | tf_op jit(solution)/shard_map/ppermute | solution.py:21
  169.1 13.8 %collective-permute-start.22 = (bf16[64,768]{1,0:T(8,128)(2,1)}, bf16[64,768]{1,0:T(8,128)(2,1)S(1)}, u32[]{:S(2)}, u32[]{:S(2)}) collective-permute-start(bf16[64,768]{1,0:T(8,128)(2,1)} %get-tuple-element.208), channel_id=1, source_target_pairs={{0,16},{4,20},{8,24},{12,28},{16,0},{20,4},{24,8},{28,12},{1,17},{... | collective-permute-start | bytes 294920 | tf_op jit(solution)/shard_map/ppermute | solution.py:21
  171.6 11.3 %collective-permute-start.23 = (bf16[64,768]{1,0:T(8,128)(2,1)}, bf16[64,768]{1,0:T(8,128)(2,1)S(1)}, u32[]{:S(2)}, u32[]{:S(2)}) collective-permute-start(bf16[64,768]{1,0:T(8,128)(2,1)} %get-tuple-element.207), channel_id=1, source_target_pairs={{0,24},{4,28},{8,16},{12,20},{16,8},{20,12},{24,0},{28,4},{1,25},{... | collective-permute-start | bytes 294920 | tf_op jit(solution)/shard_map/ppermute | solution.py:21
  181.6 28.6 %collective-permute-start.20 = (bf16[1,128,1024]{2,1,0:T(8,128)(2,1)}, bf16[1,128,1024]{2,1,0:T(8,128)(2,1)S(1)}, u32[]{:S(2)}, u32[]{:S(2)}) collective-permute-start(bf16[1,128,1024]{2,1,0:T(8,128)(2,1)} %fusion.40), channel_id=1, source_target_pairs={{0,2},{1,3},{2,0},{3,1},{4,6},{5,7},{6,4},{7,5},{8,10},{9,11},{10,... | collective-permute-start | bytes 786440 | tf_op jit(solution)/shard_map/ppermute | solution.py:21
  183.6 10.3 %collective-permute-start.28 = (f32[19,1024]{1,0:T(8,128)S(1)}, f32[19,1024]{1,0:T(8,128)S(1)}, u32[]{:S(2)}, u32[]{:S(2)}) collective-permute-start(f32[19,1024]{1,0:T(8,128)S(1)} %pad_maximum_fusion.12), channel_id=1, source_target_pairs={{0,1},{1,0},{2,3},{3,2},{4,5},{5,4},{6,7},{7,6},{8,9},{9,8},{10,11... | collective-permute-start | bytes 233480 | tf_op jit(solution)/shard_map/ppermute | solution.py:21
  184.7 18.1 %collective-permute-start.33 = (bf16[64,768]{1,0:T(8,128)(2,1)S(1)}, bf16[64,768]{1,0:T(8,128)(2,1)S(1)}, u32[]{:S(2)}, u32[]{:S(2)}) collective-permute-start(bf16[64,768]{1,0:T(8,128)(2,1)S(1)} %get-tuple-element.177), channel_id=1, source_target_pairs={{0,8},{4,12},{8,0},{12,4},{16,24},{20,28},{24,16},{28,20},{1,9},{5... | collective-permute-start | bytes 294920 | tf_op jit(solution)/shard_map/ppermute | solution.py:21
  187.7 11.5 %collective-permute-start.38 = (bf16[64,768]{1,0:T(8,128)(2,1)S(1)}, bf16[64,768]{1,0:T(8,128)(2,1)S(1)}, u32[]{:S(2)}, u32[]{:S(2)}) collective-permute-start(bf16[64,768]{1,0:T(8,128)(2,1)S(1)} %get-tuple-element.206), channel_id=1, source_target_pairs={{0,16},{4,20},{8,24},{12,28},{16,0},{20,4},{24,8},{28,12},{1,17},{... | collective-permute-start | bytes 294920 | tf_op jit(solution)/shard_map/ppermute | solution.py:21
  194.9 10.4 %collective-permute-start.34 = (bf16[64,768]{1,0:T(8,128)(2,1)S(1)}, bf16[64,768]{1,0:T(8,128)(2,1)S(1)}, u32[]{:S(2)}, u32[]{:S(2)}) collective-permute-start(bf16[64,768]{1,0:T(8,128)(2,1)S(1)} %get-tuple-element.177), channel_id=1, source_target_pairs={{0,16},{4,20},{8,24},{12,28},{16,0},{20,4},{24,8},{28,12},{1,17},{... | collective-permute-start | bytes 294920 | tf_op jit(solution)/shard_map/ppermute | solution.py:21
  201.8 22.7 %collective-permute-start.44 = (bf16[4,32,1024]{2,1,0:T(8,128)(2,1)S(1)}, bf16[4,32,1024]{2,1,0:T(8,128)(2,1)S(1)}, u32[]{:S(2)}, u32[]{:S(2)}) collective-permute-start(bf16[4,32,1024]{2,1,0:T(8,128)(2,1)S(1)} %pad_maximum_fusion.11), channel_id=1, source_target_pairs={{0,4},{4,0},{8,12},{12,8},{16,20},{20,16},{24,28},{28,24},{1,5},{5... | collective-permute-start | bytes 786440 | tf_op jit(solution)/shard_map/ppermute | solution.py:21
  210.2 27.1 %collective-permute-start.36 = (bf16[4,64,768]{2,1,0:T(8,128)(2,1)S(1)}, bf16[4,64,768]{2,1,0:T(8,128)(2,1)}, u32[]{:S(2)}, u32[]{:S(2)}) collective-permute-start(bf16[4,64,768]{2,1,0:T(8,128)(2,1)S(1)} %pad_maximum_fusion.9), channel_id=1, source_target_pairs={{0,4},{4,0},{8,12},{12,8},{16,20},{20,16},{24,28},{28,24},{1,5},{5... | collective-permute-start | bytes 1179656 | tf_op jit(solution)/shard_map/ppermute | solution.py:21
  212.4 12.0 %collective-permute-start.30 = (f32[19,1024]{1,0:T(8,128)S(1)}, f32[19,1024]{1,0:T(8,128)S(1)}, u32[]{:S(2)}, u32[]{:S(2)}) collective-permute-start(f32[19,1024]{1,0:T(8,128)S(1)} %add.318), channel_id=1, source_target_pairs={{0,4},{4,0},{8,12},{12,8},{16,20},{20,16},{24,28},{28,24},{1,5},{5... | collective-permute-start | bytes 233480 | tf_op jit(solution)/shard_map/ppermute | solution.py:21
  215.3 23.2 %collective-permute-start.43 = (bf16[4,64,768]{2,1,0:T(8,128)(2,1)S(1)}, bf16[4,64,768]{2,1,0:T(8,128)(2,1)S(1)}, u32[]{:S(2)}, u32[]{:S(2)}) collective-permute-start(bf16[4,64,768]{2,1,0:T(8,128)(2,1)S(1)} %pad_maximum_fusion.10), channel_id=1, source_target_pairs={{0,4},{4,0},{8,12},{12,8},{16,20},{20,16},{24,28},{28,24},{1,5},{5... | collective-permute-start | bytes 1179656 | tf_op jit(solution)/shard_map/ppermute | solution.py:21
  (81 other events, 419.3 us)

commit v2 on v1

--- a/solution.py
+++ b/solution.py
@@ -25,19 +25,20 @@
     return lax.axis_size(axis).bit_length() - 1
 
 
-def gather_members(block, beside=None):
-    held = block[None]
-    for bit in reversed(range(bit_count("mp"))):
-        other = swap(held, "mp", 1 << bit)
-        if beside is not None and held.shape[0] == 1:
-            other, beside = lax.optimization_barrier((other, beside))
-        held = jnp.stack([held, other], axis=1).reshape((-1,) + block.shape)
-    return held if beside is None else (held, beside)
-
-
-def core_hop(blocks):
-    pairs = blocks.reshape((-1, 2) + blocks.shape[1:])
-    return pairs[:, 0], swap(pairs[:, 1].astype(bf16), "mp", 1)
+def gather_members(block, beside):
+    held = [block]
+    mirrored = [swap(block, "mp", 1)]
+    bits = bit_count("mp")
+    for bit in reversed(range(1, bits)):
+        others = [swap(item, "mp", 1 << bit) for item in held]
+        if bit == bits - 1:
+            others, beside = lax.optimization_barrier((others, beside))
+        held = [item for pair in zip(held, others) for item in pair]
+    return held, mirrored + [swap(item, "mp", 1) for item in held[1:]], beside
+
+
+def core_hop(keep, send):
+    return keep, swap(send.astype(bf16), "mp", 1)
 
 
 def scatter_rest(keep, received, beside=None):
@@ -55,53 +56,41 @@
     return lax.all_to_all(buffer, "dp", split_axis=0, concat_axis=0, tiled=True)
 
 
-def near_step(part):
-    mine = lax.axis_index("dp") & 1
-    halves = part.reshape(2, part.shape[0] // 2, part.shape[1])
-    got = swap(lax.dynamic_index_in_dim(halves, 1 - mine, 0, keepdims=False), "dp", 1)
+def halve(held, bit):
+    mine = (lax.axis_index("dp") >> bit) & 1
+    halves = held.reshape(2, held.shape[0] // 2, held.shape[1])
+    got = swap(lax.dynamic_index_in_dim(halves, 1 - mine, 0, keepdims=False), "dp", 1 << bit)
     return lax.dynamic_index_in_dim(halves, mine, 0, keepdims=False), got
 
 
-def far_sums(keep, got):
-    rest = lax.axis_size("dp") // 2
-    mine = lax.axis_index("dp") >> 1
-    held = (keep.astype(f32) + got.astype(f32)).astype(bf16)
-    blocks = held.reshape(rest, held.shape[0] // rest, held.shape[1])
-
-    def block_of(offset):
-        return lax.dynamic_index_in_dim(blocks, mine ^ offset, 0, keepdims=False)
-
-    return [block_of(0)] + [swap(block_of(offset), "dp", 2 * offset) for offset in range(1, rest)]
-
-
-def far_gather(parts):
-    total = parts[0].astype(f32)
-    for item in parts[1:]:
-        total = total + item.astype(f32)
-    own = total.astype(bf16)
-    return [own] + [swap(own, "dp", 2 * offset) for offset in range(1, len(parts))]
-
-
-def last_step(parts):
-    own_half = jnp.stack(parts)
+def joined_halves(keep, got):
+    return (keep.astype(f32) + got.astype(f32)).astype(bf16)
+
+
+def sum_rest(near):
+    held = joined_halves(*near)
+    for bit in range(1, bit_count("dp")):
+        held = joined_halves(*halve(held, bit))
+    held = held[None]
+    for bit in reversed(range(1, bit_count("dp"))):
+        held = jnp.concatenate([held, swap(held, "dp", 1 << bit)], axis=0)
+    return held
+
+
+def last_step(own_half):
     other = swap(own_half, "dp", 1)
-    rest = lax.axis_size("dp") // 2
+    both = jnp.stack([own_half, other])
+    bits = bit_count("dp")
     me = lax.axis_index("dp")
-    both = jnp.concatenate([own_half, other], axis=0)
     rows = []
     for half in range(2):
-        for block in range(rest):
-            at = (half ^ (me & 1)) * rest + (block ^ (me >> 1))
-            rows.append(lax.dynamic_index_in_dim(both, at, 0, keepdims=False))
+        for block in range(1 << (bits - 1)):
+            at = jnp.int32(0)
+            for bit in range(1, bits):
+                differs = ((block >> (bits - 1 - bit)) & 1) ^ ((me >> bit) & 1)
+                at = at + (differs << (bits - 1 - bit))
+            rows.append(both[half ^ (me & 1), at])
     return jnp.concatenate(rows, axis=0).astype(f32)
-
-
-def sum_all(part, axes):
-    held = part
-    for axis in axes:
-        for bit in range(bit_count(axis)):
-            held = held + swap(held, axis, 1 << bit)
-    return held
 
 
 def bias_kernel(block, shift_ref, table_ref, bucket_ref, bias_ref, moved_ref):
@@ -135,7 +124,7 @@
         ),
         out_shape=[
             jax.ShapeDtypeStruct((heads, seq_len, seq_len), f32),
-            jax.ShapeDtypeStruct((seq_len, seq_len), jnp.int32),
+            pltpu.HBM((seq_len, seq_len), jnp.int32),
         ],
         compiler_params=pltpu.CompilerParams(vmem_limit_bytes=8 * MIB),
         cost_estimate=pl.CostEstimate(
@@ -152,8 +141,10 @@
     def _():
         out_ref[...] = jnp.zeros_like(out_ref)
 
-    labels = lax.broadcasted_iota(jnp.int32, (rows, buckets, seq_len), 1)
-    onehot = (table_ref[...][:, None, :] == labels).astype(f32).astype(bf16).reshape(rows * buckets, seq_len)
+    labels = lax.broadcasted_iota(jnp.int32, (buckets, seq_len), 0).astype(f32).astype(bf16)
+    table = table_ref[...].astype(f32).astype(bf16)
+    one, zero = jnp.ones((), bf16), jnp.zeros((), bf16)
+    onehot = jnp.concatenate([jnp.where(table[row : row + 1, :] == labels, one, zero) for row in range(rows)], axis=0)
     total = jnp.zeros((rows * buckets, heads * rows), f32)
     for seq in range(seqs):
         grads = grad_ref[seq].reshape(heads * rows, seq_len)
@@ -177,22 +168,35 @@
         out_specs=pl.BlockSpec((buckets, heads * rows), lambda i: (0, 0)),
         out_shape=jax.ShapeDtypeStruct((buckets, heads * rows), f32),
         compiler_params=pltpu.CompilerParams(vmem_limit_bytes=16 * MIB),
-        cost_estimate=pl.CostEstimate(
-            flops=2 * seqs * seq_len * buckets * seq_len * heads * rows,
-            bytes_accessed=2 * seqs * heads * seq_len * seq_len + 4 * seq_len * seq_len,
-            transcendentals=0,
-        ),
+        cost_estimate=pl.CostEstimate(flops=0, bytes_accessed=4 * seq_len, transcendentals=0),
         name="bucket_grad",
     )(table, score_grad)
     return jnp.sum(out.reshape(buckets, heads, rows), axis=2)
 
 
-def attend_kernel(head_size, joined_ref, bias_ref, mixed_ref, probs_ref):
+def attend_kernel(
+    head_size,
+    *refs,
+):
+    *token_refs, gain_ref, query_ref, key_ref, value_ref, bias_ref, normed_ref, joined_ref, mixed_ref, probs_ref = refs
     seq_len, width = joined_ref.shape
     head_cols = width // 3
     pair_heads = bias_ref.shape[0]
     pair_cols = pair_heads * head_size
-    start = pl.program_id(1) * pair_cols
+    block = token_refs[0].shape[0]
+
+    @pl.when(pl.program_id(0) == 0)
+    def _():
+        for at, token_ref in enumerate(token_refs):
+            values = token_ref[...].astype(f32)
+            root = lax.rsqrt(jnp.mean(values * values, axis=-1, keepdims=True) + norm_eps)
+            normed_ref[at * block : (at + 1) * block, :] = (values * root * gain_ref[...]).astype(bf16)
+        for part, weight_ref in enumerate((query_ref, key_ref, value_ref)):
+            joined_ref[:, part * head_cols : (part + 1) * head_cols] = jnp.dot(
+                normed_ref[...], weight_ref[...], preferred_element_type=f32
+            ).astype(bf16)
+
+    start = pl.program_id(0) * pair_cols
     columns = [
         joined_ref[:, pl.ds(pl.multiple_of(start + part * head_cols, pair_cols), pair_cols)] for part in range(3)
     ]
@@ -207,41 +211,78 @@
             )
             scores = scores + bias_ref[head, picked, :]
             expo = jnp.exp(scores - jnp.max(scores, axis=-1, keepdims=True))
-            probs = expo / jnp.sum(expo, axis=-1, keepdims=True)
+            probs = (expo * (1.0 / jnp.sum(expo, axis=-1, keepdims=True))).astype(bf16)
             probs_ref[0, head, picked, :] = probs
-            outs.append(jnp.dot(probs.astype(bf16), columns[2][:, cols], preferred_element_type=f32))
+            outs.append(jnp.dot(probs, columns[2][:, cols], preferred_element_type=f32))
         mixed_ref[picked, :] = jnp.concatenate(outs, axis=1).astype(bf16)
 
 
-def attend(joined, bias, head_size):
+def attend(blocks, gain, w_query, w_key, w_value, bias, head_size):
     heads, seq_len, _ = bias.shape
-    tokens, width = joined.shape
-    seqs = tokens // seq_len
-    head_cols = width // 3
+    block, width = blocks[0].shape
+    head_cols = w_query.shape[1]
     pair = min(heads, LANES // head_size)
+    weight = pl.BlockSpec((width, head_cols), lambda h: (0, 0))
+    weights = [pltpu.with_memory_space_constraint(item, pltpu.HBM) for item in (w_query, w_key, w_value)]
     return pl.pallas_call(
         functools.partial(attend_kernel, head_size),
-        grid=(seqs, heads // pair),
-        in_specs=[
-            pl.BlockSpec((seq_len, width), lambda s, h: (s, 0)),
-            pl.BlockSpec((pair, seq_len, seq_len), lambda s, h: (h, 0, 0)),
+        grid=(heads // pair,),
+        in_specs=[pl.BlockSpec((block, width), lambda h: (0, 0))] * len(blocks)
+        + [
+            pl.BlockSpec((1, width), lambda h: (0, 0)),
+            weight,
+            weight,
+            weight,
+            pl.BlockSpec((pair, seq_len, seq_len), lambda h: (h, 0, 0)),
         ],
         out_specs=[
-            pl.BlockSpec((seq_len, pair * head_size), lambda s, h: (s, h)),
-            pl.BlockSpec((1, pair, seq_len, seq_len), lambda s, h: (s, h, 0, 0)),
-        ],
+            pl.BlockSpec((seq_len, width), lambda h: (0, 0)),
+            pl.BlockSpec((seq_len, 3 * head_cols), lambda h: (0, 0)),
+            pl.BlockSpec((seq_len, pair * head_size), lambda h: (0, h)),
+            pl.BlockSpec((1, pair, seq_len, seq_len), lambda h: (0, h, 0, 0)),
+        ],
+        out_shape=[
+            pltpu.HBM((seq_len, width), bf16),
+            pltpu.HBM((seq_len, 3 * head_cols), bf16),
+            jax.ShapeDtypeStruct((seq_len, head_cols), bf16),
+            pltpu.HBM((1, heads, seq_len, seq_len), bf16),
+        ],
+        compiler_params=pltpu.CompilerParams(vmem_limit_bytes=24 * MIB),
+        cost_estimate=pl.CostEstimate(
+            flops=4 * heads * seq_len * seq_len * head_size + 6 * seq_len * width * head_cols,
+            bytes_accessed=6 * heads * seq_len * seq_len,
+            transcendentals=heads * seq_len * seq_len,
+        ),
+        name="attend",
+    )(*blocks, gain, *weights, bias)
+
+
+def output_back_kernel(*refs):
+    *block_refs, mixed_ref, weight_ref, mixed_grad_ref, part_ref = refs
+    rows = jnp.concatenate([block_ref[...] for block_ref in block_refs], axis=0)
+    part_ref[...] = lax.dot_general(
+        mixed_ref[...], rows, (((0,), (0,)), ((), ())), preferred_element_type=f32
+    ).astype(bf16)
+    mixed_grad_ref[...] = lax.dot_general(
+        rows, weight_ref[...], (((1,), (1,)), ((), ())), preferred_element_type=f32
+    ).astype(bf16)
+
+
+def output_back(blocks, mixed, weight):
+    tokens, head_cols = mixed.shape
+    width = weight.shape[1]
+    return pl.pallas_call(
+        output_back_kernel,
         out_shape=[
             jax.ShapeDtypeStruct((tokens, head_cols), bf16),
-            jax.ShapeDtypeStruct((seqs, heads, seq_len, seq_len), f32),
-        ],
-        compiler_params=pltpu.CompilerParams(vmem_limit_bytes=20 * MIB),
+            jax.ShapeDtypeStruct((head_cols, width), bf16),
+        ],
+        compiler_params=pltpu.CompilerParams(vmem_limit_bytes=16 * MIB),
         cost_estimate=pl.CostEstimate(
-            flops=4 * seqs * heads * seq_len * seq_len * head_size,
-            bytes_accessed=8 * seqs * heads * seq_len * seq_len,
-            transcendentals=seqs * heads * seq_len * seq_len,
+            flops=4 * tokens * head_cols * width, bytes_accessed=4 * tokens * width, transcendentals=0
         ),
-        name="attend",
-    )(joined, bias)
+        name="output_back",
+    )(*blocks, mixed, weight)
 
 
 def attend_back_kernel(head_size, joined_ref, grad_ref, probs_ref, out_ref, score_ref):
@@ -266,7 +307,8 @@
         outs = []
         for head in range(pair_heads):
             cols = slice(head * head_size, (head + 1) * head_size)
-            probs = probs_ref[0, head, picked, :]
+            probs_low = probs_ref[0, head, picked, :]
+            probs = probs_low.astype(f32)
             prob_grad = lax.dot_general(
                 grads[picked, cols], values[:, cols], (((1,), (1,)), ((), ())), preferred_element_type=f32
             )
@@ -275,7 +317,7 @@
             score_ref[0, head, picked, :] = score_grad
             outs.append(jnp.dot(score_grad, keys[:, cols], preferred_element_type=f32))
             key_t[head] += jnp.dot(queries_t[cols, picked], score_grad, preferred_element_type=f32)
-            value_t[head] += jnp.dot(grads_t[cols, picked], probs.astype(bf16), preferred_element_type=f32)
+            value_t[head] += jnp.dot(grads_t[cols, picked], probs_low, preferred_element_type=f32)
         out_ref[picked, place(0)] = jnp.concatenate(outs, axis=1).astype(bf16)
     out_ref[:, place(1)] = jnp.concatenate(key_t, axis=0).T.astype(bf16)
     out_ref[:, place(2)] = jnp.concatenate(value_t, axis=0).T.astype(bf16)
@@ -299,7 +341,7 @@
         ],
         out_shape=[
             jax.ShapeDtypeStruct((tokens, width), bf16),
-            jax.ShapeDtypeStruct((seqs, heads, seq_len, seq_len), bf16),
+            pltpu.HBM((seqs, heads, seq_len, seq_len), bf16),
         ],
         compiler_params=pltpu.CompilerParams(vmem_limit_bytes=20 * MIB),
         cost_estimate=pl.CostEstimate(
@@ -324,86 +366,104 @@
     return 0.5 * (1.0 + bent) + 0.5 * pre * (1.0 - bent * bent) * gelu_scale * (1.0 + 0.134145 * pre * pre)
 
 
-def expert_kernel(cuts, middle_step, blocks_ref, sort_ref, unsort_ref, first_ref, second_ref, *refs):
-    members, _, piece = blocks_ref.shape
-    back_ref, rows_ref = refs[-1], refs[-2]
-    expert_rows = sort_ref.shape[1] // cuts
+def expert_kernel(cuts, middle_step, members, *refs):
+    block_refs = refs[:members]
+    order_ref, first_ref, second_ref, *middle_refs, inner_ref, rows_out, keep_ref, send_ref = refs[members:-6]
+    first_held, second_held, inner_held, rows_ref, arrived, left = refs[-6:]
+    half = members // 2
+    all_rows, piece = block_refs[0].shape
+    experts, _, picked = order_ref.shape
+    expert_rows = picked // cuts
+    loads = []
+    for expert in range(experts):
+        for at, (source, held) in enumerate(((first_ref, first_held), (second_ref, second_held))):
+            load = pltpu.make_async_copy(source.at[expert], held.at[expert], arrived.at[2 * expert + at])
+            load.start()
+            loads.append(load)
+    places = [
+        (order_ref[expert] == lax.broadcasted_iota(jnp.int32, (all_rows, picked), 0)).astype(f32)
+        for expert in range(experts)
+    ]
+    for expert in range(experts):
+        sorting = places[expert].T.astype(bf16)
+        for member in range(members):
+            moved = jnp.dot(sorting, block_refs[member][...], preferred_element_type=f32).astype(bf16)
+            for cut in range(cuts):
+                rows_ref[
+                    expert, member * expert_rows : (member + 1) * expert_rows, cut * piece : (cut + 1) * piece
+                ] = moved[cut * expert_rows : (cut + 1) * expert_rows]
+    stores = [pltpu.make_async_copy(rows_ref, rows_out, left.at[experts])]
+    stores[0].start()
+    results = []
+    for expert in range(experts):
+        loads[2 * expert].wait()
+        inner = lax.dot_general(
+            rows_ref[expert], first_held[expert], (((1,), (1,)), ((), ())), preferred_element_type=f32
+        )
+        inner = middle_step(expert, inner, *middle_refs)
+        inner_held[expert] = inner
+        stores.append(pltpu.make_async_copy(inner_held.at[expert], inner_ref.at[expert], left.at[expert]))
+        stores[-1].start()
+        loads[2 * expert + 1].wait()
+        results.append(jnp.dot(inner, second_held[expert], preferred_element_type=f32).astype(bf16))
     for member in range(members):
-        moved = jnp.dot(sort_ref[0], blocks_ref[member], preferred_element_type=f32).astype(bf16)
-        for cut in range(cuts):
-            rows_ref[0, member * expert_rows : (member + 1) * expert_rows, cut * piece : (cut + 1) * piece] = moved[
-                cut * expert_rows : (cut + 1) * expert_rows
-            ]
-    inner = lax.dot_general(rows_ref[0], first_ref[0], (((1,), (1,)), ((), ())), preferred_element_type=f32)
-    inner = middle_step(inner, *refs[:-2])
-    result = jnp.dot(inner, second_ref[0], preferred_element_type=f32).astype(bf16)
-    for member in range(members):
-        part = jnp.concatenate(
-            [
-                result[member * expert_rows : (member + 1) * expert_rows, cut * piece : (cut + 1) * piece]
-                for cut in range(cuts)
-            ],
-            axis=0,
-        )
-        placed = jnp.dot(unsort_ref[0], part, preferred_element_type=f32).astype(bf16)
-
-        @pl.when(pl.program_id(0) == 0)
-        def _():
-            back_ref[member] = placed
-
-        @pl.when(pl.program_id(0) != 0)
-        def _():
-            back_ref[member] += placed
-
-
-def forward_step(inner, pre_ref, hidden_ref):
-    pre_ref[0] = inner
-    hidden = gelu_parts(inner)[0].astype(bf16)
-    hidden_ref[0] = hidden
-    return hidden
-
-
-def backward_step(inner, pre_ref, grad_ref):
-    grad = (inner.astype(bf16).astype(f32) * gelu_slope(pre_ref[0])).astype(bf16)
-    grad_ref[0] = grad
-    return grad
-
-
-def run_experts(blocks, sorting, unsorting, first, second, cuts, pre=None):
-    members, all_rows, piece = blocks.shape
+        parts = [
+            result[member * expert_rows : (member + 1) * expert_rows, cut * piece : (cut + 1) * piece]
+            for result in results
+            for cut in range(cuts)
+        ]
+        unsorting = jnp.concatenate([place.astype(bf16) for place in places], axis=1)
+        placed = jnp.dot(unsorting, jnp.concatenate(parts, axis=0), preferred_element_type=f32).astype(bf16)
+        target, at = (keep_ref, member) if member < half else (send_ref, member - half)
+        target[at] = placed
+    for store in stores:
+        store.wait()
+
+
+def forward_step(expert, inner, pre_ref):
+    pre_ref[expert] = inner
+    return gelu_parts(inner)[0].astype(bf16)
+
+
+def backward_step(expert, inner, pre_ref):
+    return (inner.astype(bf16).astype(f32) * gelu_slope(pre_ref[expert])).astype(bf16)
+
+
+def run_experts(blocks, order, first, second, cuts, pre=None):
+    members = len(blocks)
     experts, units, width = first.shape
-    rows = members * (sorting.shape[1] // cuts)
-
-    def per_expert(*shape):
-        return pl.BlockSpec((1,) + shape, lambda j: (j, 0, 0))
-
-    whole = pl.BlockSpec((members, all_rows, piece), lambda j: (0, 0, 0))
-    inner = jax.ShapeDtypeStruct((experts, rows, units), bf16)
-    in_specs = [
-        whole,
-        per_expert(*sorting.shape[1:]),
-        per_expert(*unsorting.shape[1:]),
-        per_expert(units, width),
-        per_expert(units, width),
-    ]
-    operands = [blocks, sorting, unsorting, first, second]
-    out_specs = [per_expert(rows, units), per_expert(rows, width), whole]
-    out_shape = [inner, jax.ShapeDtypeStruct((experts, rows, width), bf16), jax.ShapeDtypeStruct(blocks.shape, bf16)]
+    picked = order.shape[1]
+    rows = members * (picked // cuts)
+    part = jax.ShapeDtypeStruct((members // 2,) + blocks[0].shape, bf16)
+    inside = pl.BlockSpec(memory_space=pltpu.VMEM)
+    outside = pl.BlockSpec(memory_space=pltpu.HBM)
+    first, second = [pltpu.with_memory_space_constraint(item, pltpu.HBM) for item in (first, second)]
+    out_specs = [outside, outside, inside, inside]
+    in_specs = [inside] * (members + 1) + [outside, outside]
+    operands = [*blocks, order[:, None, :], first, second]
+    out_shape = [pltpu.HBM((experts, rows, units), bf16), pltpu.HBM((experts, rows, width), bf16), part, part]
     if pre is None:
         step, name = forward_step, "experts"
-        out_specs.insert(0, per_expert(rows, units))
-        out_shape.insert(0, jax.ShapeDtypeStruct(inner.shape, f32))
+        out_shape.insert(0, jax.ShapeDtypeStruct((experts, rows, units), f32))
+        out_specs.insert(0, inside)
     else:
         step, name = backward_step, "experts_back"
-        in_specs.append(per_expert(rows, units))
+        in_specs.append(inside)
         operands.append(pre)
     return pl.pallas_call(
-        functools.partial(expert_kernel, cuts, step),
-        grid=(experts,),
+        functools.partial(expert_kernel, cuts, step, members),
         in_specs=in_specs,
         out_specs=out_specs,
         out_shape=out_shape,
-        compiler_params=pltpu.CompilerParams(vmem_limit_bytes=24 * MIB),
+        scratch_shapes=[
+            pltpu.VMEM((experts, units, width), bf16),
+            pltpu.VMEM((experts, units, width), bf16),
+            pltpu.VMEM((experts, rows, units), bf16),
+            pltpu.VMEM((experts, rows, width), bf16),
+            pltpu.SemaphoreType.DMA((2 * experts,)),
+            pltpu.SemaphoreType.DMA((experts + 1,)),
+        ],
+        compiler_params=pltpu.CompilerParams(vmem_limit_bytes=26 * MIB),
         cost_estimate=pl.CostEstimate(
             flops=4 * experts * rows * units * width,
             bytes_accessed=4 * experts * units * width + 12 * experts * rows * width,
@@ -451,14 +511,15 @@
     bucket_rows = jnp.pad(rel_bias.T, ((0, 0), (0, LANES - rel_bias.shape[0])))
     shift = (member % seq_members).astype(jnp.int32)[None]
     bias, moved_table = make_bias(bucket_table, bucket_rows, shift, tok_dev)
-    w_joined = jnp.concatenate([w_query, w_key, w_value], axis=1)
-    all_tokens = gather_members(tokens, (bias, moved_table, w_joined))
-    all_tokens, (bias, moved_table, w_joined) = all_tokens
-    all_tokens = all_tokens.reshape(group_tokens, width).astype(f32)
-    unit_attn = all_tokens * root_inverse(all_tokens)
-    normed_low = (unit_attn * gain_attn).astype(bf16)
-    joined = jnp.dot(normed_low, w_joined, preferred_element_type=f32).astype(bf16)
-    mixed, probs = attend(joined, bias, head_size)
+    near_tokens, far_tokens, (bias, moved_table) = gather_members(tokens, (bias, moved_table))
+    token_blocks = [item for pair in zip(near_tokens, far_tokens) for item in pair]
+    sequences = [
+        attend(token_blocks[at : at + seq_members], gain_attn[None], w_query, w_key, w_value, bias, head_size)
+        for at in range(0, member_count, seq_members)
+    ]
+    normed_low, joined, mixed, probs = [
+        parts[0] if len(parts) == 1 else jnp.concatenate(parts, axis=0) for parts in zip(*sequences)
+    ]
     mixed_pairs = mixed.reshape(member_count // 2, 2, tok_dev, head_cols)
 
     def project(rows):
@@ -514,22 +575,21 @@
         return join_rows(rows)
 
     order = np.arange(all_rows).reshape(group_count, cuts, expert_local, capacity).transpose(2, 1, 0, 3)
-    picks = np.eye(all_rows, dtype=np.float32)[order.reshape(expert_local, -1)]
-    sorting = jnp.asarray(picks, bf16)
-    unsorting = jnp.asarray(picks.transpose(0, 2, 1), bf16)
+    order = jnp.asarray(order.reshape(expert_local, -1), jnp.int32)
     w_in_t = jnp.swapaxes(w_in, 1, 2)
 
     upstream = cotangent.astype(f32)
     sent = send_rows(moe_low)
     grad_sent = send_rows((gate_prob * upstream).astype(bf16))
-    arrived, grad_sent = gather_members(sent, grad_sent)
-
-    pre, hidden, expert_in, value_blocks = run_experts(arrived, sorting, unsorting, w_in_t, w_out, cuts)
-    grad_arrived, value_blocks = gather_members(grad_sent, value_blocks)
-    value_hop = core_hop(value_blocks)
-    pre_grad, result_grad, rows_blocks = run_experts(grad_arrived, sorting, unsorting, w_out, w_in_t, cuts, pre)
+    w_joined = jnp.concatenate([w_query, w_key, w_value], axis=1)
+    near_rows, far_rows, (grad_sent, w_joined) = gather_members(sent, (grad_sent, w_joined))
+
+    pre, hidden, expert_in, value_keep, value_send = run_experts(near_rows + far_rows, order, w_in_t, w_out, cuts)
+    near_rows, far_rows, (value_keep, value_send) = gather_members(grad_sent, (value_keep, value_send))
+    value_hop = core_hop(value_keep, value_send)
+    pre_grad, result_grad, *rows_blocks = run_experts(near_rows + far_rows, order, w_out, w_in_t, cuts, pre)
     value_sum, rows_blocks = scatter_rest(*value_hop, beside=rows_blocks)
-    rows_hop = core_hop(rows_blocks)
+    rows_hop = core_hop(*rows_blocks)
     value_back = exchange_groups(value_sum.astype(bf16))
     rows_sum, value_back = scatter_rest(*rows_hop, beside=value_back)
     rows_back = exchange_groups(rows_sum.astype(bf16))
@@ -552,40 +612,39 @@
         scaled - unit_moe * jnp.mean(scaled * unit_moe, axis=-1, keepdims=True)
     )
 
-    grad_rows, grad_w_in_t = gather_members(middle_grad.astype(bf16), grad_w_in_t)
-    grad_rows = grad_rows.reshape(group_tokens, width)
+    near_grads, far_grads, grad_w_in_t = gather_members(middle_grad.astype(bf16), grad_w_in_t)
     grad_w_in = jnp.swapaxes(grad_w_in_t, 1, 2)
-    mixed_grad = jnp.einsum("td,cd->tc", grad_rows, w_output, preferred_element_type=f32).astype(bf16)
-    output_part = jnp.einsum("tc,td->cd", mixed, grad_rows, preferred_element_type=f32).astype(bf16)
-    output_near = near_step(output_part)
+    grad_blocks = [item for pair in zip(near_grads, far_grads) for item in pair]
+    mixed_grad, output_part = output_back(grad_blocks, mixed, w_output)
+    output_near = halve(output_part, 0)
     joined_grad, score_grad = attend_back(joined, mixed_grad, probs, head_size)
-    output_near, joined_grad = lax.optimization_barrier((output_near, joined_grad))
+    output_near, joined_grad, token_blocks = lax.optimization_barrier((output_near, joined_grad, token_blocks))
     locals_ = []
     for half in range(2):
         columns = normed_low[:, half * (width // 2) : (half + 1) * (width // 2)]
         locals_.append(jnp.einsum("td,tc->dc", columns, joined_grad, preferred_element_type=f32).astype(bf16))
     locals_, joined_grad, score_grad = lax.optimization_barrier((locals_, joined_grad, score_grad))
-    first_near = near_step(locals_[0])
-    second_near = near_step(locals_[1])
-    output_sums = far_sums(*output_near)
+    first_near = halve(locals_[0], 0)
+    second_near = halve(locals_[1], 0)
     attn_partial = jnp.einsum("tc,dc->td", joined_grad, w_joined, preferred_element_type=f32)
-    attn_hop = core_hop(attn_partial.reshape(member_count, tok_dev, width))
-    gain_partial = jnp.sum(attn_partial * unit_attn, axis=0, keepdims=True)
-    first_near, output_sums, attn_hop, score_grad = lax.optimization_barrier(
-        (first_near, output_sums, attn_hop, score_grad)
-    )
-    first_sums = far_sums(*first_near)
-    output_parts = far_gather(output_sums)
+    attn_pairs = attn_partial.reshape(member_count // 2, 2, tok_dev, width)
+    attn_hop = core_hop(attn_pairs[:, 0], attn_pairs[:, 1])
+    all_tokens = jnp.concatenate(token_blocks, axis=0).astype(f32)
+    gain_partial = jnp.sum(attn_partial * (all_tokens * root_inverse(all_tokens)), axis=0, keepdims=True)
     bucket_part = bucket_grad(moved_table, score_grad, rel_bias.shape[0])
-    first_sums, second_near, bucket_part, output_parts = lax.optimization_barrier(
-        (first_sums, second_near, bucket_part, output_parts)
-    )
-    second_sums = far_sums(*second_near)
-    first_parts = far_gather(first_sums)
+    first_near, attn_hop, bucket_part, gain_partial, output_near = lax.optimization_barrier(
+        (first_near, attn_hop, bucket_part, gain_partial, output_near)
+    )
+    bucket_row = lax.dynamic_update_slice(
+        jnp.zeros((1, width), f32), bucket_part.reshape(1, -1), (0, member * bucket_part.size)
+    )
+    small = jnp.concatenate([grad_gain_moe, gain_partial, bucket_row, grad_router_t], axis=0)
+    for axis in ("mp", "dp"):
+        for bit in range(bit_count(axis)):
+            small = small + swap(small, axis, 1 << bit)
     attn_grad = scatter_rest(*attn_hop)
-    grad_w_output = last_step(output_parts)
-    second_parts = far_gather(second_sums)
-    grad_joined = jnp.concatenate([last_step(first_parts), last_step(second_parts)], axis=0)
+    grad_w_output = last_step(sum_rest(output_near))
+    grad_joined = jnp.concatenate([last_step(sum_rest(first_near)), last_step(sum_rest(second_near))], axis=0)
     grad_w_query, grad_w_key, grad_w_value = [
         grad_joined[:, part * head_cols : (part + 1) * head_cols] for part in range(3)
     ]
@@ -596,10 +655,6 @@
     input_grad = (
         middle_grad + own_root * (scaled - own_unit * jnp.mean(scaled * own_unit, axis=-1, keepdims=True))
     ).astype(bf16)
-    bucket_row = lax.dynamic_update_slice(
-        jnp.zeros((1, width), f32), bucket_part.reshape(1, -1), (0, member * bucket_part.size)
-    )
-    small = sum_all(jnp.concatenate([grad_gain_moe, gain_partial, bucket_row, grad_router_t], axis=0), ("mp", "dp"))
     grad_rel_bias = lax.dynamic_slice(small[2:3], (0, member * bucket_part.size), (1, bucket_part.size))
     grad_rel_bias = grad_rel_bias.reshape(bucket_part.shape)
     return (

time: 242 us -> 231 us (0.955)
  local copies, waits for them, and re-layouts: 25.3 us -> 16.8 us
  Pallas kernels: 35.1 us -> 43.3 us
  starting transfers between devices: 67.4 us -> 59.4 us
  matrix products: 18.9 us -> 16.4 us
    unnamed x145 -> x83, local copies, waits for them, and re-layouts: 17.7 us -> 7.74 us
    ppermute x45 -> x43, waiting for transfers between devices: 44.4 us -> 52.9 us  [swap(): return lax.ppermute(block, axis, [(i, i ^ offset) for i in range(size)])]
    ppermute x45 -> x43, starting transfers between devices: 46.7 us -> 39.3 us  [swap(): return lax.ppermute(block, axis, [(i, i ^ offset) for i in range(size)])]
    pallas_call x3 -> x4, Pallas kernels: 18.5 us -> 25.2 us  [the longest x2 14.7 us: run_experts(): pl.pallas_call(functools.partial(expert_kernel, cuts, step, members), in_...]
    all_to_all x4, waiting for transfers between devices: 29.5 us -> 23.5 us  [exchange_groups(): return lax.all_to_all(buffer, 'dp', split_axis=0, concat_axis=0, tiled=True)]
    another operation x11 -> x3, other arithmetic: 5.16 us -> 0.16 us  [last_step(): both = jnp.stack([own_half, other])]
  transfers between devices with their start and end apart: 49 -> 47, of which waited for: 25 -> 28; matrix products, arithmetic and copies ran while one was open for 15% -> 13% of each run, Pallas kernels for 12% -> 14%
where the time goes in v2:
time: 231 us; the launch traced here: 230 us
  waiting for transfers between devices  76.4 us (33%)
  starting transfers between devices  59.4 us (26%)
  Pallas kernels  43.3 us (19%)
  local copies, waits for them, and re-layouts  16.8 us (7%)
  matrix products  16.4 us (7%)
  other arithmetic  16.1 us (7%)
    ppermute x43, waiting for transfers between devices, swap(): return lax.ppermute(block, axis, [(i, i ^ offset) for i in range(size)])  52.9 us
    ppermute x43, starting transfers between devices, swap(): return lax.ppermute(block, axis, [(i, i ^ offset) for i in range(size)])  39.3 us
    all_to_all x4, waiting for transfers between devices, exchange_groups(): return lax.all_to_all(buffer, 'dp', split_axis=0, concat_axis=0, tiled=True)  23.5 us
    all_to_all x4, starting transfers between devices, exchange_groups(): return lax.all_to_all(buffer, 'dp', split_axis=0, concat_axis=0, tiled=True)  20.1 us
    pallas_call x2, Pallas kernels, run_experts(): pl.pallas_call(functools.partial(expert_kernel, cuts, step, members), in_...  14.7 us
    pallas_call x1, Pallas kernels, attend(): pl.pallas_call(functools.partial(attend_kernel, head_size), grid=(heads /...  9.73 us
    unnamed x83, local copies, waits for them, and re-layouts  7.74 us
    pallas_call x1, Pallas kernels, bucket_grad(): pl.pallas_call(functools.partial(bucket_kernel, buckets), grid=(seq_len /...  7.56 us
  transfers between devices with their start and end apart: 47, of which 28 were waited for; matrix products, arithmetic and copies ran while one was open for 13% of the time, Pallas kernels for 14%

profile of v2, /device:TPU:0, one launch (start us, length us, event | category | flops | bytes accessed | tf_op | source)
XLA Modules:
  0.0 230.1 jit_solution(5740548763880441725)
XLA Ops:
  0.7 3.0 %collective-permute-start.1 = (bf16[128,1024]{1,0:T(8,128)(2,1)}, bf16[128,1024]{1,0:T(8,128)(2,1)S(1)}, u32[]{:S(2)}, u32[]{:S(2)}) collective-permute-start(bf16[128,1024]{1,0:T(8,128)(2,1)} %refs_0_.1), channel_id=1, source_target_pairs={{0,2},{1,3},{2,0},{3,1},{4,6},{5,7},{6,4},{7,5},{8,10},{9,11},{10,... | collective-permute-start | bytes 786440 | tf_op jit(solution)/shard_map/ppermute | solution.py:21
  5.6 4.0 %bias_lookup.1 = (f32[4,512,512]{2,1,0:T(8,128)S(1)}, s32[512,512]{1,0:T(8,128)}) custom-call(s32[1]{0:T(128)} %bitcast.shift_ref, s32[512,512]{1,0:T(8,128)S(1)} %copy-done.8, f32[4,128]{1,0:T(4,128)S(1)} %pad.4.bucket_ref), custom_call_target="tpu_custom_call" | custom-call | flops 1048576 | bytes 6291456 | tf_op jit(solution)/shard_map/bias_lookup/pallas_call | solution.py:111
  13.4 9.7 %attend.1 = (bf16[512,1024]{1,0:T(8,128)(2,1)}, bf16[512,768]{1,0:T(8,128)(2,1)}, bf16[512,256]{1,0:T(8,128)(2,1)S(1)}, bf16[1,4,512,512]{3,2,1,0:T(8,128)(2,1)}) custom-call(bf16[128,1024]{1,0:T(8,128)(2,1)S(1)} %copy-done.2, bf16[128,1024]{1,0:T(8,128)(2,1)S(1)} %collective-permute-done.refs_1_, bf16[128,1024]{1,0:T(8,128)(2,1)S(1)} %collective-permute-done.1.refs_2_, ...), custom_call_target="tpu_custom_call" | custom-call | flops 1073741824 | bytes 6291456 | tf_op jit(solution)/shard_map/attend/pallas_call | solution.py:227
  27.6 6.5 %collective-permute-done.4 = bf16[1,128,1024]{2,1,0:T(8,128)(2,1)S(1)} collective-permute-done((bf16[1,128,1024]{2,1,0:T(8,128)(2,1)S(1)}, bf16[1,128,1024]{2,1,0:T(8,128)(2,1)S(1)}, u32[]{:S(2)}, u32[]{:S(2)}) %collective-permute-start.4) | collective-permute-done | bytes 262176 | tf_op jit(solution)/shard_map/ppermute | solution.py:21
  36.7 6.0 %all-to-all-start = ((bf16[8,40,512]{2,1,0:T(8,128)(2,1)}), bf16[8,40,512]{2,1,0:T(8,128)(2,1)S(1)}, u32[]{:S(2)}, u32[]{:S(2)}) async-start(bf16[8,40,512]{2,1,0:T(8,128)(2,1)} %bitcast.12), calls=%async_computation | async-start | bytes 655360 | tf_op jit(solution)/shard_map/all_to_all | solution.py:56
  43.9 8.6 %all-to-all-done = bf16[8,40,512]{2,1,0:T(8,128)(2,1)S(1)} async-done(((bf16[8,40,512]{2,1,0:T(8,128)(2,1)}), bf16[8,40,512]{2,1,0:T(8,128)(2,1)S(1)}, u32[]{:S(2)}, u32[]{:S(2)}) %all-to-all-start) | async-done | bytes 327712 | tf_op jit(solution)/shard_map/all_to_all | solution.py:56
  52.5 3.6 %all-to-all-start.1 = ((bf16[8,40,512]{2,1,0:T(8,128)(2,1)}), bf16[8,40,512]{2,1,0:T(8,128)(2,1)S(1)}, u32[]{:S(2)}, u32[]{:S(2)}) async-start(bf16[8,40,512]{2,1,0:T(8,128)(2,1)} %bitcast.14), calls=%async_computation.1 | async-start | bytes 655360 | tf_op jit(solution)/shard_map/all_to_all | solution.py:56
  57.7 2.6 %pad_maximum_fusion = bf16[1024,768]{1,0:T(8,128)(2,1)} fusion(bf16[1024,256]{1,0:T(8,128)(2,1)} %refs_7_.1, bf16[1024,256]{1,0:T(8,128)(2,1)} %refs_6_.2, bf16[1024,256]{1,0:T(8,128)(2,1)} %refs_5_.3), kind=kLoop, calls=%fused_computation.5 | loop fusion | flops 4718592 | bytes 3145728 | tf_op jit(solution)/shard_map/concatenate | solution.py:584
  60.3 5.7 %all-to-all-done.1 = bf16[8,40,512]{2,1,0:T(8,128)(2,1)S(1)} async-done(((bf16[8,40,512]{2,1,0:T(8,128)(2,1)}), bf16[8,40,512]{2,1,0:T(8,128)(2,1)S(1)}, u32[]{:S(2)}, u32[]{:S(2)}) %all-to-all-start.1) | async-done | bytes 327712 | tf_op jit(solution)/shard_map/all_to_all | solution.py:56
  67.6 6.8 %experts.1 = (f32[2,320,704]{2,1,0:T(8,128)S(1)}, bf16[2,320,704]{2,1,0:T(8,128)(2,1)}, bf16[2,320,1024]{2,1,0:T(8,128)(2,1)}, bf16[2,320,512]{2,1,0:T(8,128)(2,1)S(1)}, bf16[2,320,512]{2,1,0:T(8,128)(2,1)S(1)}) custom-call(bf16[320,512]{1,0:T(8,128)(2,1)S(1)} %bitcast.243, bf16[320,512]{1,0:T(8,128)(2,1)S(1)} %collective-permute-done.5.refs_1_, ...), custom_call_target="tpu_custom_call" | custom-call | flops 1845493760 | bytes 13631488 | tf_op jit(solution)/shard_map/experts/pallas_call | solution.py:453
  80.0 8.0 %experts_back.1 = (bf16[2,320,704]{2,1,0:T(8,128)(2,1)}, bf16[2,320,1024]{2,1,0:T(8,128)(2,1)}, bf16[2,320,512]{2,1,0:T(8,128)(2,1)S(1)}, bf16[2,320,512]{2,1,0:T(8,128)(2,1)}) custom-call(bf16[320,512]{1,0:T(8,128)(2,1)S(1)} %bitcast.240, bf16[320,512]{1,0:T(8,128)(2,1)S(1)} %collective-permute-done.6.refs_1_, ...), custom_call_target="tpu_custom_call" | custom-call | flops 1845493760 | bytes 13631488 | tf_op jit(solution)/shard_map/experts_back/pallas_call | solution.py:453
  89.1 4.6 %all-to-all-start.2 = ((bf16[8,40,512]{2,1,0:T(8,128)(2,1)}), bf16[8,40,512]{2,1,0:T(8,128)(2,1)}, u32[]{:S(2)}, u32[]{:S(2)}) async-start(bf16[8,40,512]{2,1,0:T(8,128)(2,1)} %bitcast.22), calls=%async_computation.2 | async-start | bytes 655360 | tf_op jit(solution)/shard_map/all_to_all | solution.py:56
  98.5 4.3 %fusion.116 = f32[2,704,1024]{2,1,0:T(8,128)} fusion(bf16[2,320,704]{2,1,0:T(8,128)(2,1)S(1)} %copy-done.33, bf16[2,320,1024]{2,1,0:T(8,128)(2,1)S(1)} %copy-done.30), kind=kOutput, calls=%fused_computation.274 | convolution fusion | flops 922746880 | bytes 7979008 | tf_op jit(solution)/shard_map/jrf,jrd->jfd/dot_general | solution.py:596
  109.0 5.8 %all-to-all-start.3 = ((bf16[8,40,512]{2,1,0:T(8,128)(2,1)}), bf16[8,40,512]{2,1,0:T(8,128)(2,1)S(1)}, u32[]{:S(2)}, u32[]{:S(2)}) async-start(bf16[8,40,512]{2,1,0:T(8,128)(2,1)} %bitcast.283), calls=%async_computation.3 | async-start | bytes 655360 | tf_op jit(solution)/shard_map/all_to_all | solution.py:56
  117.1 7.3 %all-to-all-done.3 = bf16[8,40,512]{2,1,0:T(8,128)(2,1)S(1)} async-done(((bf16[8,40,512]{2,1,0:T(8,128)(2,1)}), bf16[8,40,512]{2,1,0:T(8,128)(2,1)S(1)}, u32[]{:S(2)}, u32[]{:S(2)}) %all-to-all-start.3) | async-done | bytes 327712 | tf_op jit(solution)/shard_map/all_to_all | solution.py:56
  127.3 4.3 %fusion.118 = f32[2,704,1024]{2,1,0:T(8,128)} fusion(bf16[2,320,704]{2,1,0:T(8,128)(2,1)S(1)} %copy-done.32, bf16[2,320,1024]{2,1,0:T(8,128)(2,1)S(1)} %copy-done.29), kind=kOutput, calls=%fused_computation.276 | convolution fusion | flops 922746880 | bytes 7979008 | tf_op jit(solution)/shard_map/jrf,jrd->jfd/dot_general | solution.py:598
  137.0 6.5 %attend_back.1 = (bf16[512,768]{1,0:T(8,128)(2,1)S(1)}, bf16[1,4,512,512]{3,2,1,0:T(8,128)(2,1)}) custom-call(bf16[512,768]{1,0:T(8,128)(2,1)S(1)} %copy-done.9, bf16[512,256]{1,0:T(8,128)(2,1)S(1)} %get-tuple-element.97.grad_ref, bf16[1,4,512,512]{3,2,1,0:T(8,128)(2,1)S(1)} %copy-done.5), custom_call_target="tpu_custom_call" | custom-call | flops 536870912 | bytes 6291456 | tf_op jit(solution)/shard_map/attend_back/pallas_call | solution.py:330
  152.4 7.6 %bucket_grad.1 = f32[32,128]{1,0:T(8,128)S(1)} custom-call(s32[512,512]{1,0:T(8,128)S(1)} %copy-done.7, bf16[1,4,512,512]{3,2,1,0:T(8,128)(2,1)S(1)} %copy-done.6), custom_call_target="tpu_custom_call" | custom-call | bytes 2048 | tf_op jit(solution)/shard_map/bucket_grad/pallas_call | solution.py:161
  163.2 3.5 %collective-permute-done.19 = bf16[256,768]{1,0:T(8,128)(2,1)S(1)} collective-permute-done((bf16[256,768]{1,0:T(8,128)(2,1)}, bf16[256,768]{1,0:T(8,128)(2,1)S(1)}, u32[]{:S(2)}, u32[]{:S(2)}) %collective-permute-start.19) | collective-permute-done | bytes 393248 | tf_op jit(solution)/shard_map/ppermute | solution.py:21
  176.9 2.6 %collective-permute-done.23 = f32[19,1024]{1,0:T(8,128)S(1)} collective-permute-done((f32[19,1024]{1,0:T(8,128)S(1)}, f32[19,1024]{1,0:T(8,128)S(1)}, u32[]{:S(2)}, u32[]{:S(2)}) %collective-permute-start.23) | collective-permute-done | bytes 77856 | tf_op jit(solution)/shard_map/ppermute | solution.py:21
  189.2 3.9 %collective-permute-done.35 = bf16[1,64,768]{2,1,0:T(8,128)(2,1)S(1)} collective-permute-done((bf16[1,64,768]{2,1,0:T(8,128)(2,1)S(1)}, bf16[1,64,768]{2,1,0:T(8,128)(2,1)S(1)}, u32[]{:S(2)}, u32[]{:S(2)}) %collective-permute-start.35) | collective-permute-done | bytes 98336 | tf_op jit(solution)/shard_map/ppermute | solution.py:21
  199.8 5.0 %collective-permute-done.26 = f32[19,1024]{1,0:T(8,128)S(1)} collective-permute-done((f32[19,1024]{1,0:T(8,128)S(1)}, f32[19,1024]{1,0:T(8,128)S(1)}, u32[]{:S(2)}, u32[]{:S(2)}) %collective-permute-start.26) | collective-permute-done | bytes 77856 | tf_op jit(solution)/shard_map/ppermute | solution.py:21
  212.8 2.6 %collective-permute-done.42 = bf16[4,32,1024]{2,1,0:T(8,128)(2,1)S(1)} collective-permute-done((bf16[4,32,1024]{2,1,0:T(8,128)(2,1)S(1)}, bf16[4,32,1024]{2,1,0:T(8,128)(2,1)S(1)}, u32[]{:S(2)}, u32[]{:S(2)}) %collective-permute-start.42) | collective-permute-done | bytes 262176 | tf_op jit(solution)/shard_map/ppermute | solution.py:21
  216.8 10.4 %collective-permute-done.31 = bf16[4,64,768]{2,1,0:T(8,128)(2,1)S(1)} collective-permute-done((bf16[4,64,768]{2,1,0:T(8,128)(2,1)S(1)}, bf16[4,64,768]{2,1,0:T(8,128)(2,1)S(1)}, u32[]{:S(2)}, u32[]{:S(2)}) %collective-permute-start.31) | collective-permute-done | bytes 393248 | tf_op jit(solution)/shard_map/ppermute | solution.py:21
  (277 shorter events, 95.4 us)
Async XLA Ops:
  0.7 9.6 %collective-permute-start.1 = (bf16[128,1024]{1,0:T(8,128)(2,1)}, bf16[128,1024]{1,0:T(8,128)(2,1)S(1)}, u32[]{:S(2)}, u32[]{:S(2)}) collective-permute-start(bf16[128,1024]{1,0:T(8,128)(2,1)} %refs_0_.1), channel_id=1, source_target_pairs={{0,2},{1,3},{2,0},{3,1},{4,6},{5,7},{6,4},{7,5},{8,10},{9,11},{10,... | collective-permute-start | bytes 786440 | tf_op jit(solution)/shard_map/ppermute | solution.py:21
  36.7 15.8 %all-to-all-start = ((bf16[8,40,512]{2,1,0:T(8,128)(2,1)}), bf16[8,40,512]{2,1,0:T(8,128)(2,1)S(1)}, u32[]{:S(2)}, u32[]{:S(2)}) async-start(bf16[8,40,512]{2,1,0:T(8,128)(2,1)} %bitcast.12), calls=%async_computation | async-start | bytes 655360 | tf_op jit(solution)/shard_map/all_to_all | solution.py:56
  52.5 13.5 %all-to-all-start.1 = ((bf16[8,40,512]{2,1,0:T(8,128)(2,1)}), bf16[8,40,512]{2,1,0:T(8,128)(2,1)S(1)}, u32[]{:S(2)}, u32[]{:S(2)}) async-start(bf16[8,40,512]{2,1,0:T(8,128)(2,1)} %bitcast.14), calls=%async_computation.1 | async-start | bytes 655360 | tf_op jit(solution)/shard_map/all_to_all | solution.py:56
  56.1 9.8 %collective-permute-start.5 = (bf16[320,512]{1,0:T(8,128)(2,1)S(1)}, bf16[320,512]{1,0:T(8,128)(2,1)S(1)}, u32[]{:S(2)}, u32[]{:S(2)}) collective-permute-start(bf16[320,512]{1,0:T(8,128)(2,1)S(1)} %bitcast.241), channel_id=1, source_target_pairs={{0,2},{1,3},{2,0},{3,1},{4,6},{5,7},{6,4},{7,5},{8,10},{9,11},{10,... | collective-permute-start | bytes 983048 | tf_op jit(solution)/shard_map/ppermute | solution.py:21
  66.0 10.1 %collective-permute-start.6 = (bf16[320,512]{1,0:T(8,128)(2,1)S(1)}, bf16[320,512]{1,0:T(8,128)(2,1)S(1)}, u32[]{:S(2)}, u32[]{:S(2)}) collective-permute-start(bf16[320,512]{1,0:T(8,128)(2,1)S(1)} %bitcast.238), channel_id=1, source_target_pairs={{0,2},{1,3},{2,0},{3,1},{4,6},{5,7},{6,4},{7,5},{8,10},{9,11},{10,... | collective-permute-start | bytes 983048 | tf_op jit(solution)/shard_map/ppermute | solution.py:21
  78.4 9.8 %collective-permute-start.10 = (bf16[1,320,512]{2,1,0:T(8,128)(2,1)S(1)}, bf16[1,320,512]{2,1,0:T(8,128)(2,1)S(1)}, u32[]{:S(2)}, u32[]{:S(2)}) collective-permute-start(bf16[1,320,512]{2,1,0:T(8,128)(2,1)S(1)} %fusion.33), channel_id=1, source_target_pairs={{0,2},{1,3},{2,0},{3,1},{4,6},{5,7},{6,4},{7,5},{8,10},{9,11},{10,... | collective-permute-start | bytes 983048 | tf_op jit(solution)/shard_map/ppermute | solution.py:21
  89.1 15.7 %all-to-all-start.2 = ((bf16[8,40,512]{2,1,0:T(8,128)(2,1)}), bf16[8,40,512]{2,1,0:T(8,128)(2,1)}, u32[]{:S(2)}, u32[]{:S(2)}) async-start(bf16[8,40,512]{2,1,0:T(8,128)(2,1)} %bitcast.22), calls=%async_computation.2 | async-start | bytes 655360 | tf_op jit(solution)/shard_map/all_to_all | solution.py:56
  97.0 10.2 %collective-permute-start.14 = (bf16[1,320,512]{2,1,0:T(8,128)(2,1)}, bf16[1,320,512]{2,1,0:T(8,128)(2,1)}, u32[]{:S(2)}, u32[]{:S(2)}) collective-permute-start(bf16[1,320,512]{2,1,0:T(8,128)(2,1)} %fusion.34), channel_id=1, source_target_pairs={{0,2},{1,3},{2,0},{3,1},{4,6},{5,7},{6,4},{7,5},{8,10},{9,11},{10,... | collective-permute-start | bytes 983048 | tf_op jit(solution)/shard_map/ppermute | solution.py:21
  109.0 15.4 %all-to-all-start.3 = ((bf16[8,40,512]{2,1,0:T(8,128)(2,1)}), bf16[8,40,512]{2,1,0:T(8,128)(2,1)S(1)}, u32[]{:S(2)}, u32[]{:S(2)}) async-start(bf16[8,40,512]{2,1,0:T(8,128)(2,1)} %bitcast.283), calls=%async_computation.3 | async-start | bytes 655360 | tf_op jit(solution)/shard_map/all_to_all | solution.py:56
  147.3 12.9 %collective-permute-start.32 = (bf16[256,768]{1,0:T(8,128)(2,1)}, bf16[256,768]{1,0:T(8,128)(2,1)}, u32[]{:S(2)}, u32[]{:S(2)}) collective-permute-start(bf16[256,768]{1,0:T(8,128)(2,1)} %dynamic-slice_bitcast_fusion), channel_id=1, source_target_pairs={{0,4},{4,0},{8,12},{12,8},{16,20},{20,16},{24,28},{28,24},{1,5},{5... | collective-permute-start | bytes 1179656 | tf_op jit(solution)/shard_map/ppermute | solution.py:21
  148.8 17.9 %collective-permute-start.19 = (bf16[256,768]{1,0:T(8,128)(2,1)}, bf16[256,768]{1,0:T(8,128)(2,1)S(1)}, u32[]{:S(2)}, u32[]{:S(2)}) collective-permute-start(bf16[256,768]{1,0:T(8,128)(2,1)} %get-tuple-element.155), channel_id=1, source_target_pairs={{0,4},{4,0},{8,12},{12,8},{16,20},{20,16},{24,28},{28,24},{1,5},{5... | collective-permute-start | bytes 1179656 | tf_op jit(solution)/shard_map/ppermute | solution.py:21
  151.2 15.5 %collective-permute-start.20 = (bf16[2,128,1024]{2,1,0:T(8,128)(2,1)}, bf16[2,128,1024]{2,1,0:T(8,128)(2,1)}, u32[]{:S(2)}, u32[]{:S(2)}) collective-permute-start(bf16[2,128,1024]{2,1,0:T(8,128)(2,1)} %fusion.18), channel_id=1, source_target_pairs={{0,1},{1,0},{2,3},{3,2},{4,5},{5,4},{6,7},{7,6},{8,9},{9,8},{10,11... | collective-permute-start | bytes 1572872 | tf_op jit(solution)/shard_map/ppermute | solution.py:21
  162.1 10.0 %collective-permute-start.33 = (bf16[128,768]{1,0:T(8,128)(2,1)}, bf16[128,768]{1,0:T(8,128)(2,1)}, u32[]{:S(2)}, u32[]{:S(2)}) collective-permute-start(bf16[128,768]{1,0:T(8,128)(2,1)} %dynamic-slice_bitcast_fusion.5), channel_id=1, source_target_pairs={{0,8},{4,12},{8,0},{12,4},{16,24},{20,28},{24,16},{28,20},{1,9},{5... | collective-permute-start | bytes 589832 | tf_op jit(solution)/shard_map/ppermute | solution.py:21
  169.0 26.2 %collective-permute-start.21 = (bf16[1,128,1024]{2,1,0:T(8,128)(2,1)S(1)}, bf16[1,128,1024]{2,1,0:T(8,128)(2,1)S(1)}, u32[]{:S(2)}, u32[]{:S(2)}) collective-permute-start(bf16[1,128,1024]{2,1,0:T(8,128)(2,1)S(1)} %fusion.36), channel_id=1, source_target_pairs={{0,2},{1,3},{2,0},{3,1},{4,6},{5,7},{6,4},{7,5},{8,10},{9,11},{10,... | collective-permute-start | bytes 786440 | tf_op jit(solution)/shard_map/ppermute | solution.py:21
  170.6 15.4 %collective-permute-start.27 = (bf16[128,768]{1,0:T(8,128)(2,1)S(1)}, bf16[128,768]{1,0:T(8,128)(2,1)S(1)}, u32[]{:S(2)}, u32[]{:S(2)}) collective-permute-start(bf16[128,768]{1,0:T(8,128)(2,1)S(1)} %dynamic-slice_bitcast_fusion.6), channel_id=1, source_target_pairs={{0,8},{4,12},{8,0},{12,4},{16,24},{20,28},{24,16},{28,20},{1,9},{5... | collective-permute-start | bytes 589832 | tf_op jit(solution)/shard_map/ppermute | solution.py:21
  173.1 9.8 %collective-permute-start.34 = (bf16[64,768]{1,0:T(8,128)(2,1)S(1)}, bf16[64,768]{1,0:T(8,128)(2,1)S(1)}, u32[]{:S(2)}, u32[]{:S(2)}) collective-permute-start(bf16[64,768]{1,0:T(8,128)(2,1)S(1)} %dynamic-slice_bitcast_fusion.8), channel_id=1, source_target_pairs={{0,16},{4,20},{8,24},{12,28},{16,0},{20,4},{24,8},{28,12},{1,17},{... | collective-permute-start | bytes 294920 | tf_op jit(solution)/shard_map/ppermute | solution.py:21
  182.9 10.1 %collective-permute-start.35 = (bf16[1,64,768]{2,1,0:T(8,128)(2,1)S(1)}, bf16[1,64,768]{2,1,0:T(8,128)(2,1)S(1)}, u32[]{:S(2)}, u32[]{:S(2)}) collective-permute-start(bf16[1,64,768]{2,1,0:T(8,128)(2,1)S(1)} %fusion.64), channel_id=1, source_target_pairs={{0,16},{4,20},{8,24},{12,28},{16,0},{20,4},{24,8},{28,12},{1,17},{... | collective-permute-start | bytes 294920 | tf_op jit(solution)/shard_map/ppermute | solution.py:21
  183.8 10.1 %collective-permute-start.40 = (bf16[1,32,1024]{2,1,0:T(8,128)(2,1)S(1)}, bf16[1,32,1024]{2,1,0:T(8,128)(2,1)S(1)}, u32[]{:S(2)}, u32[]{:S(2)}) collective-permute-start(bf16[1,32,1024]{2,1,0:T(8,128)(2,1)S(1)} %fusion.73), channel_id=1, source_target_pairs={{0,16},{4,20},{8,24},{12,28},{16,0},{20,4},{24,8},{28,12},{1,17},{... | collective-permute-start | bytes 196616 | tf_op jit(solution)/shard_map/ppermute | solution.py:21
  186.1 12.1 %collective-permute-start.28 = (bf16[64,768]{1,0:T(8,128)(2,1)S(1)}, bf16[64,768]{1,0:T(8,128)(2,1)S(1)}, u32[]{:S(2)}, u32[]{:S(2)}) collective-permute-start(bf16[64,768]{1,0:T(8,128)(2,1)S(1)} %dynamic-slice_bitcast_fusion.9), channel_id=1, source_target_pairs={{0,16},{4,20},{8,24},{12,28},{16,0},{20,4},{24,8},{28,12},{1,17},{... | collective-permute-start | bytes 294920 | tf_op jit(solution)/shard_map/ppermute | solution.py:21
  187.0 9.7 %collective-permute-start.25 = (f32[19,1024]{1,0:T(8,128)S(1)}, f32[19,1024]{1,0:T(8,128)S(1)}, u32[]{:S(2)}, u32[]{:S(2)}) collective-permute-start(f32[19,1024]{1,0:T(8,128)S(1)} %add.314), channel_id=1, source_target_pairs={{0,8},{4,12},{8,0},{12,4},{16,24},{20,28},{24,16},{28,20},{1,9},{5... | collective-permute-start | bytes 233480 | tf_op jit(solution)/shard_map/ppermute | solution.py:21
  193.0 15.5 %collective-permute-start.36 = (bf16[2,64,768]{2,1,0:T(8,128)(2,1)S(1)}, bf16[2,64,768]{2,1,0:T(8,128)(2,1)S(1)}, u32[]{:S(2)}, u32[]{:S(2)}) collective-permute-start(bf16[2,64,768]{2,1,0:T(8,128)(2,1)S(1)} %pad_maximum_fusion.7), channel_id=1, source_target_pairs={{0,8},{4,12},{8,0},{12,4},{16,24},{20,28},{24,16},{28,20},{1,9},{5... | collective-permute-start | bytes 589832 | tf_op jit(solution)/shard_map/ppermute | solution.py:21
  193.9 12.1 %collective-permute-start.41 = (bf16[2,32,1024]{2,1,0:T(8,128)(2,1)S(1)}, bf16[2,32,1024]{2,1,0:T(8,128)(2,1)S(1)}, u32[]{:S(2)}, u32[]{:S(2)}) collective-permute-start(bf16[2,32,1024]{2,1,0:T(8,128)(2,1)S(1)} %pad_maximum_fusion.8), channel_id=1, source_target_pairs={{0,8},{4,12},{8,0},{12,4},{16,24},{20,28},{24,16},{28,20},{1,9},{5... | collective-permute-start | bytes 393224 | tf_op jit(solution)/shard_map/ppermute | solution.py:21
  208.6 19.2 %collective-permute-start.37 = (bf16[4,64,768]{2,1,0:T(8,128)(2,1)S(1)}, bf16[4,64,768]{2,1,0:T(8,128)(2,1)S(1)}, u32[]{:S(2)}, u32[]{:S(2)}) collective-permute-start(bf16[4,64,768]{2,1,0:T(8,128)(2,1)S(1)} %get-tuple-element.166), channel_id=1, source_target_pairs={{0,4},{4,0},{8,12},{12,8},{16,20},{20,16},{24,28},{28,24},{1,5},{5... | collective-permute-start | bytes 1179656 | tf_op jit(solution)/shard_map/ppermute | solution.py:21
  211.7 15.6 %collective-permute-start.31 = (bf16[4,64,768]{2,1,0:T(8,128)(2,1)S(1)}, bf16[4,64,768]{2,1,0:T(8,128)(2,1)S(1)}, u32[]{:S(2)}, u32[]{:S(2)}) collective-permute-start(bf16[4,64,768]{2,1,0:T(8,128)(2,1)S(1)} %get-tuple-element.168), channel_id=1, source_target_pairs={{0,4},{4,0},{8,12},{12,8},{16,20},{20,16},{24,28},{28,24},{1,5},{5... | collective-permute-start | bytes 1179656 | tf_op jit(solution)/shard_map/ppermute | solution.py:21
  (64 other events, 411.7 us)

commit v3 on v2

--- a/solution.py
+++ b/solution.py
@@ -14,6 +14,7 @@
 f32 = jnp.float32
 LANES = 128
 MIB = 1 << 20
+small_cost = pl.CostEstimate(flops=0, bytes_accessed=2048, transcendentals=0)
 
 
 def swap(block, axis, offset):
@@ -75,6 +76,30 @@
     for bit in reversed(range(1, bit_count("dp"))):
         held = jnp.concatenate([held, swap(held, "dp", 1 << bit)], axis=0)
     return held
+
+
+def sum_rest_direct(near):
+    rest = lax.axis_size("dp") // 2
+    bits = bit_count("dp")
+    mine = lax.axis_index("dp") >> 1
+    held = joined_halves(*near)
+    blocks = held.reshape(rest, held.shape[0] // rest, held.shape[1])
+    reverse = [sum(((q >> bit) & 1) << (bits - 2 - bit) for bit in range(bits - 1)) for q in range(rest)]
+    place = jnp.int32(0)
+    for bit in range(bits - 1):
+        place = place | (((mine >> bit) & 1) << (bits - 2 - bit))
+    total = lax.dynamic_index_in_dim(blocks, place, 0, keepdims=False).astype(f32)
+    got = [
+        swap(lax.dynamic_index_in_dim(blocks, place ^ reverse[offset], 0, keepdims=False), "dp", 2 * offset)
+        for offset in range(1, rest)
+    ]
+    for item in got:
+        total = total + item.astype(f32)
+    own = total.astype(bf16)
+    gathered = {0: own}
+    for offset in range(1, rest):
+        gathered[reverse[offset]] = swap(own, "dp", 2 * offset)
+    return jnp.stack([gathered[at] for at in range(rest)])
 
 
 def last_step(own_half):
@@ -127,9 +152,7 @@
             pltpu.HBM((seq_len, seq_len), jnp.int32),
         ],
         compiler_params=pltpu.CompilerParams(vmem_limit_bytes=8 * MIB),
-        cost_estimate=pl.CostEstimate(
-            flops=seq_len * seq_len * heads, bytes_accessed=4 * seq_len * seq_len * (heads + 2), transcendentals=0
-        ),
+        cost_estimate=small_cost,
         name="bias_lookup",
     )(shift, table, bucket_rows)
 
@@ -168,7 +191,7 @@
         out_specs=pl.BlockSpec((buckets, heads * rows), lambda i: (0, 0)),
         out_shape=jax.ShapeDtypeStruct((buckets, heads * rows), f32),
         compiler_params=pltpu.CompilerParams(vmem_limit_bytes=16 * MIB),
-        cost_estimate=pl.CostEstimate(flops=0, bytes_accessed=4 * seq_len, transcendentals=0),
+        cost_estimate=small_cost,
         name="bucket_grad",
     )(table, score_grad)
     return jnp.sum(out.reshape(buckets, heads, rows), axis=2)
@@ -200,7 +223,7 @@
     columns = [
         joined_ref[:, pl.ds(pl.multiple_of(start + part * head_cols, pair_cols), pair_cols)] for part in range(3)
     ]
-    rows = min(128, seq_len)
+    rows = min(512, seq_len)
     for chunk in range(seq_len // rows):
         picked = slice(chunk * rows, (chunk + 1) * rows)
         outs = []
@@ -248,11 +271,7 @@
             pltpu.HBM((1, heads, seq_len, seq_len), bf16),
         ],
         compiler_params=pltpu.CompilerParams(vmem_limit_bytes=24 * MIB),
-        cost_estimate=pl.CostEstimate(
-            flops=4 * heads * seq_len * seq_len * head_size + 6 * seq_len * width * head_cols,
-            bytes_accessed=6 * heads * seq_len * seq_len,
-            transcendentals=heads * seq_len * seq_len,
-        ),
+        cost_estimate=small_cost,
         name="attend",
     )(*blocks, gain, *weights, bias)
 
@@ -278,9 +297,7 @@
             jax.ShapeDtypeStruct((head_cols, width), bf16),
         ],
         compiler_params=pltpu.CompilerParams(vmem_limit_bytes=16 * MIB),
-        cost_estimate=pl.CostEstimate(
-            flops=4 * tokens * head_cols * width, bytes_accessed=4 * tokens * width, transcendentals=0
-        ),
+        cost_estimate=small_cost,
         name="output_back",
     )(*blocks, mixed, weight)
 
@@ -298,7 +315,7 @@
     queries, keys, values = [joined_ref[:, place(part)] for part in range(3)]
     grads = grad_ref[...]
     queries_t, grads_t = queries.T, grads.T
-    rows = min(128, seq_len)
+    rows = min(512, seq_len)
     query_parts = []
     key_t = [jnp.zeros((head_size, seq_len), f32) for _ in range(pair_heads)]
     value_t = [jnp.zeros((head_size, seq_len), f32) for _ in range(pair_heads)]
@@ -344,11 +361,7 @@
             pltpu.HBM((seqs, heads, seq_len, seq_len), bf16),
         ],
         compiler_params=pltpu.CompilerParams(vmem_limit_bytes=20 * MIB),
-        cost_estimate=pl.CostEstimate(
-            flops=8 * seqs * heads * seq_len * seq_len * head_size,
-            bytes_accessed=6 * seqs * heads * seq_len * seq_len,
-            transcendentals=0,
-        ),
+        cost_estimate=small_cost,
         name="attend_back",
     )(joined, mixed_grad, probs)
 
@@ -384,14 +397,15 @@
         (order_ref[expert] == lax.broadcasted_iota(jnp.int32, (all_rows, picked), 0)).astype(f32)
         for expert in range(experts)
     ]
-    for expert in range(experts):
-        sorting = places[expert].T.astype(bf16)
-        for member in range(members):
-            moved = jnp.dot(sorting, block_refs[member][...], preferred_element_type=f32).astype(bf16)
+    sorting = jnp.concatenate([place.T for place in places], axis=0).astype(bf16)
+    for member in range(members):
+        moved = jnp.dot(sorting, block_refs[member][...], preferred_element_type=f32).astype(bf16)
+        for expert in range(experts):
             for cut in range(cuts):
+                source = expert * picked + cut * expert_rows
                 rows_ref[
                     expert, member * expert_rows : (member + 1) * expert_rows, cut * piece : (cut + 1) * piece
-                ] = moved[cut * expert_rows : (cut + 1) * expert_rows]
+                ] = moved[source : source + expert_rows]
     stores = [pltpu.make_async_copy(rows_ref, rows_out, left.at[experts])]
     stores[0].start()
     results = []
@@ -406,13 +420,13 @@
         stores[-1].start()
         loads[2 * expert + 1].wait()
         results.append(jnp.dot(inner, second_held[expert], preferred_element_type=f32).astype(bf16))
+    unsorting = jnp.concatenate([place.astype(bf16) for place in places], axis=1)
     for member in range(members):
         parts = [
             result[member * expert_rows : (member + 1) * expert_rows, cut * piece : (cut + 1) * piece]
             for result in results
             for cut in range(cuts)
         ]
-        unsorting = jnp.concatenate([place.astype(bf16) for place in places], axis=1)
         placed = jnp.dot(unsorting, jnp.concatenate(parts, axis=0), preferred_element_type=f32).astype(bf16)
         target, at = (keep_ref, member) if member < half else (send_ref, member - half)
         target[at] = placed
@@ -464,11 +478,7 @@
             pltpu.SemaphoreType.DMA((experts + 1,)),
         ],
         compiler_params=pltpu.CompilerParams(vmem_limit_bytes=26 * MIB),
-        cost_estimate=pl.CostEstimate(
-            flops=4 * experts * rows * units * width,
-            bytes_accessed=4 * experts * units * width + 12 * experts * rows * width,
-            transcendentals=experts * rows * units,
-        ),
+        cost_estimate=small_cost,
         name=name,
     )(*operands)
 
@@ -644,7 +654,7 @@
             small = small + swap(small, axis, 1 << bit)
     attn_grad = scatter_rest(*attn_hop)
     grad_w_output = last_step(sum_rest(output_near))
-    grad_joined = jnp.concatenate([last_step(sum_rest(first_near)), last_step(sum_rest(second_near))], axis=0)
+    grad_joined = jnp.concatenate([last_step(sum_rest_direct(first_near)), last_step(sum_rest_direct(second_near))], axis=0)
     grad_w_query, grad_w_key, grad_w_value = [
         grad_joined[:, part * head_cols : (part + 1) * head_cols] for part in range(3)
     ]

time: 231 us -> 227 us (0.983)
  starting transfers between devices: 59.4 us -> 70.6 us
  waiting for transfers between devices: 76.4 us -> 68.2 us
  Pallas kernels: 43.3 us -> 38.3 us
  local copies, waits for them, and re-layouts: 16.8 us -> 14.1 us
    ppermute x43 -> x47, starting transfers between devices: 39.3 us -> 50.5 us  [swap(): return lax.ppermute(block, axis, [(i, i ^ offset) for i in range(size)])]
    ppermute x43 -> x47, waiting for transfers between devices: 52.9 us -> 44.7 us  [swap(): return lax.ppermute(block, axis, [(i, i ^ offset) for i in range(size)])]
    pallas_call x1, Pallas kernels: 6.47 us -> 3.94 us  [attend_back(): pl.pallas_call(functools.partial(attend_back_kernel, head_size), grid=(se...]
    pallas_call x1, Pallas kernels: 9.73 us -> 7.34 us  [attend(): pl.pallas_call(functools.partial(attend_kernel, head_size), grid=(heads /...]
  transfers between devices with their start and end apart: 47 -> 51, of which waited for: 28 -> 27; matrix products, arithmetic and copies ran while one was open for 13% -> 14% of each run, Pallas kernels for 14% -> 13%
where the time goes in v3:
time: 227 us; the launch traced here: 226 us
  starting transfers between devices  70.6 us (31%)
  waiting for transfers between devices  68.2 us (30%)
  Pallas kernels  38.3 us (17%)
  other arithmetic  16.7 us (7%)
  matrix products  16.4 us (7%)
  local copies, waits for them, and re-layouts  14.1 us (6%)
    ppermute x47, starting transfers between devices, swap(): return lax.ppermute(block, axis, [(i, i ^ offset) for i in range(size)])  50.5 us
    ppermute x47, waiting for transfers between devices, swap(): return lax.ppermute(block, axis, [(i, i ^ offset) for i in range(size)])  44.7 us
    all_to_all x4, waiting for transfers between devices, exchange_groups(): return lax.all_to_all(buffer, 'dp', split_axis=0, concat_axis=0, tiled=True)  23.4 us
    all_to_all x4, starting transfers between devices, exchange_groups(): return lax.all_to_all(buffer, 'dp', split_axis=0, concat_axis=0, tiled=True)  20.1 us
    pallas_call x2, Pallas kernels, run_experts(): pl.pallas_call(functools.partial(expert_kernel, cuts, step, members), in_...  14.7 us
    pallas_call x1, Pallas kernels, bucket_grad(): pl.pallas_call(functools.partial(bucket_kernel, buckets), grid=(seq_len /...  7.59 us
    pallas_call x1, Pallas kernels, attend(): pl.pallas_call(functools.partial(attend_kernel, head_size), grid=(heads /...  7.34 us
    unnamed x83, local copies, waits for them, and re-layouts  6.46 us
  transfers between devices with their start and end apart: 51, of which 27 were waited for; matrix products, arithmetic and copies ran while one was open for 14% of the time, Pallas kernels for 13%

profile of v3, /device:TPU:0, one launch (start us, length us, event | category | flops | bytes accessed | tf_op | source)
XLA Modules:
  0.0 225.9 jit_solution(13832886817296146110)
XLA Ops:
  0.7 3.0 %collective-permute-start.1 = (bf16[128,1024]{1,0:T(8,128)(2,1)}, bf16[128,1024]{1,0:T(8,128)(2,1)S(1)}, u32[]{:S(2)}, u32[]{:S(2)}) collective-permute-start(bf16[128,1024]{1,0:T(8,128)(2,1)} %refs_0_.1), channel_id=1, source_target_pairs={{0,2},{1,3},{2,0},{3,1},{4,6},{5,7},{6,4},{7,5},{8,10},{9,11},{10,... | collective-permute-start | bytes 786440 | tf_op jit(solution)/shard_map/ppermute | solution.py:22
  5.6 4.0 %bias_lookup.1 = (f32[4,512,512]{2,1,0:T(8,128)S(1)}, s32[512,512]{1,0:T(8,128)}) custom-call(s32[1]{0:T(128)} %bitcast.shift_ref, s32[512,512]{1,0:T(8,128)S(1)} %copy-done.8, f32[4,128]{1,0:T(4,128)S(1)} %pad.4.bucket_ref), custom_call_target="tpu_custom_call" | custom-call | bytes 2048 | tf_op jit(solution)/shard_map/bias_lookup/pallas_call | solution.py:136
  13.4 7.3 %attend.1 = (bf16[512,1024]{1,0:T(8,128)(2,1)}, bf16[512,768]{1,0:T(8,128)(2,1)}, bf16[512,256]{1,0:T(8,128)(2,1)S(1)}, bf16[1,4,512,512]{3,2,1,0:T(8,128)(2,1)}) custom-call(bf16[128,1024]{1,0:T(8,128)(2,1)S(1)} %copy-done.2, bf16[128,1024]{1,0:T(8,128)(2,1)S(1)} %collective-permute-done.refs_1_, bf16[128,1024]{1,0:T(8,128)(2,1)S(1)} %collective-permute-done.1.refs_2_, ...), custom_call_target="tpu_custom_call" | custom-call | bytes 2048 | tf_op jit(solution)/shard_map/attend/pallas_call | solution.py:250
  25.3 6.5 %collective-permute-done.4 = bf16[1,128,1024]{2,1,0:T(8,128)(2,1)S(1)} collective-permute-done((bf16[1,128,1024]{2,1,0:T(8,128)(2,1)S(1)}, bf16[1,128,1024]{2,1,0:T(8,128)(2,1)S(1)}, u32[]{:S(2)}, u32[]{:S(2)}) %collective-permute-start.4) | collective-permute-done | bytes 262176 | tf_op jit(solution)/shard_map/ppermute | solution.py:22
  34.3 6.0 %all-to-all-start = ((bf16[8,40,512]{2,1,0:T(8,128)(2,1)}), bf16[8,40,512]{2,1,0:T(8,128)(2,1)S(1)}, u32[]{:S(2)}, u32[]{:S(2)}) async-start(bf16[8,40,512]{2,1,0:T(8,128)(2,1)} %bitcast.12), calls=%async_computation | async-start | bytes 655360 | tf_op jit(solution)/shard_map/all_to_all | solution.py:57
  41.5 8.6 %all-to-all-done = bf16[8,40,512]{2,1,0:T(8,128)(2,1)S(1)} async-done(((bf16[8,40,512]{2,1,0:T(8,128)(2,1)}), bf16[8,40,512]{2,1,0:T(8,128)(2,1)S(1)}, u32[]{:S(2)}, u32[]{:S(2)}) %all-to-all-start) | async-done | bytes 327712 | tf_op jit(solution)/shard_map/all_to_all | solution.py:57
  50.1 3.6 %all-to-all-start.1 = ((bf16[8,40,512]{2,1,0:T(8,128)(2,1)}), bf16[8,40,512]{2,1,0:T(8,128)(2,1)S(1)}, u32[]{:S(2)}, u32[]{:S(2)}) async-start(bf16[8,40,512]{2,1,0:T(8,128)(2,1)} %bitcast.14), calls=%async_computation.1 | async-start | bytes 655360 | tf_op jit(solution)/shard_map/all_to_all | solution.py:57
  55.3 2.6 %pad_maximum_fusion = bf16[1024,768]{1,0:T(8,128)(2,1)} fusion(bf16[1024,256]{1,0:T(8,128)(2,1)} %refs_7_.1, bf16[1024,256]{1,0:T(8,128)(2,1)} %refs_6_.2, bf16[1024,256]{1,0:T(8,128)(2,1)} %refs_5_.3), kind=kLoop, calls=%fused_computation.5 | loop fusion | flops 4718592 | bytes 3145728 | tf_op jit(solution)/shard_map/concatenate | solution.py:594
  57.9 5.6 %all-to-all-done.1 = bf16[8,40,512]{2,1,0:T(8,128)(2,1)S(1)} async-done(((bf16[8,40,512]{2,1,0:T(8,128)(2,1)}), bf16[8,40,512]{2,1,0:T(8,128)(2,1)S(1)}, u32[]{:S(2)}, u32[]{:S(2)}) %all-to-all-start.1) | async-done | bytes 327712 | tf_op jit(solution)/shard_map/all_to_all | solution.py:57
  65.2 6.7 %experts.1 = (f32[2,320,704]{2,1,0:T(8,128)S(1)}, bf16[2,320,704]{2,1,0:T(8,128)(2,1)}, bf16[2,320,1024]{2,1,0:T(8,128)(2,1)}, bf16[2,320,512]{2,1,0:T(8,128)(2,1)S(1)}, bf16[2,320,512]{2,1,0:T(8,128)(2,1)S(1)}) custom-call(bf16[320,512]{1,0:T(8,128)(2,1)S(1)} %bitcast.243, bf16[320,512]{1,0:T(8,128)(2,1)S(1)} %collective-permute-done.5.refs_1_, ...), custom_call_target="tpu_custom_call" | custom-call | bytes 2048 | tf_op jit(solution)/shard_map/experts/pallas_call | solution.py:467
  77.6 8.0 %experts_back.1 = (bf16[2,320,704]{2,1,0:T(8,128)(2,1)}, bf16[2,320,1024]{2,1,0:T(8,128)(2,1)}, bf16[2,320,512]{2,1,0:T(8,128)(2,1)S(1)}, bf16[2,320,512]{2,1,0:T(8,128)(2,1)}) custom-call(bf16[320,512]{1,0:T(8,128)(2,1)S(1)} %bitcast.240, bf16[320,512]{1,0:T(8,128)(2,1)S(1)} %collective-permute-done.6.refs_1_, ...), custom_call_target="tpu_custom_call" | custom-call | bytes 2048 | tf_op jit(solution)/shard_map/experts_back/pallas_call | solution.py:467
  86.7 4.6 %all-to-all-start.2 = ((bf16[8,40,512]{2,1,0:T(8,128)(2,1)}), bf16[8,40,512]{2,1,0:T(8,128)(2,1)}, u32[]{:S(2)}, u32[]{:S(2)}) async-start(bf16[8,40,512]{2,1,0:T(8,128)(2,1)} %bitcast.22), calls=%async_computation.2 | async-start | bytes 655360 | tf_op jit(solution)/shard_map/all_to_all | solution.py:57
  96.1 4.3 %fusion.116 = f32[2,704,1024]{2,1,0:T(8,128)} fusion(bf16[2,320,704]{2,1,0:T(8,128)(2,1)S(1)} %copy-done.32, bf16[2,320,1024]{2,1,0:T(8,128)(2,1)S(1)} %copy-done.30), kind=kOutput, calls=%fused_computation.272 | convolution fusion | flops 922746880 | bytes 7979008 | tf_op jit(solution)/shard_map/jrf,jrd->jfd/dot_general | solution.py:606
  106.6 5.8 %all-to-all-start.3 = ((bf16[8,40,512]{2,1,0:T(8,128)(2,1)}), bf16[8,40,512]{2,1,0:T(8,128)(2,1)S(1)}, u32[]{:S(2)}, u32[]{:S(2)}) async-start(bf16[8,40,512]{2,1,0:T(8,128)(2,1)} %bitcast.283), calls=%async_computation.3 | async-start | bytes 655360 | tf_op jit(solution)/shard_map/all_to_all | solution.py:57
  114.6 7.3 %all-to-all-done.3 = bf16[8,40,512]{2,1,0:T(8,128)(2,1)S(1)} async-done(((bf16[8,40,512]{2,1,0:T(8,128)(2,1)}), bf16[8,40,512]{2,1,0:T(8,128)(2,1)S(1)}, u32[]{:S(2)}, u32[]{:S(2)}) %all-to-all-start.3) | async-done | bytes 327712 | tf_op jit(solution)/shard_map/all_to_all | solution.py:57
  124.9 4.3 %fusion.118 = f32[2,704,1024]{2,1,0:T(8,128)} fusion(bf16[2,320,704]{2,1,0:T(8,128)(2,1)S(1)} %copy-done.31, bf16[2,320,1024]{2,1,0:T(8,128)(2,1)S(1)} %copy-done.29), kind=kOutput, calls=%fused_computation.274 | convolution fusion | flops 922746880 | bytes 7979008 | tf_op jit(solution)/shard_map/jrf,jrd->jfd/dot_general | solution.py:608
  134.0 3.9 %attend_back.1 = (bf16[512,768]{1,0:T(8,128)(2,1)S(1)}, bf16[1,4,512,512]{3,2,1,0:T(8,128)(2,1)}) custom-call(bf16[512,768]{1,0:T(8,128)(2,1)S(1)} %copy-done.9, bf16[512,256]{1,0:T(8,128)(2,1)S(1)} %get-tuple-element.97.grad_ref, bf16[1,4,512,512]{3,2,1,0:T(8,128)(2,1)S(1)} %copy-done.5), custom_call_target="tpu_custom_call" | custom-call | bytes 2048 | tf_op jit(solution)/shard_map/attend_back/pallas_call | solution.py:347
  137.9 2.6 %collective-permute-done.18 = bf16[128,1024]{1,0:T(8,128)(2,1)S(1)} collective-permute-done((bf16[128,1024]{1,0:T(8,128)(2,1)S(1)}, bf16[128,1024]{1,0:T(8,128)(2,1)S(1)}, u32[]{:S(2)}, u32[]{:S(2)}) %collective-permute-start.18) | collective-permute-done | bytes 262176 | tf_op jit(solution)/shard_map/ppermute | solution.py:22
  147.2 8.1 %collective-permute-done.34 = bf16[256,768]{1,0:T(8,128)(2,1)S(1)} collective-permute-done((bf16[256,768]{1,0:T(8,128)(2,1)S(1)}, bf16[256,768]{1,0:T(8,128)(2,1)S(1)}, u32[]{:S(2)}, u32[]{:S(2)}) %collective-permute-start.34) | collective-permute-done | bytes 393248 | tf_op jit(solution)/shard_map/ppermute | solution.py:22
  159.8 7.6 %bucket_grad.1 = f32[32,128]{1,0:T(8,128)S(1)} custom-call(s32[512,512]{1,0:T(8,128)S(1)} %copy-done.7, bf16[1,4,512,512]{3,2,1,0:T(8,128)(2,1)S(1)} %copy-done.6), custom_call_target="tpu_custom_call" | custom-call | bytes 2048 | tf_op jit(solution)/shard_map/bucket_grad/pallas_call | solution.py:184
  192.3 3.1 %collective-permute-start.30 = (bf16[64,768]{1,0:T(8,128)(2,1)S(1)}, bf16[64,768]{1,0:T(8,128)(2,1)S(1)}, u32[]{:S(2)}, u32[]{:S(2)}) collective-permute-start(bf16[64,768]{1,0:T(8,128)(2,1)S(1)} %fusion.47), channel_id=1, source_target_pairs={{0,16},{4,20},{8,24},{12,28},{16,0},{20,4},{24,8},{28,12},{1,17},{... | collective-permute-start | bytes 294920 | tf_op jit(solution)/shard_map/ppermute | solution.py:22
  195.5 2.9 %collective-permute-done.32 = bf16[64,768]{1,0:T(8,128)(2,1)S(1)} collective-permute-done((bf16[64,768]{1,0:T(8,128)(2,1)S(1)}, bf16[64,768]{1,0:T(8,128)(2,1)S(1)}, u32[]{:S(2)}, u32[]{:S(2)}) %collective-permute-start.32) | collective-permute-done | bytes 98336 | tf_op jit(solution)/shard_map/ppermute | solution.py:22
  211.9 2.7 %collective-permute-done.26 = f32[19,1024]{1,0:T(8,128)S(1)} collective-permute-done((f32[19,1024]{1,0:T(8,128)S(1)}, f32[19,1024]{1,0:T(8,128)S(1)}, u32[]{:S(2)}, u32[]{:S(2)}) %collective-permute-start.26) | collective-permute-done | bytes 77856 | tf_op jit(solution)/shard_map/ppermute | solution.py:22
  217.6 2.5 %collective-permute-start.46 = (bf16[4,32,1024]{2,1,0:T(8,128)(2,1)S(1)}, bf16[4,32,1024]{2,1,0:T(8,128)(2,1)S(1)}, u32[]{:S(2)}, u32[]{:S(2)}) collective-permute-start(bf16[4,32,1024]{2,1,0:T(8,128)(2,1)S(1)} %get-tuple-element.176), channel_id=1, source_target_pairs={{0,4},{4,0},{8,12},{12,8},{16,20},{20,16},{24,28},{28,24},{1,5},{5... | collective-permute-start | bytes 786440 | tf_op jit(solution)/shard_map/ppermute | solution.py:22
  (279 shorter events, 102.5 us)
Async XLA Ops:
  0.7 9.6 %collective-permute-start.1 = (bf16[128,1024]{1,0:T(8,128)(2,1)}, bf16[128,1024]{1,0:T(8,128)(2,1)S(1)}, u32[]{:S(2)}, u32[]{:S(2)}) collective-permute-start(bf16[128,1024]{1,0:T(8,128)(2,1)} %refs_0_.1), channel_id=1, source_target_pairs={{0,2},{1,3},{2,0},{3,1},{4,6},{5,7},{6,4},{7,5},{8,10},{9,11},{10,... | collective-permute-start | bytes 786440 | tf_op jit(solution)/shard_map/ppermute | solution.py:22
  34.3 15.8 %all-to-all-start = ((bf16[8,40,512]{2,1,0:T(8,128)(2,1)}), bf16[8,40,512]{2,1,0:T(8,128)(2,1)S(1)}, u32[]{:S(2)}, u32[]{:S(2)}) async-start(bf16[8,40,512]{2,1,0:T(8,128)(2,1)} %bitcast.12), calls=%async_computation | async-start | bytes 655360 | tf_op jit(solution)/shard_map/all_to_all | solution.py:57
  50.1 13.5 %all-to-all-start.1 = ((bf16[8,40,512]{2,1,0:T(8,128)(2,1)}), bf16[8,40,512]{2,1,0:T(8,128)(2,1)S(1)}, u32[]{:S(2)}, u32[]{:S(2)}) async-start(bf16[8,40,512]{2,1,0:T(8,128)(2,1)} %bitcast.14), calls=%async_computation.1 | async-start | bytes 655360 | tf_op jit(solution)/shard_map/all_to_all | solution.py:57
  53.7 9.8 %collective-permute-start.5 = (bf16[320,512]{1,0:T(8,128)(2,1)S(1)}, bf16[320,512]{1,0:T(8,128)(2,1)S(1)}, u32[]{:S(2)}, u32[]{:S(2)}) collective-permute-start(bf16[320,512]{1,0:T(8,128)(2,1)S(1)} %bitcast.241), channel_id=1, source_target_pairs={{0,2},{1,3},{2,0},{3,1},{4,6},{5,7},{6,4},{7,5},{8,10},{9,11},{10,... | collective-permute-start | bytes 983048 | tf_op jit(solution)/shard_map/ppermute | solution.py:22
  63.6 10.1 %collective-permute-start.6 = (bf16[320,512]{1,0:T(8,128)(2,1)S(1)}, bf16[320,512]{1,0:T(8,128)(2,1)S(1)}, u32[]{:S(2)}, u32[]{:S(2)}) collective-permute-start(bf16[320,512]{1,0:T(8,128)(2,1)S(1)} %bitcast.238), channel_id=1, source_target_pairs={{0,2},{1,3},{2,0},{3,1},{4,6},{5,7},{6,4},{7,5},{8,10},{9,11},{10,... | collective-permute-start | bytes 983048 | tf_op jit(solution)/shard_map/ppermute | solution.py:22
  76.0 9.8 %collective-permute-start.10 = (bf16[1,320,512]{2,1,0:T(8,128)(2,1)S(1)}, bf16[1,320,512]{2,1,0:T(8,128)(2,1)S(1)}, u32[]{:S(2)}, u32[]{:S(2)}) collective-permute-start(bf16[1,320,512]{2,1,0:T(8,128)(2,1)S(1)} %fusion.31), channel_id=1, source_target_pairs={{0,2},{1,3},{2,0},{3,1},{4,6},{5,7},{6,4},{7,5},{8,10},{9,11},{10,... | collective-permute-start | bytes 983048 | tf_op jit(solution)/shard_map/ppermute | solution.py:22
  86.7 15.7 %all-to-all-start.2 = ((bf16[8,40,512]{2,1,0:T(8,128)(2,1)}), bf16[8,40,512]{2,1,0:T(8,128)(2,1)}, u32[]{:S(2)}, u32[]{:S(2)}) async-start(bf16[8,40,512]{2,1,0:T(8,128)(2,1)} %bitcast.22), calls=%async_computation.2 | async-start | bytes 655360 | tf_op jit(solution)/shard_map/all_to_all | solution.py:57
  94.6 10.2 %collective-permute-start.14 = (bf16[1,320,512]{2,1,0:T(8,128)(2,1)}, bf16[1,320,512]{2,1,0:T(8,128)(2,1)}, u32[]{:S(2)}, u32[]{:S(2)}) collective-permute-start(bf16[1,320,512]{2,1,0:T(8,128)(2,1)} %fusion.32), channel_id=1, source_target_pairs={{0,2},{1,3},{2,0},{3,1},{4,6},{5,7},{6,4},{7,5},{8,10},{9,11},{10,... | collective-permute-start | bytes 983048 | tf_op jit(solution)/shard_map/ppermute | solution.py:22
  106.6 15.4 %all-to-all-start.3 = ((bf16[8,40,512]{2,1,0:T(8,128)(2,1)}), bf16[8,40,512]{2,1,0:T(8,128)(2,1)S(1)}, u32[]{:S(2)}, u32[]{:S(2)}) async-start(bf16[8,40,512]{2,1,0:T(8,128)(2,1)} %bitcast.283), calls=%async_computation.3 | async-start | bytes 655360 | tf_op jit(solution)/shard_map/all_to_all | solution.py:57
  143.2 12.1 %collective-permute-start.34 = (bf16[256,768]{1,0:T(8,128)(2,1)S(1)}, bf16[256,768]{1,0:T(8,128)(2,1)S(1)}, u32[]{:S(2)}, u32[]{:S(2)}) collective-permute-start(bf16[256,768]{1,0:T(8,128)(2,1)S(1)} %dynamic-slice_bitcast_fusion), channel_id=1, source_target_pairs={{0,4},{4,0},{8,12},{12,8},{16,20},{20,16},{24,28},{28,24},{1,5},{5... | collective-permute-start | bytes 1179656 | tf_op jit(solution)/shard_map/ppermute | solution.py:22
  144.8 27.3 %collective-permute-start.19 = (bf16[256,768]{1,0:T(8,128)(2,1)}, bf16[256,768]{1,0:T(8,128)(2,1)}, u32[]{:S(2)}, u32[]{:S(2)}) collective-permute-start(bf16[256,768]{1,0:T(8,128)(2,1)} %get-tuple-element.155), channel_id=1, source_target_pairs={{0,4},{4,0},{8,12},{12,8},{16,20},{20,16},{24,28},{28,24},{1,5},{5... | collective-permute-start | bytes 1179656 | tf_op jit(solution)/shard_map/ppermute | solution.py:22
  147.2 24.9 %collective-permute-start.20 = (bf16[2,128,1024]{2,1,0:T(8,128)(2,1)}, bf16[2,128,1024]{2,1,0:T(8,128)(2,1)}, u32[]{:S(2)}, u32[]{:S(2)}) collective-permute-start(bf16[2,128,1024]{2,1,0:T(8,128)(2,1)} %fusion.18), channel_id=1, source_target_pairs={{0,1},{1,0},{2,3},{3,2},{4,5},{5,4},{6,7},{7,6},{8,9},{9,8},{10,11... | collective-permute-start | bytes 1572872 | tf_op jit(solution)/shard_map/ppermute | solution.py:22
  156.2 11.4 %collective-permute-start.35 = (bf16[64,768]{1,0:T(8,128)(2,1)}, bf16[64,768]{1,0:T(8,128)(2,1)S(1)}, u32[]{:S(2)}, u32[]{:S(2)}) collective-permute-start(bf16[64,768]{1,0:T(8,128)(2,1)} %get-tuple-element.167), channel_id=1, source_target_pairs={{0,8},{4,12},{8,0},{12,4},{16,24},{20,28},{24,16},{28,20},{1,9},{5... | collective-permute-start | bytes 294920 | tf_op jit(solution)/shard_map/ppermute | solution.py:22
  157.3 10.3 %collective-permute-start.37 = (bf16[64,768]{1,0:T(8,128)(2,1)}, bf16[64,768]{1,0:T(8,128)(2,1)S(1)}, u32[]{:S(2)}, u32[]{:S(2)}) collective-permute-start(bf16[64,768]{1,0:T(8,128)(2,1)} %get-tuple-element.168), channel_id=1, source_target_pairs={{0,24},{4,28},{8,16},{12,20},{16,8},{20,12},{24,0},{28,4},{1,25},{... | collective-permute-start | bytes 294920 | tf_op jit(solution)/shard_map/ppermute | solution.py:22
  158.7 8.9 %collective-permute-start.36 = (bf16[64,768]{1,0:T(8,128)(2,1)S(1)}, bf16[64,768]{1,0:T(8,128)(2,1)S(1)}, u32[]{:S(2)}, u32[]{:S(2)}) collective-permute-start(bf16[64,768]{1,0:T(8,128)(2,1)S(1)} %get-tuple-element.169), channel_id=1, source_target_pairs={{0,16},{4,20},{8,24},{12,28},{16,0},{20,4},{24,8},{28,12},{1,17},{... | collective-permute-start | bytes 294920 | tf_op jit(solution)/shard_map/ppermute | solution.py:22
  172.3 9.5 %collective-permute-start.22 = (f32[19,1024]{1,0:T(8,128)S(1)}, f32[19,1024]{1,0:T(8,128)S(1)}, u32[]{:S(2)}, u32[]{:S(2)}) collective-permute-start(f32[19,1024]{1,0:T(8,128)S(1)} %pad_maximum_fusion.7), channel_id=1, source_target_pairs={{0,1},{1,0},{2,3},{3,2},{4,5},{5,4},{6,7},{7,6},{8,9},{9,8},{10,11... | collective-permute-start | bytes 233480 | tf_op jit(solution)/shard_map/ppermute | solution.py:22
  176.0 30.7 %collective-permute-start.21 = (bf16[1,128,1024]{2,1,0:T(8,128)(2,1)S(1)}, bf16[1,128,1024]{2,1,0:T(8,128)(2,1)S(1)}, u32[]{:S(2)}, u32[]{:S(2)}) collective-permute-start(bf16[1,128,1024]{2,1,0:T(8,128)(2,1)S(1)} %fusion.34), channel_id=1, source_target_pairs={{0,2},{1,3},{2,0},{3,1},{4,6},{5,7},{6,4},{7,5},{8,10},{9,11},{10,... | collective-permute-start | bytes 786440 | tf_op jit(solution)/shard_map/ppermute | solution.py:22
  181.8 9.0 %collective-permute-start.28 = (bf16[64,768]{1,0:T(8,128)(2,1)S(1)}, bf16[64,768]{1,0:T(8,128)(2,1)S(1)}, u32[]{:S(2)}, u32[]{:S(2)}) collective-permute-start(bf16[64,768]{1,0:T(8,128)(2,1)S(1)} %get-tuple-element.174), channel_id=1, source_target_pairs={{0,16},{4,20},{8,24},{12,28},{16,0},{20,4},{24,8},{28,12},{1,17},{... | collective-permute-start | bytes 294920 | tf_op jit(solution)/shard_map/ppermute | solution.py:22
  182.2 38.3 %collective-permute-start.41 = (bf16[4,64,768]{2,1,0:T(8,128)(2,1)S(1)}, bf16[4,64,768]{2,1,0:T(8,128)(2,1)S(1)}, u32[]{:S(2)}, u32[]{:S(2)}) collective-permute-start(bf16[4,64,768]{2,1,0:T(8,128)(2,1)S(1)} %get-tuple-element.166), channel_id=1, source_target_pairs={{0,4},{4,0},{8,12},{12,8},{16,20},{20,16},{24,28},{28,24},{1,5},{5... | collective-permute-start | bytes 1179656 | tf_op jit(solution)/shard_map/ppermute | solution.py:22
  183.8 8.5 %collective-permute-start.23 = (f32[19,1024]{1,0:T(8,128)S(1)}, f32[19,1024]{1,0:T(8,128)S(1)}, u32[]{:S(2)}, u32[]{:S(2)}) collective-permute-start(f32[19,1024]{1,0:T(8,128)S(1)} %fusion.103), channel_id=1, source_target_pairs={{0,2},{1,3},{2,0},{3,1},{4,6},{5,7},{6,4},{7,5},{8,10},{9,11},{10,... | collective-permute-start | bytes 233480 | tf_op jit(solution)/shard_map/ppermute | solution.py:22
  192.3 8.6 %collective-permute-start.31 = (bf16[64,768]{1,0:T(8,128)(2,1)S(1)}, bf16[64,768]{1,0:T(8,128)(2,1)S(1)}, u32[]{:S(2)}, u32[]{:S(2)}) collective-permute-start(bf16[64,768]{1,0:T(8,128)(2,1)S(1)} %fusion.47), channel_id=1, source_target_pairs={{0,8},{4,12},{8,0},{12,4},{16,24},{20,28},{24,16},{28,20},{1,9},{5... | collective-permute-start | bytes 294920 | tf_op jit(solution)/shard_map/ppermute | solution.py:22
  192.3 9.2 %collective-permute-start.30 = (bf16[64,768]{1,0:T(8,128)(2,1)S(1)}, bf16[64,768]{1,0:T(8,128)(2,1)S(1)}, u32[]{:S(2)}, u32[]{:S(2)}) collective-permute-start(bf16[64,768]{1,0:T(8,128)(2,1)S(1)} %fusion.47), channel_id=1, source_target_pairs={{0,16},{4,20},{8,24},{12,28},{16,0},{20,4},{24,8},{28,12},{1,17},{... | collective-permute-start | bytes 294920 | tf_op jit(solution)/shard_map/ppermute | solution.py:22
  201.6 18.4 %collective-permute-start.33 = (bf16[4,64,768]{2,1,0:T(8,128)(2,1)S(1)}, bf16[4,64,768]{2,1,0:T(8,128)(2,1)S(1)}, u32[]{:S(2)}, u32[]{:S(2)}) collective-permute-start(bf16[4,64,768]{2,1,0:T(8,128)(2,1)S(1)} %get-tuple-element.171), channel_id=1, source_target_pairs={{0,4},{4,0},{8,12},{12,8},{16,20},{20,16},{24,28},{28,24},{1,5},{5... | collective-permute-start | bytes 1179656 | tf_op jit(solution)/shard_map/ppermute | solution.py:22
  206.6 10.1 %collective-permute-start.45 = (bf16[2,32,1024]{2,1,0:T(8,128)(2,1)S(1)}, bf16[2,32,1024]{2,1,0:T(8,128)(2,1)}, u32[]{:S(2)}, u32[]{:S(2)}) collective-permute-start(bf16[2,32,1024]{2,1,0:T(8,128)(2,1)S(1)} %pad_maximum_fusion.6), channel_id=1, source_target_pairs={{0,8},{4,12},{8,0},{12,4},{16,24},{20,28},{24,16},{28,20},{1,9},{5... | collective-permute-start | bytes 393224 | tf_op jit(solution)/shard_map/ppermute | solution.py:22
  (68 other events, 430.1 us)

commit v4 on v3

--- a/solution.py
+++ b/solution.py
@@ -246,7 +246,8 @@
     head_cols = w_query.shape[1]
     pair = min(heads, LANES // head_size)
     weight = pl.BlockSpec((width, head_cols), lambda h: (0, 0))
-    weights = [pltpu.with_memory_space_constraint(item, pltpu.HBM) for item in (w_query, w_key, w_value)]
+    gain, *weights = [pltpu.with_memory_space_constraint(item, pltpu.HBM) for item in (gain, w_query, w_key, w_value)]
+    blocks = [pltpu.with_memory_space_constraint(blocks[0], pltpu.HBM)] + blocks[1:]
     return pl.pallas_call(
         functools.partial(attend_kernel, head_size),
         grid=(heads // pair,),
@@ -390,9 +391,9 @@
     loads = []
     for expert in range(experts):
         for at, (source, held) in enumerate(((first_ref, first_held), (second_ref, second_held))):
-            load = pltpu.make_async_copy(source.at[expert], held.at[expert], arrived.at[2 * expert + at])
-            load.start()
-            loads.append(load)
+            loads.append(pltpu.make_async_copy(source.at[expert], held.at[expert], arrived.at[2 * expert + at]))
+    for load in loads[:2]:
+        load.start()
     places = [
         (order_ref[expert] == lax.broadcasted_iota(jnp.int32, (all_rows, picked), 0)).astype(f32)
         for expert in range(experts)
@@ -411,6 +412,9 @@
     results = []
     for expert in range(experts):
         loads[2 * expert].wait()
+        if 2 * expert + 2 < len(loads):
+            loads[2 * expert + 2].start()
+            loads[2 * expert + 3].start()
         inner = lax.dot_general(
             rows_ref[expert], first_held[expert], (((1,), (1,)), ((), ())), preferred_element_type=f32
         )
@@ -650,7 +654,7 @@
     )
     small = jnp.concatenate([grad_gain_moe, gain_partial, bucket_row, grad_router_t], axis=0)
     for axis in ("mp", "dp"):
-        for bit in range(bit_count(axis)):
+        for bit in reversed(range(bit_count(axis))):
             small = small + swap(small, axis, 1 << bit)
     attn_grad = scatter_rest(*attn_hop)
     grad_w_output = last_step(sum_rest(output_near))

time: 227 us -> 224 us (0.987)
    unnamed x83 -> x85, local copies, waits for them, and re-layouts: 6.46 us -> 4.84 us
  transfers between devices with their start and end apart: 51 -> 51, of which waited for: 27 -> 28; matrix products, arithmetic and copies ran while one was open for 14% -> 14% of each run, Pallas kernels for 13% -> 14%
where the time goes in v4:
time: 224 us; the launch traced here: 223 us
  starting transfers between devices  71.4 us (32%)
  waiting for transfers between devices  67.4 us (30%)
  Pallas kernels  38.2 us (17%)
  matrix products  16.4 us (7%)
  other arithmetic  15.8 us (7%)
  local copies, waits for them, and re-layouts  12.5 us (6%)
    ppermute x47, starting transfers between devices, swap(): return lax.ppermute(block, axis, [(i, i ^ offset) for i in range(size)])  51.3 us
    ppermute x47, waiting for transfers between devices, swap(): return lax.ppermute(block, axis, [(i, i ^ offset) for i in range(size)])  44.1 us
    all_to_all x4, waiting for transfers between devices, exchange_groups(): return lax.all_to_all(buffer, 'dp', split_axis=0, concat_axis=0, tiled=True)  23.4 us
    all_to_all x4, starting transfers between devices, exchange_groups(): return lax.all_to_all(buffer, 'dp', split_axis=0, concat_axis=0, tiled=True)  20.1 us
    pallas_call x2, Pallas kernels, run_experts(): pl.pallas_call(functools.partial(expert_kernel, cuts, step, members), in_...  14.7 us
    pallas_call x1, Pallas kernels, bucket_grad(): pl.pallas_call(functools.partial(bucket_kernel, buckets), grid=(seq_len /...  7.57 us
    pallas_call x1, Pallas kernels, attend(): pl.pallas_call(functools.partial(attend_kernel, head_size), grid=(heads /...  7.25 us
    unnamed x85, local copies, waits for them, and re-layouts  4.84 us
  transfers between devices with their start and end apart: 51, of which 28 were waited for; matrix products, arithmetic and copies ran while one was open for 14% of the time, Pallas kernels for 14%

profile of v4, /device:TPU:0, one launch (start us, length us, event | category | flops | bytes accessed | tf_op | source)
XLA Modules:
  0.0 223.3 jit_solution(12421787636013782437)
XLA Ops:
  0.7 3.0 %collective-permute-start.1 = (bf16[128,1024]{1,0:T(8,128)(2,1)}, bf16[128,1024]{1,0:T(8,128)(2,1)S(1)}, u32[]{:S(2)}, u32[]{:S(2)}) collective-permute-start(bf16[128,1024]{1,0:T(8,128)(2,1)} %refs_0_.1), channel_id=1, source_target_pairs={{0,2},{1,3},{2,0},{3,1},{4,6},{5,7},{6,4},{7,5},{8,10},{9,11},{10,... | collective-permute-start | bytes 786440 | tf_op jit(solution)/shard_map/ppermute | solution.py:22
  5.6 4.0 %bias_lookup.1 = (f32[4,512,512]{2,1,0:T(8,128)S(1)}, s32[512,512]{1,0:T(8,128)}) custom-call(s32[1]{0:T(128)} %bitcast.shift_ref, s32[512,512]{1,0:T(8,128)S(1)} %copy-done.6, f32[4,128]{1,0:T(4,128)S(1)} %pad.4.bucket_ref), custom_call_target="tpu_custom_call" | custom-call | bytes 2048 | tf_op jit(solution)/shard_map/bias_lookup/pallas_call | solution.py:136
  11.8 7.3 %attend.1 = (bf16[512,1024]{1,0:T(8,128)(2,1)}, bf16[512,768]{1,0:T(8,128)(2,1)}, bf16[512,256]{1,0:T(8,128)(2,1)S(1)}, bf16[1,4,512,512]{3,2,1,0:T(8,128)(2,1)}) custom-call(bf16[128,1024]{1,0:T(8,128)(2,1)} %refs_0_.1, bf16[128,1024]{1,0:T(8,128)(2,1)S(1)} %collective-permute-done.refs_1_, bf16[128,1024]{1,0:T(8,128)(2,1)S(1)} %collective-permute-done.1.refs_2_, ...), custom_call_target="tpu_custom_call" | custom-call | bytes 2048 | tf_op jit(solution)/shard_map/attend/pallas_call | solution.py:251
  23.5 6.5 %collective-permute-done.4 = bf16[1,128,1024]{2,1,0:T(8,128)(2,1)S(1)} collective-permute-done((bf16[1,128,1024]{2,1,0:T(8,128)(2,1)S(1)}, bf16[1,128,1024]{2,1,0:T(8,128)(2,1)S(1)}, u32[]{:S(2)}, u32[]{:S(2)}) %collective-permute-start.4) | collective-permute-done | bytes 262176 | tf_op jit(solution)/shard_map/ppermute | solution.py:22
  32.6 6.0 %all-to-all-start = ((bf16[8,40,512]{2,1,0:T(8,128)(2,1)}), bf16[8,40,512]{2,1,0:T(8,128)(2,1)S(1)}, u32[]{:S(2)}, u32[]{:S(2)}) async-start(bf16[8,40,512]{2,1,0:T(8,128)(2,1)} %bitcast.12), calls=%async_computation | async-start | bytes 655360 | tf_op jit(solution)/shard_map/all_to_all | solution.py:57
  39.8 8.6 %all-to-all-done = bf16[8,40,512]{2,1,0:T(8,128)(2,1)S(1)} async-done(((bf16[8,40,512]{2,1,0:T(8,128)(2,1)}), bf16[8,40,512]{2,1,0:T(8,128)(2,1)S(1)}, u32[]{:S(2)}, u32[]{:S(2)}) %all-to-all-start) | async-done | bytes 327712 | tf_op jit(solution)/shard_map/all_to_all | solution.py:57
  48.4 3.6 %all-to-all-start.1 = ((bf16[8,40,512]{2,1,0:T(8,128)(2,1)}), bf16[8,40,512]{2,1,0:T(8,128)(2,1)S(1)}, u32[]{:S(2)}, u32[]{:S(2)}) async-start(bf16[8,40,512]{2,1,0:T(8,128)(2,1)} %bitcast.14), calls=%async_computation.1 | async-start | bytes 655360 | tf_op jit(solution)/shard_map/all_to_all | solution.py:57
  53.6 2.6 %pad_maximum_fusion = bf16[1024,768]{1,0:T(8,128)(2,1)} fusion(bf16[1024,256]{1,0:T(8,128)(2,1)} %refs_7_.1, bf16[1024,256]{1,0:T(8,128)(2,1)} %refs_6_.2, bf16[1024,256]{1,0:T(8,128)(2,1)} %refs_5_.3), kind=kLoop, calls=%fused_computation.5 | loop fusion | flops 4718592 | bytes 3145728 | tf_op jit(solution)/shard_map/concatenate | solution.py:598
  56.2 5.6 %all-to-all-done.1 = bf16[8,40,512]{2,1,0:T(8,128)(2,1)S(1)} async-done(((bf16[8,40,512]{2,1,0:T(8,128)(2,1)}), bf16[8,40,512]{2,1,0:T(8,128)(2,1)S(1)}, u32[]{:S(2)}, u32[]{:S(2)}) %all-to-all-start.1) | async-done | bytes 327712 | tf_op jit(solution)/shard_map/all_to_all | solution.py:57
  63.5 6.7 %experts.1 = (f32[2,320,704]{2,1,0:T(8,128)S(1)}, bf16[2,320,704]{2,1,0:T(8,128)(2,1)}, bf16[2,320,1024]{2,1,0:T(8,128)(2,1)}, bf16[2,320,512]{2,1,0:T(8,128)(2,1)S(1)}, bf16[2,320,512]{2,1,0:T(8,128)(2,1)S(1)}) custom-call(bf16[320,512]{1,0:T(8,128)(2,1)S(1)} %bitcast.243, bf16[320,512]{1,0:T(8,128)(2,1)S(1)} %collective-permute-done.5.refs_1_, ...), custom_call_target="tpu_custom_call" | custom-call | bytes 2048 | tf_op jit(solution)/shard_map/experts/pallas_call | solution.py:471
  75.9 7.9 %experts_back.1 = (bf16[2,320,704]{2,1,0:T(8,128)(2,1)}, bf16[2,320,1024]{2,1,0:T(8,128)(2,1)}, bf16[2,320,512]{2,1,0:T(8,128)(2,1)S(1)}, bf16[2,320,512]{2,1,0:T(8,128)(2,1)}) custom-call(bf16[320,512]{1,0:T(8,128)(2,1)S(1)} %bitcast.240, bf16[320,512]{1,0:T(8,128)(2,1)S(1)} %collective-permute-done.6.refs_1_, ...), custom_call_target="tpu_custom_call" | custom-call | bytes 2048 | tf_op jit(solution)/shard_map/experts_back/pallas_call | solution.py:471
  84.9 4.6 %all-to-all-start.2 = ((bf16[8,40,512]{2,1,0:T(8,128)(2,1)}), bf16[8,40,512]{2,1,0:T(8,128)(2,1)}, u32[]{:S(2)}, u32[]{:S(2)}) async-start(bf16[8,40,512]{2,1,0:T(8,128)(2,1)} %bitcast.22), calls=%async_computation.2 | async-start | bytes 655360 | tf_op jit(solution)/shard_map/all_to_all | solution.py:57
  94.4 4.3 %fusion.116 = f32[2,704,1024]{2,1,0:T(8,128)} fusion(bf16[2,320,704]{2,1,0:T(8,128)(2,1)S(1)} %copy-done.30, bf16[2,320,1024]{2,1,0:T(8,128)(2,1)S(1)} %copy-done.28), kind=kOutput, calls=%fused_computation.272 | convolution fusion | flops 922746880 | bytes 7979008 | tf_op jit(solution)/shard_map/jrf,jrd->jfd/dot_general | solution.py:610
  100.6 2.4 %collective-permute-done.14 = bf16[1,320,512]{2,1,0:T(8,128)(2,1)} collective-permute-done((bf16[1,320,512]{2,1,0:T(8,128)(2,1)}, bf16[1,320,512]{2,1,0:T(8,128)(2,1)}, u32[]{:S(2)}, u32[]{:S(2)}) %collective-permute-start.14) | collective-permute-done | bytes 327712 | tf_op jit(solution)/shard_map/ppermute | solution.py:22
  104.8 5.8 %all-to-all-start.3 = ((bf16[8,40,512]{2,1,0:T(8,128)(2,1)}), bf16[8,40,512]{2,1,0:T(8,128)(2,1)S(1)}, u32[]{:S(2)}, u32[]{:S(2)}) async-start(bf16[8,40,512]{2,1,0:T(8,128)(2,1)} %bitcast.282), calls=%async_computation.3 | async-start | bytes 655360 | tf_op jit(solution)/shard_map/all_to_all | solution.py:57
  112.9 7.3 %all-to-all-done.3 = bf16[8,40,512]{2,1,0:T(8,128)(2,1)S(1)} async-done(((bf16[8,40,512]{2,1,0:T(8,128)(2,1)}), bf16[8,40,512]{2,1,0:T(8,128)(2,1)S(1)}, u32[]{:S(2)}, u32[]{:S(2)}) %all-to-all-start.3) | async-done | bytes 327712 | tf_op jit(solution)/shard_map/all_to_all | solution.py:57
  123.3 4.3 %fusion.118 = f32[2,704,1024]{2,1,0:T(8,128)} fusion(bf16[2,320,704]{2,1,0:T(8,128)(2,1)S(1)} %copy-done.29, bf16[2,320,1024]{2,1,0:T(8,128)(2,1)S(1)} %copy-done.27), kind=kOutput, calls=%fused_computation.274 | convolution fusion | flops 922746880 | bytes 7979008 | tf_op jit(solution)/shard_map/jrf,jrd->jfd/dot_general | solution.py:612
  132.3 3.9 %attend_back.1 = (bf16[512,768]{1,0:T(8,128)(2,1)S(1)}, bf16[1,4,512,512]{3,2,1,0:T(8,128)(2,1)}) custom-call(bf16[512,768]{1,0:T(8,128)(2,1)S(1)} %copy-done.7, bf16[512,256]{1,0:T(8,128)(2,1)S(1)} %get-tuple-element.97.grad_ref, bf16[1,4,512,512]{3,2,1,0:T(8,128)(2,1)S(1)} %copy-done.3), custom_call_target="tpu_custom_call" | custom-call | bytes 2048 | tf_op jit(solution)/shard_map/attend_back/pallas_call | solution.py:348
  136.2 2.7 %collective-permute-done.18 = bf16[128,1024]{1,0:T(8,128)(2,1)S(1)} collective-permute-done((bf16[128,1024]{1,0:T(8,128)(2,1)S(1)}, bf16[128,1024]{1,0:T(8,128)(2,1)S(1)}, u32[]{:S(2)}, u32[]{:S(2)}) %collective-permute-start.18) | collective-permute-done | bytes 262176 | tf_op jit(solution)/shard_map/ppermute | solution.py:22
  145.5 8.1 %collective-permute-done.34 = bf16[256,768]{1,0:T(8,128)(2,1)S(1)} collective-permute-done((bf16[256,768]{1,0:T(8,128)(2,1)S(1)}, bf16[256,768]{1,0:T(8,128)(2,1)S(1)}, u32[]{:S(2)}, u32[]{:S(2)}) %collective-permute-start.34) | collective-permute-done | bytes 393248 | tf_op jit(solution)/shard_map/ppermute | solution.py:22
  158.1 7.6 %bucket_grad.1 = f32[32,128]{1,0:T(8,128)S(1)} custom-call(s32[512,512]{1,0:T(8,128)S(1)} %copy-done.5, bf16[1,4,512,512]{3,2,1,0:T(8,128)(2,1)S(1)} %copy-done.4), custom_call_target="tpu_custom_call" | custom-call | bytes 2048 | tf_op jit(solution)/shard_map/bucket_grad/pallas_call | solution.py:184
  188.6 3.5 %collective-permute-done.43 = bf16[32,1024]{1,0:T(8,128)(2,1)S(1)} collective-permute-done((bf16[32,1024]{1,0:T(8,128)(2,1)S(1)}, bf16[32,1024]{1,0:T(8,128)(2,1)S(1)}, u32[]{:S(2)}, u32[]{:S(2)}) %collective-permute-start.43) | collective-permute-done | bytes 65568 | tf_op jit(solution)/shard_map/ppermute | solution.py:22
  194.3 6.0 %collective-permute-start.24 = (f32[19,1024]{1,0:T(8,128)S(1)}, f32[19,1024]{1,0:T(8,128)S(1)}, u32[]{:S(2)}, u32[]{:S(2)}) collective-permute-start(f32[19,1024]{1,0:T(8,128)S(1)} %add.326), channel_id=1, source_target_pairs={{0,16},{4,20},{8,24},{12,28},{16,0},{20,4},{24,8},{28,12},{1,17},{... | collective-permute-start | bytes 233480 | tf_op jit(solution)/shard_map/ppermute | solution.py:22
  203.6 2.4 %collective-permute-start.25 = (f32[19,1024]{1,0:T(8,128)S(1)}, f32[19,1024]{1,0:T(8,128)S(1)}, u32[]{:S(2)}, u32[]{:S(2)}) collective-permute-start(f32[19,1024]{1,0:T(8,128)S(1)} %add.327), channel_id=1, source_target_pairs={{0,8},{4,12},{8,0},{12,4},{16,24},{20,28},{24,16},{28,20},{1,9},{5... | collective-permute-start | bytes 233480 | tf_op jit(solution)/shard_map/ppermute | solution.py:22
  (281 shorter events, 96.8 us)
Async XLA Ops:
  0.7 9.6 %collective-permute-start.1 = (bf16[128,1024]{1,0:T(8,128)(2,1)}, bf16[128,1024]{1,0:T(8,128)(2,1)S(1)}, u32[]{:S(2)}, u32[]{:S(2)}) collective-permute-start(bf16[128,1024]{1,0:T(8,128)(2,1)} %refs_0_.1), channel_id=1, source_target_pairs={{0,2},{1,3},{2,0},{3,1},{4,6},{5,7},{6,4},{7,5},{8,10},{9,11},{10,... | collective-permute-start | bytes 786440 | tf_op jit(solution)/shard_map/ppermute | solution.py:22
  32.6 15.8 %all-to-all-start = ((bf16[8,40,512]{2,1,0:T(8,128)(2,1)}), bf16[8,40,512]{2,1,0:T(8,128)(2,1)S(1)}, u32[]{:S(2)}, u32[]{:S(2)}) async-start(bf16[8,40,512]{2,1,0:T(8,128)(2,1)} %bitcast.12), calls=%async_computation | async-start | bytes 655360 | tf_op jit(solution)/shard_map/all_to_all | solution.py:57
  48.4 13.5 %all-to-all-start.1 = ((bf16[8,40,512]{2,1,0:T(8,128)(2,1)}), bf16[8,40,512]{2,1,0:T(8,128)(2,1)S(1)}, u32[]{:S(2)}, u32[]{:S(2)}) async-start(bf16[8,40,512]{2,1,0:T(8,128)(2,1)} %bitcast.14), calls=%async_computation.1 | async-start | bytes 655360 | tf_op jit(solution)/shard_map/all_to_all | solution.py:57
  52.0 9.8 %collective-permute-start.5 = (bf16[320,512]{1,0:T(8,128)(2,1)S(1)}, bf16[320,512]{1,0:T(8,128)(2,1)S(1)}, u32[]{:S(2)}, u32[]{:S(2)}) collective-permute-start(bf16[320,512]{1,0:T(8,128)(2,1)S(1)} %bitcast.241), channel_id=1, source_target_pairs={{0,2},{1,3},{2,0},{3,1},{4,6},{5,7},{6,4},{7,5},{8,10},{9,11},{10,... | collective-permute-start | bytes 983048 | tf_op jit(solution)/shard_map/ppermute | solution.py:22
  61.9 10.1 %collective-permute-start.6 = (bf16[320,512]{1,0:T(8,128)(2,1)S(1)}, bf16[320,512]{1,0:T(8,128)(2,1)S(1)}, u32[]{:S(2)}, u32[]{:S(2)}) collective-permute-start(bf16[320,512]{1,0:T(8,128)(2,1)S(1)} %bitcast.238), channel_id=1, source_target_pairs={{0,2},{1,3},{2,0},{3,1},{4,6},{5,7},{6,4},{7,5},{8,10},{9,11},{10,... | collective-permute-start | bytes 983048 | tf_op jit(solution)/shard_map/ppermute | solution.py:22
  74.3 9.8 %collective-permute-start.10 = (bf16[1,320,512]{2,1,0:T(8,128)(2,1)S(1)}, bf16[1,320,512]{2,1,0:T(8,128)(2,1)S(1)}, u32[]{:S(2)}, u32[]{:S(2)}) collective-permute-start(bf16[1,320,512]{2,1,0:T(8,128)(2,1)S(1)} %fusion.31), channel_id=1, source_target_pairs={{0,2},{1,3},{2,0},{3,1},{4,6},{5,7},{6,4},{7,5},{8,10},{9,11},{10,... | collective-permute-start | bytes 983048 | tf_op jit(solution)/shard_map/ppermute | solution.py:22
  84.9 15.7 %all-to-all-start.2 = ((bf16[8,40,512]{2,1,0:T(8,128)(2,1)}), bf16[8,40,512]{2,1,0:T(8,128)(2,1)}, u32[]{:S(2)}, u32[]{:S(2)}) async-start(bf16[8,40,512]{2,1,0:T(8,128)(2,1)} %bitcast.22), calls=%async_computation.2 | async-start | bytes 655360 | tf_op jit(solution)/shard_map/all_to_all | solution.py:57
  92.9 10.2 %collective-permute-start.14 = (bf16[1,320,512]{2,1,0:T(8,128)(2,1)}, bf16[1,320,512]{2,1,0:T(8,128)(2,1)}, u32[]{:S(2)}, u32[]{:S(2)}) collective-permute-start(bf16[1,320,512]{2,1,0:T(8,128)(2,1)} %fusion.32), channel_id=1, source_target_pairs={{0,2},{1,3},{2,0},{3,1},{4,6},{5,7},{6,4},{7,5},{8,10},{9,11},{10,... | collective-permute-start | bytes 983048 | tf_op jit(solution)/shard_map/ppermute | solution.py:22
  104.8 15.4 %all-to-all-start.3 = ((bf16[8,40,512]{2,1,0:T(8,128)(2,1)}), bf16[8,40,512]{2,1,0:T(8,128)(2,1)S(1)}, u32[]{:S(2)}, u32[]{:S(2)}) async-start(bf16[8,40,512]{2,1,0:T(8,128)(2,1)} %bitcast.282), calls=%async_computation.3 | async-start | bytes 655360 | tf_op jit(solution)/shard_map/all_to_all | solution.py:57
  141.5 12.1 %collective-permute-start.34 = (bf16[256,768]{1,0:T(8,128)(2,1)S(1)}, bf16[256,768]{1,0:T(8,128)(2,1)S(1)}, u32[]{:S(2)}, u32[]{:S(2)}) collective-permute-start(bf16[256,768]{1,0:T(8,128)(2,1)S(1)} %dynamic-slice_bitcast_fusion), channel_id=1, source_target_pairs={{0,4},{4,0},{8,12},{12,8},{16,20},{20,16},{24,28},{28,24},{1,5},{5... | collective-permute-start | bytes 1179656 | tf_op jit(solution)/shard_map/ppermute | solution.py:22
  143.1 27.3 %collective-permute-start.19 = (bf16[256,768]{1,0:T(8,128)(2,1)}, bf16[256,768]{1,0:T(8,128)(2,1)}, u32[]{:S(2)}, u32[]{:S(2)}) collective-permute-start(bf16[256,768]{1,0:T(8,128)(2,1)} %get-tuple-element.155), channel_id=1, source_target_pairs={{0,4},{4,0},{8,12},{12,8},{16,20},{20,16},{24,28},{28,24},{1,5},{5... | collective-permute-start | bytes 1179656 | tf_op jit(solution)/shard_map/ppermute | solution.py:22
  145.5 24.9 %collective-permute-start.20 = (bf16[2,128,1024]{2,1,0:T(8,128)(2,1)}, bf16[2,128,1024]{2,1,0:T(8,128)(2,1)}, u32[]{:S(2)}, u32[]{:S(2)}) collective-permute-start(bf16[2,128,1024]{2,1,0:T(8,128)(2,1)} %fusion.18), channel_id=1, source_target_pairs={{0,1},{1,0},{2,3},{3,2},{4,5},{5,4},{6,7},{7,6},{8,9},{9,8},{10,11... | collective-permute-start | bytes 1572872 | tf_op jit(solution)/shard_map/ppermute | solution.py:22
  154.5 11.4 %collective-permute-start.35 = (bf16[64,768]{1,0:T(8,128)(2,1)}, bf16[64,768]{1,0:T(8,128)(2,1)S(1)}, u32[]{:S(2)}, u32[]{:S(2)}) collective-permute-start(bf16[64,768]{1,0:T(8,128)(2,1)} %get-tuple-element.167), channel_id=1, source_target_pairs={{0,8},{4,12},{8,0},{12,4},{16,24},{20,28},{24,16},{28,20},{1,9},{5... | collective-permute-start | bytes 294920 | tf_op jit(solution)/shard_map/ppermute | solution.py:22
  155.6 10.3 %collective-permute-start.37 = (bf16[64,768]{1,0:T(8,128)(2,1)}, bf16[64,768]{1,0:T(8,128)(2,1)S(1)}, u32[]{:S(2)}, u32[]{:S(2)}) collective-permute-start(bf16[64,768]{1,0:T(8,128)(2,1)} %get-tuple-element.168), channel_id=1, source_target_pairs={{0,24},{4,28},{8,16},{12,20},{16,8},{20,12},{24,0},{28,4},{1,25},{... | collective-permute-start | bytes 294920 | tf_op jit(solution)/shard_map/ppermute | solution.py:22
  157.0 8.9 %collective-permute-start.36 = (bf16[64,768]{1,0:T(8,128)(2,1)S(1)}, bf16[64,768]{1,0:T(8,128)(2,1)S(1)}, u32[]{:S(2)}, u32[]{:S(2)}) collective-permute-start(bf16[64,768]{1,0:T(8,128)(2,1)S(1)} %get-tuple-element.169), channel_id=1, source_target_pairs={{0,16},{4,20},{8,24},{12,28},{16,0},{20,4},{24,8},{28,12},{1,17},{... | collective-permute-start | bytes 294920 | tf_op jit(solution)/shard_map/ppermute | solution.py:22
  166.0 9.9 %collective-permute-start.40 = (bf16[64,768]{1,0:T(8,128)(2,1)S(1)}, bf16[64,768]{1,0:T(8,128)(2,1)S(1)}, u32[]{:S(2)}, u32[]{:S(2)}) collective-permute-start(bf16[64,768]{1,0:T(8,128)(2,1)S(1)} %fusion.44), channel_id=1, source_target_pairs={{0,24},{4,28},{8,16},{12,20},{16,8},{20,12},{24,0},{28,4},{1,25},{... | collective-permute-start | bytes 294920 | tf_op jit(solution)/shard_map/ppermute | solution.py:22
  170.6 10.0 %collective-permute-start.22 = (f32[19,1024]{1,0:T(8,128)S(1)}, f32[19,1024]{1,0:T(8,128)S(1)}, u32[]{:S(2)}, u32[]{:S(2)}) collective-permute-start(f32[19,1024]{1,0:T(8,128)S(1)} %pad_maximum_fusion.7), channel_id=1, source_target_pairs={{0,2},{1,3},{2,0},{3,1},{4,6},{5,7},{6,4},{7,5},{8,10},{9,11},{10,... | collective-permute-start | bytes 233480 | tf_op jit(solution)/shard_map/ppermute | solution.py:22
  175.8 31.6 %collective-permute-start.21 = (bf16[1,128,1024]{2,1,0:T(8,128)(2,1)S(1)}, bf16[1,128,1024]{2,1,0:T(8,128)(2,1)S(1)}, u32[]{:S(2)}, u32[]{:S(2)}) collective-permute-start(bf16[1,128,1024]{2,1,0:T(8,128)(2,1)S(1)} %fusion.34), channel_id=1, source_target_pairs={{0,2},{1,3},{2,0},{3,1},{4,6},{5,7},{6,4},{7,5},{8,10},{9,11},{10,... | collective-permute-start | bytes 786440 | tf_op jit(solution)/shard_map/ppermute | solution.py:22
  181.0 36.6 %collective-permute-start.41 = (bf16[4,64,768]{2,1,0:T(8,128)(2,1)S(1)}, bf16[4,64,768]{2,1,0:T(8,128)(2,1)S(1)}, u32[]{:S(2)}, u32[]{:S(2)}) collective-permute-start(bf16[4,64,768]{2,1,0:T(8,128)(2,1)S(1)} %get-tuple-element.166), channel_id=1, source_target_pairs={{0,4},{4,0},{8,12},{12,8},{16,20},{20,16},{24,28},{28,24},{1,5},{5... | collective-permute-start | bytes 1179656 | tf_op jit(solution)/shard_map/ppermute | solution.py:22
  188.6 11.8 %collective-permute-start.31 = (bf16[64,768]{1,0:T(8,128)(2,1)S(1)}, bf16[64,768]{1,0:T(8,128)(2,1)S(1)}, u32[]{:S(2)}, u32[]{:S(2)}) collective-permute-start(bf16[64,768]{1,0:T(8,128)(2,1)S(1)} %fusion.47), channel_id=1, source_target_pairs={{0,8},{4,12},{8,0},{12,4},{16,24},{20,28},{24,16},{28,20},{1,9},{5... | collective-permute-start | bytes 294920 | tf_op jit(solution)/shard_map/ppermute | solution.py:22
  192.1 9.1 %collective-permute-start.30 = (bf16[64,768]{1,0:T(8,128)(2,1)S(1)}, bf16[64,768]{1,0:T(8,128)(2,1)S(1)}, u32[]{:S(2)}, u32[]{:S(2)}) collective-permute-start(bf16[64,768]{1,0:T(8,128)(2,1)S(1)} %fusion.47), channel_id=1, source_target_pairs={{0,16},{4,20},{8,24},{12,28},{16,0},{20,4},{24,8},{28,12},{1,17},{... | collective-permute-start | bytes 294920 | tf_op jit(solution)/shard_map/ppermute | solution.py:22
  194.3 9.2 %collective-permute-start.24 = (f32[19,1024]{1,0:T(8,128)S(1)}, f32[19,1024]{1,0:T(8,128)S(1)}, u32[]{:S(2)}, u32[]{:S(2)}) collective-permute-start(f32[19,1024]{1,0:T(8,128)S(1)} %add.326), channel_id=1, source_target_pairs={{0,16},{4,20},{8,24},{12,28},{16,0},{20,4},{24,8},{28,12},{1,17},{... | collective-permute-start | bytes 233480 | tf_op jit(solution)/shard_map/ppermute | solution.py:22
  201.3 15.9 %collective-permute-start.33 = (bf16[4,64,768]{2,1,0:T(8,128)(2,1)S(1)}, bf16[4,64,768]{2,1,0:T(8,128)(2,1)S(1)}, u32[]{:S(2)}, u32[]{:S(2)}) collective-permute-start(bf16[4,64,768]{2,1,0:T(8,128)(2,1)S(1)} %get-tuple-element.171), channel_id=1, source_target_pairs={{0,4},{4,0},{8,12},{12,8},{16,20},{20,16},{24,28},{28,24},{1,5},{5... | collective-permute-start | bytes 1179656 | tf_op jit(solution)/shard_map/ppermute | solution.py:22
  206.3 9.1 %collective-permute-start.45 = (bf16[2,32,1024]{2,1,0:T(8,128)(2,1)S(1)}, bf16[2,32,1024]{2,1,0:T(8,128)(2,1)S(1)}, u32[]{:S(2)}, u32[]{:S(2)}) collective-permute-start(bf16[2,32,1024]{2,1,0:T(8,128)(2,1)S(1)} %pad_maximum_fusion.6), channel_id=1, source_target_pairs={{0,8},{4,12},{8,0},{12,4},{16,24},{20,28},{24,16},{28,20},{1,9},{5... | collective-permute-start | bytes 393224 | tf_op jit(solution)/shard_map/ppermute | solution.py:22
  (69 other events, 475.0 us)

commit v5 on v4

--- a/solution.py
+++ b/solution.py
@@ -271,7 +271,7 @@
             jax.ShapeDtypeStruct((seq_len, head_cols), bf16),
             pltpu.HBM((1, heads, seq_len, seq_len), bf16),
         ],
-        compiler_params=pltpu.CompilerParams(vmem_limit_bytes=24 * MIB),
+        compiler_params=pltpu.CompilerParams(vmem_limit_bytes=18 * MIB),
         cost_estimate=small_cost,
         name="attend",
     )(*blocks, gain, *weights, bias)
@@ -361,7 +361,7 @@
             jax.ShapeDtypeStruct((tokens, width), bf16),
             pltpu.HBM((seqs, heads, seq_len, seq_len), bf16),
         ],
-        compiler_params=pltpu.CompilerParams(vmem_limit_bytes=20 * MIB),
+        compiler_params=pltpu.CompilerParams(vmem_limit_bytes=16 * MIB),
         cost_estimate=small_cost,
         name="attend_back",
     )(joined, mixed_grad, probs)
@@ -481,7 +481,7 @@
             pltpu.SemaphoreType.DMA((2 * experts,)),
             pltpu.SemaphoreType.DMA((experts + 1,)),
         ],
-        compiler_params=pltpu.CompilerParams(vmem_limit_bytes=26 * MIB),
+        compiler_params=pltpu.CompilerParams(vmem_limit_bytes=22 * MIB),
         cost_estimate=small_cost,
         name=name,
     )(*operands)
@@ -646,8 +646,8 @@
     all_tokens = jnp.concatenate(token_blocks, axis=0).astype(f32)
     gain_partial = jnp.sum(attn_partial * (all_tokens * root_inverse(all_tokens)), axis=0, keepdims=True)
     bucket_part = bucket_grad(moved_table, score_grad, rel_bias.shape[0])
-    first_near, attn_hop, bucket_part, gain_partial, output_near = lax.optimization_barrier(
-        (first_near, attn_hop, bucket_part, gain_partial, output_near)
+    first_near, attn_hop, bucket_part, output_near = lax.optimization_barrier(
+        (first_near, attn_hop, bucket_part, output_near)
     )
     bucket_row = lax.dynamic_update_slice(
         jnp.zeros((1, width), f32), bucket_part.reshape(1, -1), (0, member * bucket_part.size)

time: 224 us -> 224 us (level)
  starting transfers between devices: 71.4 us -> 68.1 us
  waiting for transfers between devices: 67.4 us -> 70.7 us
    ppermute x47, starting transfers between devices: 51.3 us -> 48 us  [swap(): return lax.ppermute(block, axis, [(i, i ^ offset) for i in range(size)])]
    ppermute x47, waiting for transfers between devices: 44.1 us -> 47.3 us  [swap(): return lax.ppermute(block, axis, [(i, i ^ offset) for i in range(size)])]
where the time goes in v5:
time: 224 us; the launch traced here: 223 us
  waiting for transfers between devices  70.7 us (32%)
  starting transfers between devices  68.1 us (30%)
  Pallas kernels  38.2 us (17%)
  matrix products  16.4 us (7%)
  other arithmetic  15.8 us (7%)
  local copies, waits for them, and re-layouts  12.5 us (6%)
    ppermute x47, starting transfers between devices, swap(): return lax.ppermute(block, axis, [(i, i ^ offset) for i in range(size)])  48 us
    ppermute x47, waiting for transfers between devices, swap(): return lax.ppermute(block, axis, [(i, i ^ offset) for i in range(size)])  47.3 us
    all_to_all x4, waiting for transfers between devices, exchange_groups(): return lax.all_to_all(buffer, 'dp', split_axis=0, concat_axis=0, tiled=True)  23.4 us
    all_to_all x4, starting transfers between devices, exchange_groups(): return lax.all_to_all(buffer, 'dp', split_axis=0, concat_axis=0, tiled=True)  20.1 us
    pallas_call x2, Pallas kernels, run_experts(): pl.pallas_call(functools.partial(expert_kernel, cuts, step, members), in_...  14.7 us
    pallas_call x1, Pallas kernels, bucket_grad(): pl.pallas_call(functools.partial(bucket_kernel, buckets), grid=(seq_len /...  7.57 us
    pallas_call x1, Pallas kernels, attend(): pl.pallas_call(functools.partial(attend_kernel, head_size), grid=(heads /...  7.25 us
    unnamed x85, local copies, waits for them, and re-layouts  4.84 us
  transfers between devices with their start and end apart: 51, of which 28 were waited for; matrix products, arithmetic and copies ran while one was open for 14% of the time, Pallas kernels for 14%

profile of v5, /device:TPU:0, one launch (start us, length us, event | category | flops | bytes accessed | tf_op | source)
XLA Modules:
  0.0 223.3 jit_solution(15650601270700808560)
XLA Ops:
  0.7 3.0 %collective-permute-start.1 = (bf16[128,1024]{1,0:T(8,128)(2,1)}, bf16[128,1024]{1,0:T(8,128)(2,1)S(1)}, u32[]{:S(2)}, u32[]{:S(2)}) collective-permute-start(bf16[128,1024]{1,0:T(8,128)(2,1)} %refs_0_.1), channel_id=1, source_target_pairs={{0,2},{1,3},{2,0},{3,1},{4,6},{5,7},{6,4},{7,5},{8,10},{9,11},{10,... | collective-permute-start | bytes 786440 | tf_op jit(solution)/shard_map/ppermute | solution.py:22
  5.6 4.0 %bias_lookup.1 = (f32[4,512,512]{2,1,0:T(8,128)S(1)}, s32[512,512]{1,0:T(8,128)}) custom-call(s32[1]{0:T(128)} %bitcast.shift_ref, s32[512,512]{1,0:T(8,128)S(1)} %copy-done.6, f32[4,128]{1,0:T(4,128)S(1)} %pad.4.bucket_ref), custom_call_target="tpu_custom_call" | custom-call | bytes 2048 | tf_op jit(solution)/shard_map/bias_lookup/pallas_call | solution.py:136
  11.8 7.3 %attend.1 = (bf16[512,1024]{1,0:T(8,128)(2,1)}, bf16[512,768]{1,0:T(8,128)(2,1)}, bf16[512,256]{1,0:T(8,128)(2,1)S(1)}, bf16[1,4,512,512]{3,2,1,0:T(8,128)(2,1)}) custom-call(bf16[128,1024]{1,0:T(8,128)(2,1)} %refs_0_.1, bf16[128,1024]{1,0:T(8,128)(2,1)S(1)} %collective-permute-done.refs_1_, bf16[128,1024]{1,0:T(8,128)(2,1)S(1)} %collective-permute-done.1.refs_2_, ...), custom_call_target="tpu_custom_call" | custom-call | bytes 2048 | tf_op jit(solution)/shard_map/attend/pallas_call | solution.py:251
  23.5 6.5 %collective-permute-done.4 = bf16[1,128,1024]{2,1,0:T(8,128)(2,1)S(1)} collective-permute-done((bf16[1,128,1024]{2,1,0:T(8,128)(2,1)S(1)}, bf16[1,128,1024]{2,1,0:T(8,128)(2,1)S(1)}, u32[]{:S(2)}, u32[]{:S(2)}) %collective-permute-start.4) | collective-permute-done | bytes 262176 | tf_op jit(solution)/shard_map/ppermute | solution.py:22
  32.6 6.0 %all-to-all-start = ((bf16[8,40,512]{2,1,0:T(8,128)(2,1)}), bf16[8,40,512]{2,1,0:T(8,128)(2,1)S(1)}, u32[]{:S(2)}, u32[]{:S(2)}) async-start(bf16[8,40,512]{2,1,0:T(8,128)(2,1)} %bitcast.12), calls=%async_computation | async-start | bytes 655360 | tf_op jit(solution)/shard_map/all_to_all | solution.py:57
  39.8 8.6 %all-to-all-done = bf16[8,40,512]{2,1,0:T(8,128)(2,1)S(1)} async-done(((bf16[8,40,512]{2,1,0:T(8,128)(2,1)}), bf16[8,40,512]{2,1,0:T(8,128)(2,1)S(1)}, u32[]{:S(2)}, u32[]{:S(2)}) %all-to-all-start) | async-done | bytes 327712 | tf_op jit(solution)/shard_map/all_to_all | solution.py:57
  48.4 3.6 %all-to-all-start.1 = ((bf16[8,40,512]{2,1,0:T(8,128)(2,1)}), bf16[8,40,512]{2,1,0:T(8,128)(2,1)S(1)}, u32[]{:S(2)}, u32[]{:S(2)}) async-start(bf16[8,40,512]{2,1,0:T(8,128)(2,1)} %bitcast.14), calls=%async_computation.1 | async-start | bytes 655360 | tf_op jit(solution)/shard_map/all_to_all | solution.py:57
  53.6 2.6 %pad_maximum_fusion = bf16[1024,768]{1,0:T(8,128)(2,1)} fusion(bf16[1024,256]{1,0:T(8,128)(2,1)} %refs_7_.1, bf16[1024,256]{1,0:T(8,128)(2,1)} %refs_6_.2, bf16[1024,256]{1,0:T(8,128)(2,1)} %refs_5_.3), kind=kLoop, calls=%fused_computation.5 | loop fusion | flops 4718592 | bytes 3145728 | tf_op jit(solution)/shard_map/concatenate | solution.py:598
  56.2 5.6 %all-to-all-done.1 = bf16[8,40,512]{2,1,0:T(8,128)(2,1)S(1)} async-done(((bf16[8,40,512]{2,1,0:T(8,128)(2,1)}), bf16[8,40,512]{2,1,0:T(8,128)(2,1)S(1)}, u32[]{:S(2)}, u32[]{:S(2)}) %all-to-all-start.1) | async-done | bytes 327712 | tf_op jit(solution)/shard_map/all_to_all | solution.py:57
  63.5 6.7 %experts.1 = (f32[2,320,704]{2,1,0:T(8,128)S(1)}, bf16[2,320,704]{2,1,0:T(8,128)(2,1)}, bf16[2,320,1024]{2,1,0:T(8,128)(2,1)}, bf16[2,320,512]{2,1,0:T(8,128)(2,1)S(1)}, bf16[2,320,512]{2,1,0:T(8,128)(2,1)S(1)}) custom-call(bf16[320,512]{1,0:T(8,128)(2,1)S(1)} %bitcast.243, bf16[320,512]{1,0:T(8,128)(2,1)S(1)} %collective-permute-done.5.refs_1_, ...), custom_call_target="tpu_custom_call" | custom-call | bytes 2048 | tf_op jit(solution)/shard_map/experts/pallas_call | solution.py:471
  75.9 7.9 %experts_back.1 = (bf16[2,320,704]{2,1,0:T(8,128)(2,1)}, bf16[2,320,1024]{2,1,0:T(8,128)(2,1)}, bf16[2,320,512]{2,1,0:T(8,128)(2,1)S(1)}, bf16[2,320,512]{2,1,0:T(8,128)(2,1)}) custom-call(bf16[320,512]{1,0:T(8,128)(2,1)S(1)} %bitcast.240, bf16[320,512]{1,0:T(8,128)(2,1)S(1)} %collective-permute-done.6.refs_1_, ...), custom_call_target="tpu_custom_call" | custom-call | bytes 2048 | tf_op jit(solution)/shard_map/experts_back/pallas_call | solution.py:471
  84.9 4.6 %all-to-all-start.2 = ((bf16[8,40,512]{2,1,0:T(8,128)(2,1)}), bf16[8,40,512]{2,1,0:T(8,128)(2,1)}, u32[]{:S(2)}, u32[]{:S(2)}) async-start(bf16[8,40,512]{2,1,0:T(8,128)(2,1)} %bitcast.22), calls=%async_computation.2 | async-start | bytes 655360 | tf_op jit(solution)/shard_map/all_to_all | solution.py:57
  94.4 4.3 %fusion.116 = f32[2,704,1024]{2,1,0:T(8,128)} fusion(bf16[2,320,704]{2,1,0:T(8,128)(2,1)S(1)} %copy-done.30, bf16[2,320,1024]{2,1,0:T(8,128)(2,1)S(1)} %copy-done.28), kind=kOutput, calls=%fused_computation.272 | convolution fusion | flops 922746880 | bytes 7979008 | tf_op jit(solution)/shard_map/jrf,jrd->jfd/dot_general | solution.py:610
  104.8 5.8 %all-to-all-start.3 = ((bf16[8,40,512]{2,1,0:T(8,128)(2,1)}), bf16[8,40,512]{2,1,0:T(8,128)(2,1)S(1)}, u32[]{:S(2)}, u32[]{:S(2)}) async-start(bf16[8,40,512]{2,1,0:T(8,128)(2,1)} %bitcast.282), calls=%async_computation.3 | async-start | bytes 655360 | tf_op jit(solution)/shard_map/all_to_all | solution.py:57
  112.9 7.3 %all-to-all-done.3 = bf16[8,40,512]{2,1,0:T(8,128)(2,1)S(1)} async-done(((bf16[8,40,512]{2,1,0:T(8,128)(2,1)}), bf16[8,40,512]{2,1,0:T(8,128)(2,1)S(1)}, u32[]{:S(2)}, u32[]{:S(2)}) %all-to-all-start.3) | async-done | bytes 327712 | tf_op jit(solution)/shard_map/all_to_all | solution.py:57
  123.3 4.3 %fusion.118 = f32[2,704,1024]{2,1,0:T(8,128)} fusion(bf16[2,320,704]{2,1,0:T(8,128)(2,1)S(1)} %copy-done.29, bf16[2,320,1024]{2,1,0:T(8,128)(2,1)S(1)} %copy-done.27), kind=kOutput, calls=%fused_computation.274 | convolution fusion | flops 922746880 | bytes 7979008 | tf_op jit(solution)/shard_map/jrf,jrd->jfd/dot_general | solution.py:612
  132.3 3.9 %attend_back.1 = (bf16[512,768]{1,0:T(8,128)(2,1)S(1)}, bf16[1,4,512,512]{3,2,1,0:T(8,128)(2,1)}) custom-call(bf16[512,768]{1,0:T(8,128)(2,1)S(1)} %copy-done.7, bf16[512,256]{1,0:T(8,128)(2,1)S(1)} %get-tuple-element.96.grad_ref, bf16[1,4,512,512]{3,2,1,0:T(8,128)(2,1)S(1)} %copy-done.3), custom_call_target="tpu_custom_call" | custom-call | bytes 2048 | tf_op jit(solution)/shard_map/attend_back/pallas_call | solution.py:348
  136.2 2.7 %collective-permute-done.18 = bf16[128,1024]{1,0:T(8,128)(2,1)S(1)} collective-permute-done((bf16[128,1024]{1,0:T(8,128)(2,1)S(1)}, bf16[128,1024]{1,0:T(8,128)(2,1)S(1)}, u32[]{:S(2)}, u32[]{:S(2)}) %collective-permute-start.18) | collective-permute-done | bytes 262176 | tf_op jit(solution)/shard_map/ppermute | solution.py:22
  145.5 8.1 %collective-permute-done.34 = bf16[256,768]{1,0:T(8,128)(2,1)S(1)} collective-permute-done((bf16[256,768]{1,0:T(8,128)(2,1)S(1)}, bf16[256,768]{1,0:T(8,128)(2,1)S(1)}, u32[]{:S(2)}, u32[]{:S(2)}) %collective-permute-start.34) | collective-permute-done | bytes 393248 | tf_op jit(solution)/shard_map/ppermute | solution.py:22
  158.1 7.6 %bucket_grad.1 = f32[32,128]{1,0:T(8,128)S(1)} custom-call(s32[512,512]{1,0:T(8,128)S(1)} %copy-done.5, bf16[1,4,512,512]{3,2,1,0:T(8,128)(2,1)S(1)} %copy-done.4), custom_call_target="tpu_custom_call" | custom-call | bytes 2048 | tf_op jit(solution)/shard_map/bucket_grad/pallas_call | solution.py:184
  188.6 3.5 %collective-permute-done.43 = bf16[32,1024]{1,0:T(8,128)(2,1)S(1)} collective-permute-done((bf16[32,1024]{1,0:T(8,128)(2,1)S(1)}, bf16[32,1024]{1,0:T(8,128)(2,1)S(1)}, u32[]{:S(2)}, u32[]{:S(2)}) %collective-permute-start.43) | collective-permute-done | bytes 65568 | tf_op jit(solution)/shard_map/ppermute | solution.py:22
  194.3 6.0 %collective-permute-start.24 = (f32[19,1024]{1,0:T(8,128)S(1)}, f32[19,1024]{1,0:T(8,128)S(1)}, u32[]{:S(2)}, u32[]{:S(2)}) collective-permute-start(f32[19,1024]{1,0:T(8,128)S(1)} %add.326), channel_id=1, source_target_pairs={{0,16},{4,20},{8,24},{12,28},{16,0},{20,4},{24,8},{28,12},{1,17},{... | collective-permute-start | bytes 233480 | tf_op jit(solution)/shard_map/ppermute | solution.py:22
  210.0 3.3 %collective-permute-done.26 = f32[19,1024]{1,0:T(8,128)S(1)} collective-permute-done((f32[19,1024]{1,0:T(8,128)S(1)}, f32[19,1024]{1,0:T(8,128)S(1)}, u32[]{:S(2)}, u32[]{:S(2)}) %collective-permute-start.26) | collective-permute-done | bytes 77856 | tf_op jit(solution)/shard_map/ppermute | solution.py:22
  218.4 3.5 %collective-permute-done.46 = bf16[4,32,1024]{2,1,0:T(8,128)(2,1)S(1)} collective-permute-done((bf16[4,32,1024]{2,1,0:T(8,128)(2,1)S(1)}, bf16[4,32,1024]{2,1,0:T(8,128)(2,1)S(1)}, u32[]{:S(2)}, u32[]{:S(2)}) %collective-permute-start.46) | collective-permute-done | bytes 262176 | tf_op jit(solution)/shard_map/ppermute | solution.py:22
  (281 shorter events, 95.0 us)
Async XLA Ops:
  0.7 9.6 %collective-permute-start.1 = (bf16[128,1024]{1,0:T(8,128)(2,1)}, bf16[128,1024]{1,0:T(8,128)(2,1)S(1)}, u32[]{:S(2)}, u32[]{:S(2)}) collective-permute-start(bf16[128,1024]{1,0:T(8,128)(2,1)} %refs_0_.1), channel_id=1, source_target_pairs={{0,2},{1,3},{2,0},{3,1},{4,6},{5,7},{6,4},{7,5},{8,10},{9,11},{10,... | collective-permute-start | bytes 786440 | tf_op jit(solution)/shard_map/ppermute | solution.py:22
  32.6 15.8 %all-to-all-start = ((bf16[8,40,512]{2,1,0:T(8,128)(2,1)}), bf16[8,40,512]{2,1,0:T(8,128)(2,1)S(1)}, u32[]{:S(2)}, u32[]{:S(2)}) async-start(bf16[8,40,512]{2,1,0:T(8,128)(2,1)} %bitcast.12), calls=%async_computation | async-start | bytes 655360 | tf_op jit(solution)/shard_map/all_to_all | solution.py:57
  48.4 13.5 %all-to-all-start.1 = ((bf16[8,40,512]{2,1,0:T(8,128)(2,1)}), bf16[8,40,512]{2,1,0:T(8,128)(2,1)S(1)}, u32[]{:S(2)}, u32[]{:S(2)}) async-start(bf16[8,40,512]{2,1,0:T(8,128)(2,1)} %bitcast.14), calls=%async_computation.1 | async-start | bytes 655360 | tf_op jit(solution)/shard_map/all_to_all | solution.py:57
  52.0 9.8 %collective-permute-start.5 = (bf16[320,512]{1,0:T(8,128)(2,1)S(1)}, bf16[320,512]{1,0:T(8,128)(2,1)S(1)}, u32[]{:S(2)}, u32[]{:S(2)}) collective-permute-start(bf16[320,512]{1,0:T(8,128)(2,1)S(1)} %bitcast.241), channel_id=1, source_target_pairs={{0,2},{1,3},{2,0},{3,1},{4,6},{5,7},{6,4},{7,5},{8,10},{9,11},{10,... | collective-permute-start | bytes 983048 | tf_op jit(solution)/shard_map/ppermute | solution.py:22
  61.9 10.1 %collective-permute-start.6 = (bf16[320,512]{1,0:T(8,128)(2,1)S(1)}, bf16[320,512]{1,0:T(8,128)(2,1)S(1)}, u32[]{:S(2)}, u32[]{:S(2)}) collective-permute-start(bf16[320,512]{1,0:T(8,128)(2,1)S(1)} %bitcast.238), channel_id=1, source_target_pairs={{0,2},{1,3},{2,0},{3,1},{4,6},{5,7},{6,4},{7,5},{8,10},{9,11},{10,... | collective-permute-start | bytes 983048 | tf_op jit(solution)/shard_map/ppermute | solution.py:22
  74.3 9.8 %collective-permute-start.10 = (bf16[1,320,512]{2,1,0:T(8,128)(2,1)S(1)}, bf16[1,320,512]{2,1,0:T(8,128)(2,1)S(1)}, u32[]{:S(2)}, u32[]{:S(2)}) collective-permute-start(bf16[1,320,512]{2,1,0:T(8,128)(2,1)S(1)} %fusion.31), channel_id=1, source_target_pairs={{0,2},{1,3},{2,0},{3,1},{4,6},{5,7},{6,4},{7,5},{8,10},{9,11},{10,... | collective-permute-start | bytes 983048 | tf_op jit(solution)/shard_map/ppermute | solution.py:22
  84.9 15.7 %all-to-all-start.2 = ((bf16[8,40,512]{2,1,0:T(8,128)(2,1)}), bf16[8,40,512]{2,1,0:T(8,128)(2,1)}, u32[]{:S(2)}, u32[]{:S(2)}) async-start(bf16[8,40,512]{2,1,0:T(8,128)(2,1)} %bitcast.22), calls=%async_computation.2 | async-start | bytes 655360 | tf_op jit(solution)/shard_map/all_to_all | solution.py:57
  92.9 10.2 %collective-permute-start.14 = (bf16[1,320,512]{2,1,0:T(8,128)(2,1)}, bf16[1,320,512]{2,1,0:T(8,128)(2,1)}, u32[]{:S(2)}, u32[]{:S(2)}) collective-permute-start(bf16[1,320,512]{2,1,0:T(8,128)(2,1)} %fusion.32), channel_id=1, source_target_pairs={{0,2},{1,3},{2,0},{3,1},{4,6},{5,7},{6,4},{7,5},{8,10},{9,11},{10,... | collective-permute-start | bytes 983048 | tf_op jit(solution)/shard_map/ppermute | solution.py:22
  104.8 15.4 %all-to-all-start.3 = ((bf16[8,40,512]{2,1,0:T(8,128)(2,1)}), bf16[8,40,512]{2,1,0:T(8,128)(2,1)S(1)}, u32[]{:S(2)}, u32[]{:S(2)}) async-start(bf16[8,40,512]{2,1,0:T(8,128)(2,1)} %bitcast.282), calls=%async_computation.3 | async-start | bytes 655360 | tf_op jit(solution)/shard_map/all_to_all | solution.py:57
  141.5 12.1 %collective-permute-start.34 = (bf16[256,768]{1,0:T(8,128)(2,1)S(1)}, bf16[256,768]{1,0:T(8,128)(2,1)S(1)}, u32[]{:S(2)}, u32[]{:S(2)}) collective-permute-start(bf16[256,768]{1,0:T(8,128)(2,1)S(1)} %dynamic-slice_bitcast_fusion), channel_id=1, source_target_pairs={{0,4},{4,0},{8,12},{12,8},{16,20},{20,16},{24,28},{28,24},{1,5},{5... | collective-permute-start | bytes 1179656 | tf_op jit(solution)/shard_map/ppermute | solution.py:22
  143.1 27.3 %collective-permute-start.19 = (bf16[256,768]{1,0:T(8,128)(2,1)}, bf16[256,768]{1,0:T(8,128)(2,1)}, u32[]{:S(2)}, u32[]{:S(2)}) collective-permute-start(bf16[256,768]{1,0:T(8,128)(2,1)} %get-tuple-element.153), channel_id=1, source_target_pairs={{0,4},{4,0},{8,12},{12,8},{16,20},{20,16},{24,28},{28,24},{1,5},{5... | collective-permute-start | bytes 1179656 | tf_op jit(solution)/shard_map/ppermute | solution.py:22
  145.5 24.9 %collective-permute-start.20 = (bf16[2,128,1024]{2,1,0:T(8,128)(2,1)}, bf16[2,128,1024]{2,1,0:T(8,128)(2,1)}, u32[]{:S(2)}, u32[]{:S(2)}) collective-permute-start(bf16[2,128,1024]{2,1,0:T(8,128)(2,1)} %fusion.18), channel_id=1, source_target_pairs={{0,1},{1,0},{2,3},{3,2},{4,5},{5,4},{6,7},{7,6},{8,9},{9,8},{10,11... | collective-permute-start | bytes 1572872 | tf_op jit(solution)/shard_map/ppermute | solution.py:22
  154.5 11.4 %collective-permute-start.35 = (bf16[64,768]{1,0:T(8,128)(2,1)}, bf16[64,768]{1,0:T(8,128)(2,1)S(1)}, u32[]{:S(2)}, u32[]{:S(2)}) collective-permute-start(bf16[64,768]{1,0:T(8,128)(2,1)} %get-tuple-element.165), channel_id=1, source_target_pairs={{0,8},{4,12},{8,0},{12,4},{16,24},{20,28},{24,16},{28,20},{1,9},{5... | collective-permute-start | bytes 294920 | tf_op jit(solution)/shard_map/ppermute | solution.py:22
  155.6 10.3 %collective-permute-start.37 = (bf16[64,768]{1,0:T(8,128)(2,1)}, bf16[64,768]{1,0:T(8,128)(2,1)S(1)}, u32[]{:S(2)}, u32[]{:S(2)}) collective-permute-start(bf16[64,768]{1,0:T(8,128)(2,1)} %get-tuple-element.166), channel_id=1, source_target_pairs={{0,24},{4,28},{8,16},{12,20},{16,8},{20,12},{24,0},{28,4},{1,25},{... | collective-permute-start | bytes 294920 | tf_op jit(solution)/shard_map/ppermute | solution.py:22
  157.0 8.9 %collective-permute-start.36 = (bf16[64,768]{1,0:T(8,128)(2,1)S(1)}, bf16[64,768]{1,0:T(8,128)(2,1)S(1)}, u32[]{:S(2)}, u32[]{:S(2)}) collective-permute-start(bf16[64,768]{1,0:T(8,128)(2,1)S(1)} %get-tuple-element.167), channel_id=1, source_target_pairs={{0,16},{4,20},{8,24},{12,28},{16,0},{20,4},{24,8},{28,12},{1,17},{... | collective-permute-start | bytes 294920 | tf_op jit(solution)/shard_map/ppermute | solution.py:22
  166.0 9.9 %collective-permute-start.40 = (bf16[64,768]{1,0:T(8,128)(2,1)S(1)}, bf16[64,768]{1,0:T(8,128)(2,1)S(1)}, u32[]{:S(2)}, u32[]{:S(2)}) collective-permute-start(bf16[64,768]{1,0:T(8,128)(2,1)S(1)} %fusion.44), channel_id=1, source_target_pairs={{0,24},{4,28},{8,16},{12,20},{16,8},{20,12},{24,0},{28,4},{1,25},{... | collective-permute-start | bytes 294920 | tf_op jit(solution)/shard_map/ppermute | solution.py:22
  170.6 10.0 %collective-permute-start.22 = (f32[19,1024]{1,0:T(8,128)S(1)}, f32[19,1024]{1,0:T(8,128)S(1)}, u32[]{:S(2)}, u32[]{:S(2)}) collective-permute-start(f32[19,1024]{1,0:T(8,128)S(1)} %pad_maximum_fusion.7), channel_id=1, source_target_pairs={{0,2},{1,3},{2,0},{3,1},{4,6},{5,7},{6,4},{7,5},{8,10},{9,11},{10,... | collective-permute-start | bytes 233480 | tf_op jit(solution)/shard_map/ppermute | solution.py:22
  175.8 31.6 %collective-permute-start.21 = (bf16[1,128,1024]{2,1,0:T(8,128)(2,1)S(1)}, bf16[1,128,1024]{2,1,0:T(8,128)(2,1)S(1)}, u32[]{:S(2)}, u32[]{:S(2)}) collective-permute-start(bf16[1,128,1024]{2,1,0:T(8,128)(2,1)S(1)} %fusion.34), channel_id=1, source_target_pairs={{0,2},{1,3},{2,0},{3,1},{4,6},{5,7},{6,4},{7,5},{8,10},{9,11},{10,... | collective-permute-start | bytes 786440 | tf_op jit(solution)/shard_map/ppermute | solution.py:22
  181.0 35.1 %collective-permute-start.41 = (bf16[4,64,768]{2,1,0:T(8,128)(2,1)S(1)}, bf16[4,64,768]{2,1,0:T(8,128)(2,1)S(1)}, u32[]{:S(2)}, u32[]{:S(2)}) collective-permute-start(bf16[4,64,768]{2,1,0:T(8,128)(2,1)S(1)} %get-tuple-element.164), channel_id=1, source_target_pairs={{0,4},{4,0},{8,12},{12,8},{16,20},{20,16},{24,28},{28,24},{1,5},{5... | collective-permute-start | bytes 1179656 | tf_op jit(solution)/shard_map/ppermute | solution.py:22
  188.6 11.8 %collective-permute-start.31 = (bf16[64,768]{1,0:T(8,128)(2,1)S(1)}, bf16[64,768]{1,0:T(8,128)(2,1)S(1)}, u32[]{:S(2)}, u32[]{:S(2)}) collective-permute-start(bf16[64,768]{1,0:T(8,128)(2,1)S(1)} %fusion.47), channel_id=1, source_target_pairs={{0,8},{4,12},{8,0},{12,4},{16,24},{20,28},{24,16},{28,20},{1,9},{5... | collective-permute-start | bytes 294920 | tf_op jit(solution)/shard_map/ppermute | solution.py:22
  192.1 9.1 %collective-permute-start.30 = (bf16[64,768]{1,0:T(8,128)(2,1)S(1)}, bf16[64,768]{1,0:T(8,128)(2,1)S(1)}, u32[]{:S(2)}, u32[]{:S(2)}) collective-permute-start(bf16[64,768]{1,0:T(8,128)(2,1)S(1)} %fusion.47), channel_id=1, source_target_pairs={{0,16},{4,20},{8,24},{12,28},{16,0},{20,4},{24,8},{28,12},{1,17},{... | collective-permute-start | bytes 294920 | tf_op jit(solution)/shard_map/ppermute | solution.py:22
  194.3 9.2 %collective-permute-start.24 = (f32[19,1024]{1,0:T(8,128)S(1)}, f32[19,1024]{1,0:T(8,128)S(1)}, u32[]{:S(2)}, u32[]{:S(2)}) collective-permute-start(f32[19,1024]{1,0:T(8,128)S(1)} %add.326), channel_id=1, source_target_pairs={{0,16},{4,20},{8,24},{12,28},{16,0},{20,4},{24,8},{28,12},{1,17},{... | collective-permute-start | bytes 233480 | tf_op jit(solution)/shard_map/ppermute | solution.py:22
  201.3 14.4 %collective-permute-start.33 = (bf16[4,64,768]{2,1,0:T(8,128)(2,1)S(1)}, bf16[4,64,768]{2,1,0:T(8,128)(2,1)S(1)}, u32[]{:S(2)}, u32[]{:S(2)}) collective-permute-start(bf16[4,64,768]{2,1,0:T(8,128)(2,1)S(1)} %get-tuple-element.169), channel_id=1, source_target_pairs={{0,4},{4,0},{8,12},{12,8},{16,20},{20,16},{24,28},{28,24},{1,5},{5... | collective-permute-start | bytes 1179656 | tf_op jit(solution)/shard_map/ppermute | solution.py:22
  206.3 9.1 %collective-permute-start.45 = (bf16[2,32,1024]{2,1,0:T(8,128)(2,1)S(1)}, bf16[2,32,1024]{2,1,0:T(8,128)(2,1)S(1)}, u32[]{:S(2)}, u32[]{:S(2)}) collective-permute-start(bf16[2,32,1024]{2,1,0:T(8,128)(2,1)S(1)} %pad_maximum_fusion.6), channel_id=1, source_target_pairs={{0,8},{4,12},{8,0},{12,4},{16,24},{20,28},{24,16},{28,20},{1,9},{5... | collective-permute-start | bytes 393224 | tf_op jit(solution)/shard_map/ppermute | solution.py:22
  (69 other events, 467.4 us)
